TPU v7x, 32 devices: a whole 2x2x4 slice. The times are simulated.
32 devices in a mesh: dp: 16 (over z, y, core), mp: 2 (over x).
Axes of the slice: x: 2, y: 2, z: 4, core: 2. Of those that a mesh axis runs over, the one named last changes fastest.
Arguments:
- image_pooled: bfloat16 [2048, 1152], P('dp'), may hold values from -6 to 6
- text_last: bfloat16 [2048, 1152], P('dp'), may hold values from -6 to 6
- caption_of: int32 [2048], P('dp'), may hold values from 0 to 2047
- image_gain: float32 [1152], replicated, may hold values from 0.1 to 1.9
- text_gain: float32 [1152], replicated, may hold values from 0.1 to 1.9
- mlp_up: bfloat16 [1152, 4304], P(None, 'mp'), may hold values from -0.1875 to 0.1875
- mlp_down: bfloat16 [4304, 1152], P('mp'), may hold values from -0.09375 to 0.09375
- adapter: bfloat16 [1152, 1152], P('mp'), may hold values from -0.0029296875 to 0.0029296875
- logit_scale: float32 [1], replicated, may hold values from 30 to 100
- logit_bias: float32 [1], replicated, may hold values from -4 to -1
Outputs:
- grad_adapter: bfloat16 [1152, 1152], P('mp')
- mean_loss: float32 [1], replicated
Inputs may be any that keep to these rules, and one draw needn't show every extreme that they name: caption_of[j] is the index of the image that text j describes.
All inputs are finite; a program needn't handle non-finite values.
Results may differ from a plain program's by a relative error of at most 0.00175.
The roundings to bfloat16 on the way count: a program that leaves them out, or rounds other values in their place, can miss the bound.
Values may be sent and summed in bfloat16 or wider, within the bound.
No kernel may reach another device: no remote copies, remote signals or barrier semaphores. Data moves between devices by JAX's collectives and lax.ppermute only.
A program may use at most 128 MiB of HBM per device.

v0:
```python
import jax
import jax.numpy as jnp
import numpy as np
from jax import lax
from jax.sharding import PartitionSpec as P

EPS = 1e-06
CORE, Y, Z_LOW, Z_HIGH = 1, 2, 4, 8


def layer_norm(values, gain):
    values = values.astype(jnp.float32)
    center = values - jnp.mean(values, axis=-1, keepdims=True)
    spread = jnp.mean(center * center, axis=-1, keepdims=True)
    return center * lax.rsqrt(spread + EPS) * gain


def text_resid(grads, text_unit, inverse, factor):
    scaled = grads * factor
    along = jnp.sum(text_unit * scaled, axis=-1, keepdims=True)
    return (scaled - text_unit * along) * inverse


def outer_sum(left, right):
    return lax.dot_general(
        left.astype(jnp.float32),
        right,
        (((0,), (0,)), ((), ())),
        precision=lax.Precision.HIGHEST,
        preferred_element_type=jnp.float32,
    )


def general_plan(
    image_pooled,
    text_last,
    caption_of,
    image_gain,
    text_gain,
    mlp_up,
    mlp_down,
    adapter,
    logit_scale,
    logit_bias,
):
    row_count = image_pooled.shape[0]
    mp_count = lax.axis_size("mp")
    mp_index = lax.axis_index("mp")
    dp_count = lax.axis_size("dp")
    half_rows = row_count // mp_count
    pair_count = row_count * dp_count
    image_norm = layer_norm(image_pooled, image_gain).astype(jnp.bfloat16)
    hidden = jax.nn.gelu(
        jnp.dot(image_norm, mlp_up, preferred_element_type=jnp.float32), approximate=True
    ).astype(jnp.bfloat16)
    branch = lax.psum_scatter(
        jnp.dot(hidden, mlp_down, preferred_element_type=jnp.float32),
        "mp",
        scatter_dimension=0,
        tiled=True,
    )
    own_pooled = lax.dynamic_slice_in_dim(image_pooled, mp_index * half_rows, half_rows, 0)
    feature = own_pooled.astype(jnp.float32) + branch
    image_unit = (
        feature * lax.rsqrt(jnp.sum(feature * feature, axis=-1, keepdims=True) + EPS)
    ).astype(jnp.bfloat16)
    text_norm = layer_norm(text_last, text_gain).astype(jnp.bfloat16)
    in_width = adapter.shape[0]
    text_part = lax.dynamic_slice_in_dim(text_norm, mp_index * in_width, in_width, 1)
    texts = lax.psum(jnp.dot(text_part, adapter, preferred_element_type=jnp.float32), "mp")
    inverse = lax.rsqrt(jnp.sum(texts * texts, axis=-1, keepdims=True) + EPS)
    text_unit = texts * inverse
    text_embed = text_unit.astype(jnp.bfloat16)
    scale = logit_scale[0]
    shift = logit_bias[0]
    piece = lax.all_gather(image_unit, "dp", axis=0, tiled=True)
    count = piece.shape[0]
    position = jnp.arange(count, dtype=jnp.int32)
    image_index = position // half_rows * row_count + mp_index * half_rows + position % half_rows
    logits = lax.dot_general(
        text_embed, piece, (((1,), (1,)), ((), ())), preferred_element_type=jnp.float32
    )
    labels = jnp.where(caption_of[:, None] == image_index[None, :], 1.0, -1.0).astype(jnp.float32)
    scores = scale * logits + shift
    loss_sum = jnp.sum(jax.nn.softplus(-labels * scores))
    pair_weight = (-labels * jax.nn.sigmoid(-labels * scores)).astype(jnp.bfloat16)
    grads = jnp.dot(pair_weight, piece, preferred_element_type=jnp.float32)
    grads, loss_sum = (grads, loss_sum)
    factor = scale / pair_count
    full_grads, loss_part = lax.psum((grads, loss_sum.reshape(1)), "mp")
    upper = outer_sum(text_part, text_resid(full_grads, text_unit, inverse, factor))
    grad_total, loss_total = lax.psum((upper, loss_part), "dp")
    mean_loss = loss_total / (pair_count * pair_count)
    return (grad_total.astype(jnp.bfloat16), mean_loss)


def swap(values, axis, bit):
    count = lax.axis_size(axis)
    return lax.ppermute(values, axis, [(i, i ^ bit) for i in range(count)])


def swap_x(values):
    return swap(values, "mp", 1)


def swap_core(values):
    return swap(values, "dp", CORE)


def join(mine, other, upper):
    return jnp.concatenate([jnp.where(upper, other, mine), jnp.where(upper, mine, other)], axis=0)


def bit_of(index, bit):
    return (index & bit) != 0


def dot_f32(left, right, left_axis, right_axis):
    return lax.dot_general(
        left, right, (((left_axis,), (right_axis,)), ((), ())), preferred_element_type=jnp.float32
    )


def after(value, *held):
    return lax.optimization_barrier((value,) + held)[0]


def half_of(values, upper, half):
    return jnp.where(upper, values[half:], values[:half])


def pair_terms(scores, matched):
    decay = jnp.exp(-jnp.abs(scores))
    loss = jnp.maximum(scores, 0.0) + jnp.log1p(decay) - jnp.where(matched, scores, 0.0)
    ratio = 1.0 / (1.0 + decay)
    above = jnp.where((scores >= 0.0) != matched, ratio, decay * ratio)
    return loss, jnp.where(matched, -above, above)


def slice_plan(
    image_pooled,
    text_last,
    caption_of,
    image_gain,
    text_gain,
    mlp_up,
    mlp_down,
    adapter,
    logit_scale,
    logit_bias,
):
    rows = image_pooled.shape[0]
    half_rows = rows // 2
    quarter = rows // 4
    dp = lax.axis_index("dp")
    mp = lax.axis_index("mp")
    dp_count = lax.axis_size("dp")
    pair_count = rows * dp_count
    width = image_pooled.shape[1]
    own_c, own_y, own_z1, own_z2 = (bit_of(dp, b) for b in (CORE, Y, Z_LOW, Z_HIGH))
    own_x = bit_of(mp, 1)
    upper_of = {Y: own_y, Z_LOW: own_z1, Z_HIGH: own_z2}

    def grow(values, bit, *held):
        other = swap(values, "dp", bit)
        if held:
            other = after(other, *held)
        return join(values, other, upper_of[bit])

    parts = jnp.concatenate([caption_of // 128, caption_of % 128]).astype(jnp.bfloat16)
    extra = jnp.pad(parts[None, :], ((0, 7), (0, width - 2 * rows)))
    text_a = jnp.concatenate([text_last[:half_rows], extra], axis=0)
    text_b = text_last[half_rows:]
    image_pooled = after(image_pooled, text_a)
    text_a = grow(text_a, Z_HIGH)
    text_b = grow(text_b, Y)

    in_width = adapter.shape[0]
    in_half = in_width // 2
    piece = swap_x(half_of(adapter, own_c, in_half))

    image_norm = layer_norm(image_pooled, image_gain).astype(jnp.bfloat16)
    hidden = jax.nn.gelu(
        jnp.dot(image_norm, mlp_up, preferred_element_type=jnp.float32), approximate=True
    ).astype(jnp.bfloat16)
    branch = jnp.dot(hidden, mlp_down, preferred_element_type=jnp.float32)
    arrived = swap_x(half_of(branch, ~own_x, half_rows))
    feature = half_of(image_pooled, own_x, half_rows).astype(jnp.float32) + (
        half_of(branch, own_x, half_rows) + arrived
    )
    image_unit = (
        feature * lax.rsqrt(jnp.sum(feature * feature, axis=-1, keepdims=True) + EPS)
    ).astype(jnp.bfloat16)

    text_a = after(text_a, branch)
    text_b = after(text_b, branch)
    text_a = grow(text_a, Z_LOW)
    text_b = grow(text_b, Z_HIGH)
    other_adapter = join(piece, swap_core(piece), own_c)

    image_a = image_unit[:quarter]
    image_b = image_unit[quarter:]
    image_a = grow(image_a, Z_HIGH)
    image_b = join(image_b, swap_x(image_b), own_x)
    text_a = after(text_a, image_unit)
    text_b = after(text_b, image_unit)
    text_a = grow(text_a, Y)
    text_b = grow(text_b, Z_LOW)
    image_a = grow(image_a, Z_LOW)
    image_b = grow(image_b, Z_HIGH)
    image_a = grow(image_a, Y)
    image_b = grow(image_b, Z_LOW)
    far_a = swap_x(image_a)
    far_b = swap(image_b, "dp", Y)

    blocks = text_a.reshape(-1, half_rows + 8, width)
    parts = blocks[:, half_rows, : 2 * rows].astype(jnp.int32)
    captions = (parts[:, :rows] * 128 + parts[:, rows:]).reshape(2, 2, 2, 2, half_rows)
    cap_a = captions[:, :, :, 0].reshape(-1)
    cap_b = captions[:, :, :, 1].transpose(1, 2, 0, 3).reshape(-1)
    caption = jnp.concatenate([cap_a, cap_b])
    texts_raw = jnp.concatenate([blocks[:, :half_rows].reshape(-1, width), text_b], axis=0)

    text_norm = layer_norm(texts_raw, text_gain).astype(jnp.bfloat16)
    low, high = text_norm[:, :in_width], text_norm[:, in_width:]
    text_part = jnp.where(own_x, high, low)
    text_rest = jnp.where(own_x, low, high)
    texts = dot_f32(text_part, adapter, 1, 0) + dot_f32(text_rest, other_adapter, 1, 0)
    inverse = lax.rsqrt(jnp.sum(texts * texts, axis=-1, keepdims=True) + EPS)
    text_unit = texts * inverse
    text_embed = text_unit.astype(jnp.bfloat16)
    scale = logit_scale[0]
    shift = logit_bias[0]

    def places(bits):
        place = np.arange(quarter)
        for step in bits:
            place = np.concatenate([place, place + step])
        return place

    where_a = places((Z_HIGH * rows, Z_LOW * rows, Y * rows))
    where_b = places((half_rows, Z_HIGH * rows, Z_LOW * rows)) + quarter
    core_at = (dp & CORE) * rows
    y_at = (dp & Y) * rows
    x_at = mp * half_rows

    def score(images, place, offset):
        partner = swap_core(images)
        loss = 0.0
        weights = []
        for part, at in ((images, core_at), (partner, rows - core_at)):
            scores = scale * dot_f32(text_embed, part, 1, 1) + shift
            matched = (caption - (offset + at))[:, None] == place.astype(np.int32)[None, :]
            terms, weight = pair_terms(scores, matched)
            loss = loss + jnp.sum(terms)
            weights.append(weight.astype(jnp.bfloat16))
        return loss, dot_f32(jnp.concatenate(weights, 1), jnp.concatenate([images, partner]), 1, 0)

    loss_a, grads_a = score(image_a, where_a, x_at)
    loss_b, grads_b = score(image_b, where_b, y_at)
    loss_c, grads_c = score(far_a, where_a, half_rows - x_at)
    loss_d, grads_d = score(far_b, where_b, Y * rows - y_at)
    loss = (loss_a + loss_c) + (loss_b + loss_d)
    grads = (grads_a + grads_c) + (grads_b + grads_d)

    resid = text_resid(grads, text_unit, inverse, scale / pair_count)
    top = lax.reduce_precision(resid, 8, 7)
    rest = (resid - top).astype(jnp.bfloat16)
    top = top.astype(jnp.bfloat16)

    def outer(part):
        return dot_f32(part, top, 0, 0) + dot_f32(part, rest, 0, 0)

    first, second = text_part[:, :in_half], text_part[:, in_half:]
    given = outer(jnp.where(own_c, first, second))
    kept = outer(jnp.where(own_c, second, first))
    total = (kept + swap_core(given)).astype(jnp.bfloat16)
    grad_adapter = join(total, swap_core(total), own_c)
    loss = loss.reshape(1)
    mean_loss = (loss + swap_core(loss)) / (pair_count * pair_count)
    return grad_adapter, mean_loss


def solution(mesh):
    placed = (
        P("dp", None),
        P("dp", None),
        P("dp"),
        P(),
        P(),
        P(None, "mp"),
        P("mp", None),
        P("mp", None),
        P(),
        P(),
    )
    plan = slice_plan if dict(mesh.shape) == {"dp": 16, "mp": 2} else general_plan
    return jax.shard_map(
        plan, mesh=mesh, in_specs=placed, out_specs=(P("mp", None), P()), check_vma=False
    )
```

profile of v0, /device:TPU:0, one launch (start us, length us, event | category | flops | bytes accessed | tf_op | source)
XLA Modules:
  0.0 148.0 jit_solution(12107030385775265251)
XLA Ops:
  1.6 3.0 %collective-permute-start.4 = (bf16[64,1152]{1,0:T(8,128)(2,1)S(1)}, bf16[64,1152]{1,0:T(8,128)(2,1)S(1)}, u32[]{:S(2)}, u32[]{:S(2)}) collective-permute-start(bf16[64,1152]{1,0:T(8,128)(2,1)S(1)} %slice.68), channel_id=1, source_target_pairs={{0,4},{2,6},{4,0},{6,2},{8,12},{10,14},{12,8},{14,10},{16,20},{18,... | collective-permute-start | bytes 442376 | tf_op jit(solution)/shard_map/ppermute | solution.py:99
  6.0 1.6 %collective-permute-start.7 = (bf16[288,1152]{1,0:T(8,128)(2,1)S(1)}, bf16[288,1152]{1,0:T(8,128)(2,1)}, u32[]{:S(2)}, u32[]{:S(2)}) collective-permute-start(bf16[288,1152]{1,0:T(8,128)(2,1)S(1)} %slice_select_fusion), channel_id=1, source_target_pairs={{0,1},{1,0},{2,3},{3,2},{4,5},{5,4},{6,7},{7,6},{8,9},{9,8},{10,11... | collective-permute-start | bytes 1990664 | tf_op jit(solution)/shard_map/ppermute | solution.py:99
  9.7 2.7 %collective-permute-start = (bf16[72,1152]{1,0:T(8,128)(2,1)S(1)}, bf16[72,1152]{1,0:T(8,128)(2,1)S(1)}, u32[]{:S(2)}, u32[]{:S(2)}) collective-permute-start(bf16[72,1152]{1,0:T(8,128)(2,1)S(1)} %pad_maximum_fusion.11), channel_id=1, source_target_pairs={{0,16},{2,18},{4,20},{6,22},{8,24},{10,26},{12,28},{14,30},{16,0},... | collective-permute-start | bytes 497672 | tf_op jit(solution)/shard_map/ppermute | solution.py:99
  12.7 7.6 %fusion.94 = f32[128,1152]{1,0:T(8,128)S(1)} fusion(bf16[2152,1152]{1,0:T(8,128)(2,1)} %param.24, bf16[1152,2152]{0,1:T(8,128)(2,1)} %param.23, bf16[128,1152]{1,0:T(8,128)(2,1)S(1)} %copy-done.2, f32[1152]{0:T(1024)S(1)} %copy-done.8, f32[128]{0:T(128)S(1)} %add_rsqrt_fusion.3, f32[128]{0:T(128)S(1)} %broadcast_multiply_fusion.1), kind=kOutput, calls=%fused_computation.176 | convolution fusion | flops 1272517632 | bytes 10806784 | tf_op jit(solution)/shard_map/dot_general | solution.py:186
  21.5 1.6 %collective-permute-start.1 = (bf16[144,1152]{1,0:T(8,128)(2,1)S(1)}, bf16[144,1152]{1,0:T(8,128)(2,1)S(1)}, u32[]{:S(2)}, u32[]{:S(2)}) collective-permute-start(bf16[144,1152]{1,0:T(8,128)(2,1)S(1)} %pad_maximum_fusion.7), channel_id=1, source_target_pairs={{0,8},{2,10},{4,12},{6,14},{8,0},{10,2},{12,4},{14,6},{16,24},{18,... | collective-permute-start | bytes 995336 | tf_op jit(solution)/shard_map/ppermute | solution.py:99
  23.2 5.6 %collective-permute-done.2 = f32[64,1152]{1,0:T(8,128)S(1)} collective-permute-done((f32[64,1152]{1,0:T(8,128)S(1)}, f32[64,1152]{1,0:T(8,128)S(1)}, u32[]{:S(2)}, u32[]{:S(2)}) %collective-permute-start.2) | collective-permute-done | bytes 294944 | tf_op jit(solution)/shard_map/ppermute | solution.py:99
  29.1 2.7 %collective-permute-start.9 = (bf16[32,1152]{1,0:T(8,128)(2,1)S(1)}, bf16[32,1152]{1,0:T(8,128)(2,1)S(1)}, u32[]{:S(2)}, u32[]{:S(2)}) collective-permute-start(bf16[32,1152]{1,0:T(8,128)(2,1)S(1)} %get-tuple-element.61), channel_id=1, source_target_pairs={{0,16},{2,18},{4,20},{6,22},{8,24},{10,26},{12,28},{14,30},{16,0},... | collective-permute-start | bytes 221192 | tf_op jit(solution)/shard_map/ppermute | solution.py:99
  31.8 1.5 %collective-permute-start.15 = (bf16[32,1152]{1,0:T(8,128)(2,1)S(1)}, bf16[32,1152]{1,0:T(8,128)(2,1)S(1)}, u32[]{:S(2)}, u32[]{:S(2)}) collective-permute-start(bf16[32,1152]{1,0:T(8,128)(2,1)S(1)} %get-tuple-element.62), channel_id=1, source_target_pairs={{0,1},{1,0},{2,3},{3,2},{4,5},{5,4},{6,7},{7,6},{8,9},{9,8},{10,11... | collective-permute-start | bytes 221192 | tf_op jit(solution)/shard_map/ppermute | solution.py:99
  33.3 3.9 %collective-permute-done.5 = bf16[128,1152]{1,0:T(8,128)(2,1)S(1)} collective-permute-done((bf16[128,1152]{1,0:T(8,128)(2,1)S(1)}, bf16[128,1152]{1,0:T(8,128)(2,1)S(1)}, u32[]{:S(2)}, u32[]{:S(2)}) %collective-permute-start.5) | collective-permute-done | bytes 294944 | tf_op jit(solution)/shard_map/ppermute | solution.py:99
  38.6 2.2 %collective-permute-start.10 = (bf16[64,1152]{1,0:T(8,128)(2,1)S(1)}, bf16[64,1152]{1,0:T(8,128)(2,1)S(1)}, u32[]{:S(2)}, u32[]{:S(2)}) collective-permute-start(bf16[64,1152]{1,0:T(8,128)(2,1)S(1)} %pad_maximum_fusion.12), channel_id=1, source_target_pairs={{0,8},{2,10},{4,12},{6,14},{8,0},{10,2},{12,4},{14,6},{16,24},{18,... | collective-permute-start | bytes 442376 | tf_op jit(solution)/shard_map/ppermute | solution.py:99
  40.9 11.7 %collective-permute-done.16 = bf16[64,1152]{1,0:T(8,128)(2,1)S(1)} collective-permute-done((bf16[64,1152]{1,0:T(8,128)(2,1)S(1)}, bf16[64,1152]{1,0:T(8,128)(2,1)S(1)}, u32[]{:S(2)}, u32[]{:S(2)}) %collective-permute-start.16) | collective-permute-done | bytes 147488 | tf_op jit(solution)/shard_map/ppermute | solution.py:99
  52.6 4.4 %collective-permute-done.10 = bf16[64,1152]{1,0:T(8,128)(2,1)S(1)} collective-permute-done((bf16[64,1152]{1,0:T(8,128)(2,1)S(1)}, bf16[64,1152]{1,0:T(8,128)(2,1)S(1)}, u32[]{:S(2)}, u32[]{:S(2)}) %collective-permute-start.10) | collective-permute-done | bytes 147488 | tf_op jit(solution)/shard_map/ppermute | solution.py:99
  57.8 1.6 %collective-permute-start.11 = (bf16[128,1152]{1,0:T(8,128)(2,1)S(1)}, bf16[128,1152]{1,0:T(8,128)(2,1)S(1)}, u32[]{:S(2)}, u32[]{:S(2)}) collective-permute-start(bf16[128,1152]{1,0:T(8,128)(2,1)S(1)} %pad_maximum_fusion.9), channel_id=1, source_target_pairs={{0,4},{2,6},{4,0},{6,2},{8,12},{10,14},{12,8},{14,10},{16,20},{18,... | collective-permute-start | bytes 884744 | tf_op jit(solution)/shard_map/ppermute | solution.py:99
  59.4 4.5 %collective-permute-done.17 = bf16[128,1152]{1,0:T(8,128)(2,1)S(1)} collective-permute-done((bf16[128,1152]{1,0:T(8,128)(2,1)S(1)}, bf16[128,1152]{1,0:T(8,128)(2,1)S(1)}, u32[]{:S(2)}, u32[]{:S(2)}) %collective-permute-start.17) | collective-permute-done | bytes 294944 | tf_op jit(solution)/shard_map/ppermute | solution.py:99
  64.9 13.6 %collective-permute-done.11 = bf16[128,1152]{1,0:T(8,128)(2,1)S(1)} collective-permute-done((bf16[128,1152]{1,0:T(8,128)(2,1)S(1)}, bf16[128,1152]{1,0:T(8,128)(2,1)S(1)}, u32[]{:S(2)}, u32[]{:S(2)}) %collective-permute-start.11) | collective-permute-done | bytes 294944 | tf_op jit(solution)/shard_map/ppermute | solution.py:99
  80.1 1.4 collective-permute-start.13
  82.3 2.3 %fusion.2 = f32[1024]{0:T(1024)S(1)} fusion(f32[1024]{0:T(1024)S(1)} %broadcast_multiply_fusion, bf16[256,1152]{1,0:T(8,128)(2,1)S(1)} %get-tuple-element.29, bf16[256,1152]{1,0:T(8,128)(2,1)S(1)} %get-tuple-element.28, bf16[512,1152]{1,0:T(8,128)(2,1)S(1)} %bitcast.53), kind=kLoop, calls=%fused_computation.8 | loop fusion | flops 10615808 | bytes 2367488 | tf_op jit(solution)/shard_map/reduce_sum | solution.py:14
  84.6 2.1 %fusion.4 = bf16[1024,1152]{1,0:T(8,128)(2,1)S(1)} fusion(f32[1152]{0:T(1024)S(1)} %copy-done.7, f32[1024]{0:T(1024)S(1)} %add_rsqrt_fusion.1, f32[1024]{0:T(1024)S(1)} %broadcast_multiply_fusion, bf16[256,1152]{1,0:T(8,128)(2,1)S(1)} %get-tuple-element.29, bf16[256,1152]{1,0:T(8,128)(2,1)S(1)} %get-tuple-element.28, bf16[512,1152]{1,0:T(8,128)(2,1)S(1)} %bitcast.54), kind=kLoop, calls=%fused_computation.10 | loop fusion | flops 11796480 | bytes 4731392 | tf_op jit(solution)/shard_map/convert_element_type | solution.py:224
  89.5 2.1 %fusion.132 = f32[1024,1152]{1,0:T(8,128)S(1)} fusion(bf16[1024,576]{1,0:T(8,128)(2,1)S(1)} %broadcast_select_fusion, bf16[576,1152]{1,0:T(8,128)(2,1)S(1)} %copy-done.3), kind=kOutput, calls=%fused_computation.264 | convolution fusion | flops 1358954496 | bytes 7225344 | tf_op jit(solution)/shard_map/dot_general | solution.py:119
  91.6 1.6 %broadcast_select_fusion.8 = (bf16[288,1152]{1,0:T(8,128)(2,1)S(1)}, bf16[288,1152]{1,0:T(8,128)(2,1)S(1)}) fusion(bf16[288,1152]{1,0:T(8,128)(2,1)} %collective-permute-done.8, bf16[288,1152]{1,0:T(8,128)(2,1)} %collective-permute-done.7, pred[]{:T(512)S(6)} %ne.59), kind=kLoop, calls=%fused_computation.167 | loop fusion | flops 663552 | bytes 2654209 | tf_op jit(solution)/shard_map/jit(_where)/select_n | solution.py:111
  93.7 2.5 %multiply_reduce_fusion.1 = (f32[1024]{0:T(1024)S(1)}, f32[1024,1152]{1,0:T(8,128)S(1)}) fusion(f32[1024,1152]{1,0:T(8,128)S(1)} %fusion.132, bf16[288,1152]{1,0:T(8,128)(2,1)S(1)} %get-tuple-element.25, bf16[288,1152]{1,0:T(8,128)(2,1)S(1)} %get-tuple-element.24, pred[]{:T(512)S(6)} %ne.60, bf16[1024,1152]{1,0:T(8,128)(2,1)S(1)} %copy-done.1), kind=kOutput, calls=%fused_computation.15 | convolution fusion | flops 1365736448 | bytes 13389825 | tf_op jit(solution)/shard_map/dot_general | solution.py:119
  99.5 2.0 %fusion.9 = f32[1024,256]{0,1:T(8,128)S(1)} fusion(bf16[1024,1152]{1,0:T(8,128)(2,1)S(1)} %multiply_convert_fusion, bf16[256,1152]{1,0:T(8,128)(2,1)} %collective-permute-done.19, f32[]{:T(128)} %bitcast.46, f32[]{:T(128)} %bitcast.38), kind=kOutput, calls=%fused_computation.59 | convolution fusion | flops 604504064 | bytes 3997704 | tf_op jit(solution)/shard_map/dot_general | solution.py:119
  101.5 2.0 %fusion.13 = f32[1024,256]{0,1:T(8,128)S(1)} fusion(bf16[1024,1152]{1,0:T(8,128)(2,1)S(1)} %multiply_convert_fusion, bf16[256,1152]{1,0:T(8,128)(2,1)} %collective-permute-done.13, f32[]{:T(128)} %bitcast.50, f32[]{:T(128)} %bitcast.42), kind=kOutput, calls=%fused_computation.67 | convolution fusion | flops 604504064 | bytes 3997704 | tf_op jit(solution)/shard_map/dot_general | solution.py:119
  103.5 2.0 %fusion.10 = f32[1024,256]{0,1:T(8,128)S(1)} fusion(bf16[1024,1152]{1,0:T(8,128)(2,1)S(1)} %multiply_convert_fusion, bf16[256,1152]{1,0:T(8,128)(2,1)} %collective-permute-done.18, f32[]{:T(128)} %bitcast.47, f32[]{:T(128)} %bitcast.39), kind=kOutput, calls=%fused_computation.61 | convolution fusion | flops 604504064 | bytes 3997704 | tf_op jit(solution)/shard_map/dot_general | solution.py:119
  105.4 2.0 %fusion.14 = f32[1024,256]{0,1:T(8,128)S(1)} fusion(bf16[1024,1152]{1,0:T(8,128)(2,1)S(1)} %multiply_convert_fusion, bf16[256,1152]{1,0:T(8,128)(2,1)} %collective-permute-done.12, f32[]{:T(128)} %bitcast.51, f32[]{:T(128)} %bitcast.43), kind=kOutput, calls=%fused_computation.69 | convolution fusion | flops 604504064 | bytes 3997704 | tf_op jit(solution)/shard_map/dot_general | solution.py:119
  107.4 6.1 %fusion.72 = (f32[]{:T(128)}, f32[]{:T(128)}, f32[]{:T(128)}, f32[]{:T(128)}, bf16[1024,256]{0,1:T(8,128)(2,1)S(1)}, /*index=5*/bf16[1024,256]{0,1:T(8,128)(2,1)...) fusion(s32[1024]{0:T(1024)S(1)} %get-tuple-element.66, s32[256]{0:T(256)S(1)} %copy-done.10, ...), kind=kOutput, calls=%fused_computation.131 | convolution fusion | flops 622329856 | bytes 8209432 | tf_op jit(solution)/shard_map/dot_general | solution.py:119
  113.5 2.7 %fusion.30 = f32[1024,1152]{1,0:T(8,128)S(1)} fusion(bf16[256,1152]{1,0:T(8,128)(2,1)} %collective-permute-done.18, bf16[128,1152]{1,0:T(8,128)(2,1)S(1)} %copy-done.5, bf16[128,1152]{1,0:T(8,128)(2,1)S(1)} %get-tuple-element.44, bf16[1024,256]{0,1:T(8,128)(2,1)S(1)} %get-tuple-element.30, bf16[1024,256]{0,1:T(8,128)(2,1)S(1)} %get-tuple-element.32), kind=kOutput, calls=%fused_computation.89 | convolution fusion | flops 1213595648 | bytes 6946816 | tf_op jit(solution)/shard_map/dot_general | solution.py:119
  116.2 5.8 %fusion.60 = (f32[]{:T(128)}, f32[]{:T(128)}, f32[]{:T(128)}, f32[]{:T(128)}, bf16[1024,256]{0,1:T(8,128)(2,1)S(1)}, /*index=5*/bf16[1024,256]{0,1:T(8,128)(2,1)...) fusion(s32[1024]{0:T(1024)S(1)} %get-tuple-element.70, s32[256]{0:T(256)S(1)} %copy-done.9, ...), kind=kOutput, calls=%fused_computation.119 | convolution fusion | flops 622329856 | bytes 8209432 | tf_op jit(solution)/shard_map/dot_general | solution.py:119
  122.0 2.6 %fusion.21 = f32[1024,1152]{1,0:T(8,128)S(1)} fusion(bf16[256,1152]{1,0:T(8,128)(2,1)} %collective-permute-done.12, bf16[128,1152]{1,0:T(8,128)(2,1)S(1)} %get-tuple-element.41, bf16[128,1152]{1,0:T(8,128)(2,1)S(1)} %get-tuple-element.40, bf16[1024,256]{0,1:T(8,128)(2,1)S(1)} %get-tuple-element.34, bf16[1024,256]{0,1:T(8,128)(2,1)S(1)} %get-tuple-element.36), kind=kOutput, calls=%fused_computation.80 | convolution fusion | flops 1213595648 | bytes 6946816 | tf_op jit(solution)/shard_map/dot_general | solution.py:119
  124.7 2.7 %convolution_add_fusion = f32[1024,1152]{1,0:T(8,128)S(1)} fusion(f32[1024,1152]{1,0:T(8,128)S(1)} %fusion.30, bf16[256,1152]{1,0:T(8,128)(2,1)S(1)} %collective-permute-done.20, bf16[256,1152]{1,0:T(8,128)(2,1)} %collective-permute-done.19, bf16[1024,256]{0,1:T(8,128)(2,1)S(1)} %get-tuple-element.33, bf16[1024,256]{0,1:T(8,128)(2,1)S(1)} %get-tuple-element.31), kind=kOutput, calls=%fused_computation.6 | convolution fusion | flops 1213595648 | bytes 11665408 | tf_op jit(solution)/shard_map/dot_general | solution.py:119
  127.3 3.6 %multiply_reduce_fusion = (f32[1024]{0:T(1024)S(1)}, f32[1024,1152]{1,0:T(8,128)S(1)}) fusion(f32[1024,1152]{1,0:T(8,128)S(1)} %get-tuple-element.76, f32[1024]{0:T(1024)S(1)} %add_rsqrt_fusion, f32[]{:T(128)S(6)} %div.70, f32[1024,1152]{1,0:T(8,128)S(1)} %convolution_add_fusion, f32[1024,1152]{1,0:T(8,128)S(1)} %fusion.21, ...), kind=kOutput, calls=%fused_computation.13 | convolution fusion | flops 1219492864 | bytes 21110788 | tf_op jit(solution)/shard_map/dot_general | solution.py:119
  135.4 1.7 %collective-permute-done.21 = f32[288,1152]{1,0:T(8,128)S(1)} collective-permute-done((f32[288,1152]{1,0:T(8,128)S(1)}, f32[288,1152]{1,0:T(8,128)S(1)}, u32[]{:S(2)}, u32[]{:S(2)}) %collective-permute-start.21) | collective-permute-done | bytes 1327136 | tf_op jit(solution)/shard_map/ppermute | solution.py:99
  (117 shorter events, 25.5 us)
Async XLA Ops:
  0.6 9.0 %copy-start.6 = (bf16[128,1152]{1,0:T(8,128)(2,1)S(1)}, bf16[128,1152]{1,0:T(8,128)(2,1)}, u32[]{:S(2)}) copy-start(bf16[128,1152]{1,0:T(8,128)(2,1)} %param.19) | copy-start | bytes 884740
  0.6 11.7 %copy-start.2 = (bf16[128,1152]{1,0:T(8,128)(2,1)S(1)}, bf16[128,1152]{1,0:T(8,128)(2,1)}, u32[]{:S(2)}) copy-start(bf16[128,1152]{1,0:T(8,128)(2,1)} %param.18) | copy-start | bytes 884740
  0.6 12.1 %copy-start.8 = (f32[1152]{0:T(1024)S(1)}, f32[1152]{0:T(1024)}, u32[]{:S(2)}) copy-start(f32[1152]{0:T(1024)} %param.21) | copy-start | bytes 13828
  1.6 7.9 %collective-permute-start.4 = (bf16[64,1152]{1,0:T(8,128)(2,1)S(1)}, bf16[64,1152]{1,0:T(8,128)(2,1)S(1)}, u32[]{:S(2)}, u32[]{:S(2)}) collective-permute-start(bf16[64,1152]{1,0:T(8,128)(2,1)S(1)} %slice.68), channel_id=1, source_target_pairs={{0,4},{2,6},{4,0},{6,2},{8,12},{10,14},{12,8},{14,10},{16,20},{18,... | collective-permute-start | bytes 442376 | tf_op jit(solution)/shard_map/ppermute | solution.py:99
  6.0 51.7 %collective-permute-start.7 = (bf16[288,1152]{1,0:T(8,128)(2,1)S(1)}, bf16[288,1152]{1,0:T(8,128)(2,1)}, u32[]{:S(2)}, u32[]{:S(2)}) collective-permute-start(bf16[288,1152]{1,0:T(8,128)(2,1)S(1)} %slice_select_fusion), channel_id=1, source_target_pairs={{0,1},{1,0},{2,3},{3,2},{4,5},{5,4},{6,7},{7,6},{8,9},{9,8},{10,11... | collective-permute-start | bytes 1990664 | tf_op jit(solution)/shard_map/ppermute | solution.py:99
  9.7 11.8 %collective-permute-start = (bf16[72,1152]{1,0:T(8,128)(2,1)S(1)}, bf16[72,1152]{1,0:T(8,128)(2,1)S(1)}, u32[]{:S(2)}, u32[]{:S(2)}) collective-permute-start(bf16[72,1152]{1,0:T(8,128)(2,1)S(1)} %pad_maximum_fusion.11), channel_id=1, source_target_pairs={{0,16},{2,18},{4,20},{6,22},{8,24},{10,26},{12,28},{14,30},{16,0},... | collective-permute-start | bytes 497672 | tf_op jit(solution)/shard_map/ppermute | solution.py:99
  20.3 16.9 %collective-permute-start.5 = (bf16[128,1152]{1,0:T(8,128)(2,1)S(1)}, bf16[128,1152]{1,0:T(8,128)(2,1)S(1)}, u32[]{:S(2)}, u32[]{:S(2)}) collective-permute-start(bf16[128,1152]{1,0:T(8,128)(2,1)S(1)} %pad_maximum_fusion.8), channel_id=1, source_target_pairs={{0,16},{2,18},{4,20},{6,22},{8,24},{10,26},{12,28},{14,30},{16,0},... | collective-permute-start | bytes 884744 | tf_op jit(solution)/shard_map/ppermute | solution.py:99
  20.7 8.1 %collective-permute-start.2 = (f32[64,1152]{1,0:T(8,128)S(1)}, f32[64,1152]{1,0:T(8,128)S(1)}, u32[]{:S(2)}, u32[]{:S(2)}) collective-permute-start(f32[64,1152]{1,0:T(8,128)S(1)} %slice_select_fusion.1), channel_id=1, source_target_pairs={{0,1},{1,0},{2,3},{3,2},{4,5},{5,4},{6,7},{7,6},{8,9},{9,8},{10,11... | collective-permute-start | bytes 884744 | tf_op jit(solution)/shard_map/ppermute | solution.py:99
  21.5 19.3 %collective-permute-start.1 = (bf16[144,1152]{1,0:T(8,128)(2,1)S(1)}, bf16[144,1152]{1,0:T(8,128)(2,1)S(1)}, u32[]{:S(2)}, u32[]{:S(2)}) collective-permute-start(bf16[144,1152]{1,0:T(8,128)(2,1)S(1)} %pad_maximum_fusion.7), channel_id=1, source_target_pairs={{0,8},{2,10},{4,12},{6,14},{8,0},{10,2},{12,4},{14,6},{16,24},{18,... | collective-permute-start | bytes 995336 | tf_op jit(solution)/shard_map/ppermute | solution.py:99
  29.1 8.9 %collective-permute-start.9 = (bf16[32,1152]{1,0:T(8,128)(2,1)S(1)}, bf16[32,1152]{1,0:T(8,128)(2,1)S(1)}, u32[]{:S(2)}, u32[]{:S(2)}) collective-permute-start(bf16[32,1152]{1,0:T(8,128)(2,1)S(1)} %get-tuple-element.61), channel_id=1, source_target_pairs={{0,16},{2,18},{4,20},{6,22},{8,24},{10,26},{12,28},{14,30},{16,0},... | collective-permute-start | bytes 221192 | tf_op jit(solution)/shard_map/ppermute | solution.py:99
  31.8 6.2 %collective-permute-start.15 = (bf16[32,1152]{1,0:T(8,128)(2,1)S(1)}, bf16[32,1152]{1,0:T(8,128)(2,1)S(1)}, u32[]{:S(2)}, u32[]{:S(2)}) collective-permute-start(bf16[32,1152]{1,0:T(8,128)(2,1)S(1)} %get-tuple-element.62), channel_id=1, source_target_pairs={{0,1},{1,0},{2,3},{3,2},{4,5},{5,4},{6,7},{7,6},{8,9},{9,8},{10,11... | collective-permute-start | bytes 221192 | tf_op jit(solution)/shard_map/ppermute | solution.py:99
  37.3 42.6 %collective-permute-start.6 = (bf16[256,1152]{1,0:T(8,128)(2,1)S(1)}, bf16[256,1152]{1,0:T(8,128)(2,1)S(1)}, u32[]{:S(2)}, u32[]{:S(2)}) collective-permute-start(bf16[256,1152]{1,0:T(8,128)(2,1)S(1)} %pad_maximum_fusion.4), channel_id=1, source_target_pairs={{0,8},{2,10},{4,12},{6,14},{8,0},{10,2},{12,4},{14,6},{16,24},{18,... | collective-permute-start | bytes 1769480 | tf_op jit(solution)/shard_map/ppermute | solution.py:99
  38.1 14.5 %collective-permute-start.16 = (bf16[64,1152]{1,0:T(8,128)(2,1)S(1)}, bf16[64,1152]{1,0:T(8,128)(2,1)S(1)}, u32[]{:S(2)}, u32[]{:S(2)}) collective-permute-start(bf16[64,1152]{1,0:T(8,128)(2,1)S(1)} %pad_maximum_fusion.13), channel_id=1, source_target_pairs={{0,16},{2,18},{4,20},{6,22},{8,24},{10,26},{12,28},{14,30},{16,0},... | collective-permute-start | bytes 442376 | tf_op jit(solution)/shard_map/ppermute | solution.py:99
  38.6 18.3 %collective-permute-start.10 = (bf16[64,1152]{1,0:T(8,128)(2,1)S(1)}, bf16[64,1152]{1,0:T(8,128)(2,1)S(1)}, u32[]{:S(2)}, u32[]{:S(2)}) collective-permute-start(bf16[64,1152]{1,0:T(8,128)(2,1)S(1)} %pad_maximum_fusion.12), channel_id=1, source_target_pairs={{0,8},{2,10},{4,12},{6,14},{8,0},{10,2},{12,4},{14,6},{16,24},{18,... | collective-permute-start | bytes 442376 | tf_op jit(solution)/shard_map/ppermute | solution.py:99
  57.1 6.8 %collective-permute-start.17 = (bf16[128,1152]{1,0:T(8,128)(2,1)S(1)}, bf16[128,1152]{1,0:T(8,128)(2,1)S(1)}, u32[]{:S(2)}, u32[]{:S(2)}) collective-permute-start(bf16[128,1152]{1,0:T(8,128)(2,1)S(1)} %pad_maximum_fusion.10), channel_id=1, source_target_pairs={{0,8},{2,10},{4,12},{6,14},{8,0},{10,2},{12,4},{14,6},{16,24},{18,... | collective-permute-start | bytes 884744 | tf_op jit(solution)/shard_map/ppermute | solution.py:99
  57.2 22.8 %collective-permute-start.3 = (bf16[288,1152]{1,0:T(8,128)(2,1)S(1)}, bf16[288,1152]{1,0:T(8,128)(2,1)S(1)}, u32[]{:S(2)}, u32[]{:S(2)}) collective-permute-start(bf16[288,1152]{1,0:T(8,128)(2,1)S(1)} %pad_maximum_fusion.3), channel_id=1, source_target_pairs={{0,4},{2,6},{4,0},{6,2},{8,12},{10,14},{12,8},{14,10},{16,20},{18,... | collective-permute-start | bytes 1990664 | tf_op jit(solution)/shard_map/ppermute | solution.py:99
  57.7 33.9 %collective-permute-start.8 = (bf16[288,1152]{1,0:T(8,128)(2,1)}, bf16[288,1152]{1,0:T(8,128)(2,1)}, u32[]{:S(2)}, u32[]{:S(2)}) collective-permute-start(bf16[288,1152]{1,0:T(8,128)(2,1)} %collective-permute-done.7), channel_id=1, source_target_pairs={{0,2},{2,0},{4,6},{6,4},{8,10},{10,8},{12,14},{14,12},{16,18},{18,... | collective-permute-start | bytes 1990664 | tf_op jit(solution)/shard_map/ppermute | solution.py:99
  57.8 20.7 %collective-permute-start.11 = (bf16[128,1152]{1,0:T(8,128)(2,1)S(1)}, bf16[128,1152]{1,0:T(8,128)(2,1)S(1)}, u32[]{:S(2)}, u32[]{:S(2)}) collective-permute-start(bf16[128,1152]{1,0:T(8,128)(2,1)S(1)} %pad_maximum_fusion.9), channel_id=1, source_target_pairs={{0,4},{2,6},{4,0},{6,2},{8,12},{10,14},{12,8},{14,10},{16,20},{18,... | collective-permute-start | bytes 884744 | tf_op jit(solution)/shard_map/ppermute | solution.py:99
  64.0 16.1 %copy-start.4 = (bf16[128,1152]{1,0:T(8,128)(2,1)}, bf16[128,1152]{1,0:T(8,128)(2,1)S(1)}, u32[]{:S(2)}) copy-start(bf16[128,1152]{1,0:T(8,128)(2,1)S(1)} %get-tuple-element.45) | copy-start | bytes 884740
  64.9 38.6 %collective-permute-start.18 = (bf16[256,1152]{1,0:T(8,128)(2,1)}, bf16[256,1152]{1,0:T(8,128)(2,1)}, u32[]{:S(2)}, u32[]{:S(2)}) collective-permute-start(bf16[256,1152]{1,0:T(8,128)(2,1)} %pad_maximum_fusion.6), channel_id=1, source_target_pairs={{0,2},{2,0},{4,6},{6,4},{8,10},{10,8},{12,14},{14,12},{16,18},{18,... | collective-permute-start | bytes 1769480 | tf_op jit(solution)/shard_map/ppermute | solution.py:99
  78.5 20.5 %collective-permute-start.19 = (bf16[256,1152]{1,0:T(8,128)(2,1)}, bf16[256,1152]{1,0:T(8,128)(2,1)}, u32[]{:S(2)}, u32[]{:S(2)}) collective-permute-start(bf16[256,1152]{1,0:T(8,128)(2,1)} %pad_maximum_fusion.6), channel_id=1, source_target_pairs={{0,4},{2,6},{4,0},{6,2},{8,12},{10,14},{12,8},{14,10},{16,20},{18,... | collective-permute-start | bytes 1769480 | tf_op jit(solution)/shard_map/ppermute | solution.py:99
  79.9 25.5 %collective-permute-start.12 = (bf16[256,1152]{1,0:T(8,128)(2,1)}, bf16[256,1152]{1,0:T(8,128)(2,1)}, u32[]{:S(2)}, u32[]{:S(2)}) collective-permute-start(bf16[256,1152]{1,0:T(8,128)(2,1)} %pad_maximum_fusion.5), channel_id=1, source_target_pairs={{0,2},{2,0},{4,6},{6,4},{8,10},{10,8},{12,14},{14,12},{16,18},{18,... | collective-permute-start | bytes 1769480 | tf_op jit(solution)/shard_map/ppermute | solution.py:99
  80.1 19.2 %collective-permute-start.13 = (bf16[256,1152]{1,0:T(8,128)(2,1)}, bf16[256,1152]{1,0:T(8,128)(2,1)}, u32[]{:S(2)}, u32[]{:S(2)}) collective-permute-start(bf16[256,1152]{1,0:T(8,128)(2,1)} %pad_maximum_fusion.5), channel_id=1, source_target_pairs={{0,1},{1,0},{2,3},{3,2},{4,5},{5,4},{6,7},{7,6},{8,9},{9,8},{10,11... | collective-permute-start | bytes 1769480 | tf_op jit(solution)/shard_map/ppermute | solution.py:99
  81.9 2.7 %copy-start.7 = (f32[1152]{0:T(1024)S(1)}, f32[1152]{0:T(1024)}, u32[]{:S(2)}) copy-start(f32[1152]{0:T(1024)} %param.22) | copy-start | bytes 13828
  91.6 2.1 %copy-start.1 = (bf16[1024,1152]{1,0:T(8,128)(2,1)S(1)}, bf16[1024,1152]{1,0:T(8,128)(2,1)}, u32[]{:S(2)}) copy-start(bf16[1024,1152]{1,0:T(8,128)(2,1)} %copy-done) | copy-start | bytes 7077892
  98.9 8.5 %collective-permute-start.20 = (bf16[256,1152]{1,0:T(8,128)(2,1)}, bf16[256,1152]{1,0:T(8,128)(2,1)S(1)}, u32[]{:S(2)}, u32[]{:S(2)}) collective-permute-start(bf16[256,1152]{1,0:T(8,128)(2,1)} %collective-permute-done.19), channel_id=1, source_target_pairs={{0,2},{2,0},{4,6},{6,4},{8,10},{10,8},{12,14},{14,12},{16,18},{18,... | collective-permute-start | bytes 1769480 | tf_op jit(solution)/shard_map/ppermute | solution.py:99
  99.2 16.9 %collective-permute-start.14 = (bf16[256,1152]{1,0:T(8,128)(2,1)}, bf16[256,1152]{1,0:T(8,128)(2,1)S(1)}, u32[]{:S(2)}, u32[]{:S(2)}) collective-permute-start(bf16[256,1152]{1,0:T(8,128)(2,1)} %collective-permute-done.13), channel_id=1, source_target_pairs={{0,2},{2,0},{4,6},{6,4},{8,10},{10,8},{12,14},{14,12},{16,18},{18,... | collective-permute-start | bytes 1769480 | tf_op jit(solution)/shard_map/ppermute | solution.py:99
  105.4 2.0 %copy-start.10 = (s32[256]{0:T(256)S(1)}, s32[256]{0:T(256)}, u32[]{:S(2)}) copy-start(s32[256]{0:T(256)} %constant.89) | copy-start | bytes 3076
  113.5 2.7 %copy-start.9 = (s32[256]{0:T(256)S(1)}, s32[256]{0:T(256)}, u32[]{:S(2)}) copy-start(s32[256]{0:T(256)} %constant.88) | copy-start | bytes 3076
  134.0 3.1 %collective-permute-start.21 = (f32[288,1152]{1,0:T(8,128)S(1)}, f32[288,1152]{1,0:T(8,128)S(1)}, u32[]{:S(2)}, u32[]{:S(2)}) collective-permute-start(f32[288,1152]{1,0:T(8,128)S(1)} %convolution_add_fusion.3), channel_id=1, source_target_pairs={{0,2},{2,0},{4,6},{6,4},{8,10},{10,8},{12,14},{14,12},{16,18},{18,... | collective-permute-start | bytes 3981320 | tf_op jit(solution)/shard_map/ppermute | solution.py:99
  138.2 7.3 %collective-permute-start.22 = (bf16[288,1152]{1,0:T(8,128)(2,1)S(1)}, bf16[288,1152]{1,0:T(8,128)(2,1)S(1)}, u32[]{:S(2)}, u32[]{:S(2)}) collective-permute-start(bf16[288,1152]{1,0:T(8,128)(2,1)S(1)} %fusion.7), channel_id=1, source_target_pairs={{0,2},{2,0},{4,6},{6,4},{8,10},{10,8},{12,14},{14,12},{16,18},{18,... | collective-permute-start | bytes 1990664 | tf_op jit(solution)/shard_map/ppermute | solution.py:99
  143.7 1.2 collective-permute-start.23
  (3 other events, 3.7 us)
where the time goes:
time: 150 us; the launch traced here: 148 us
  matrix products  49.7 us (33%)
  waiting for transfers between devices  45.9 us (31%)
  starting transfers between devices  23.4 us (16%)
  other arithmetic  15 us (10%)
  between operations  9.48 us (6%)
  local copies, waits for them, and re-layouts  4.48 us (3%)
    ppermute x24, waiting for transfers between devices, swap(): return lax.ppermute(values, axis, [(i, i ^ bit) for i in range(count)])  45.9 us
    dot_general x18, matrix products, dot_f32(): lax.dot_general(left, right, (((left_axis,), (right_axis,)), ((), ())), p...  42.2 us
    ppermute x24, starting transfers between devices, swap(): return lax.ppermute(values, axis, [(i, i ^ bit) for i in range(count)])  23.4 us
    dot_general x1, matrix products, slice_plan(): branch = jnp.dot(hidden, mlp_down, preferred_element_type=jnp.float32)  7.56 us
    concatenate x12, other arithmetic, join(): jnp.concatenate([jnp.where(upper, other, mine), jnp.where(upper, mine, ot...  3.29 us
    unnamed x23, local copies, waits for them, and re-layouts  3.05 us
  transfers between devices with their start and end apart: 24, of which 8 were waited for; matrix products, arithmetic and copies ran while one was open for 30% of the time, Pallas kernels for 0%

commit v1 on v0

--- a/solution.py
+++ b/solution.py
@@ -1,11 +1,20 @@
+import functools
+
 import jax
 import jax.numpy as jnp
 import numpy as np
 from jax import lax
+from jax.experimental import pallas as pl
+from jax.experimental.pallas import tpu as pltpu
 from jax.sharding import PartitionSpec as P
 
 EPS = 1e-06
 CORE, Y, Z_LOW, Z_HIGH = 1, 2, 4, 8
+CAPTION_BASE = 128
+EXTRA = 8
+BLOCK = 256
+MIB = 1024 * 1024
+SMEM = pl.BlockSpec(memory_space=pltpu.SMEM)
 
 
 def layer_norm(values, gain):
@@ -115,26 +124,230 @@
     return (index & bit) != 0
 
 
+def after(value, *held):
+    return lax.optimization_barrier((value,) + held)[0]
+
+
+def half_of(values, upper, half):
+    return jnp.where(upper, values[half:], values[:half])
+
+
 def dot_f32(left, right, left_axis, right_axis):
     return lax.dot_general(
         left, right, (((left_axis,), (right_axis,)), ((), ())), preferred_element_type=jnp.float32
     )
 
 
-def after(value, *held):
-    return lax.optimization_barrier((value,) + held)[0]
-
-
-def half_of(values, upper, half):
-    return jnp.where(upper, values[half:], values[:half])
-
-
-def pair_terms(scores, matched):
+def rows_spec(block, width):
+    return pl.BlockSpec((block, width), lambda i: (i, 0))
+
+
+def whole_spec(shape):
+    return pl.BlockSpec(shape, lambda i: (0,) * len(shape))
+
+
+def text_kernel(
+    flags_ref, mine_a, other_a, mine_b, other_b, gain_ref, adapter_ref,
+    embed_ref, unit_ref, inverse_ref, caption_ref, turned_ref, held,
+):
+    step = pl.program_id(0)
+    rows = held.shape[1] - EXTRA
+    for color, (mine, other) in enumerate(((mine_a, other_a), (mine_b, other_b))):
+        upper = flags_ref[1 + color]
+
+        @pl.when(step == 2 * color + upper)
+        def _():
+            held[...] = mine[...]
+
+        @pl.when(step == 2 * color + 1 - upper)
+        def _():
+            held[...] = other[...]
+
+    block = held[...]
+    values = block[:, :rows].reshape(-1, block.shape[-1]).astype(jnp.float32)
+    center = values - jnp.mean(values, axis=-1, keepdims=True)
+    spread = jnp.mean(center * center, axis=-1, keepdims=True)
+    normed = (center * lax.rsqrt(spread + EPS) * gain_ref[...]).astype(jnp.bfloat16)
+    texts = jnp.dot(normed, adapter_ref[...], preferred_element_type=jnp.float32)
+    inverse = lax.rsqrt(jnp.sum(texts * texts, axis=-1, keepdims=True) + EPS)
+    unit = texts * inverse
+    unit_ref[...] = unit
+    inverse_ref[...] = inverse
+    embed_ref[...] = unit.astype(jnp.bfloat16)
+    row = lax.broadcasted_iota(jnp.int32, (rows, 2 * rows), 0)
+    lane = lax.broadcasted_iota(jnp.int32, (rows, 2 * rows), 1)
+    places = jnp.where(lane == row, float(CAPTION_BASE), jnp.where(lane == row + rows, 1.0, 0.0))
+    for k in range(block.shape[0]):
+        parts = block[k, rows : rows + EXTRA, : 2 * rows].astype(jnp.float32)[:1]
+        number = jnp.sum(parts * places, axis=-1, keepdims=True)
+        caption_ref[k * rows : (k + 1) * rows, :] = number.astype(jnp.int32)
+    turned = normed.T
+    half = turned.shape[0] // 2
+
+    @pl.when(flags_ref[0] == 0)
+    def _():
+        turned_ref[...] = turned[:half]
+
+    @pl.when(flags_ref[0] != 0)
+    def _():
+        turned_ref[...] = turned[half:]
+
+
+def text_side(flags, pieces, gain, adapter):
+    parts, padded, width = pieces[0].shape
+    block = parts * (padded - EXTRA)
+    count = 4 * block
+    half = width // 2
+    return pl.pallas_call(
+        text_kernel,
+        grid=(4,),
+        in_specs=[SMEM]
+        + [whole_spec(piece.shape) for piece in pieces]
+        + [whole_spec((1, width)), whole_spec((width, width))],
+        out_specs=[
+            rows_spec(block, width),
+            rows_spec(block, width),
+            rows_spec(block, 1),
+            rows_spec(block, 1),
+            pl.BlockSpec((half, block), lambda i: (0, i)),
+        ],
+        out_shape=[
+            jax.ShapeDtypeStruct((count, width), jnp.bfloat16),
+            jax.ShapeDtypeStruct((count, width), jnp.float32),
+            jax.ShapeDtypeStruct((count, 1), jnp.float32),
+            jax.ShapeDtypeStruct((count, 1), jnp.int32),
+            jax.ShapeDtypeStruct((half, count), jnp.bfloat16),
+        ],
+        scratch_shapes=[pltpu.VMEM(pieces[0].shape, jnp.bfloat16)],
+        compiler_params=pltpu.CompilerParams(vmem_limit_bytes=40 * MIB),
+        cost_estimate=pl.CostEstimate(
+            flops=4 * count * width * width, bytes_accessed=10 * count * width, transcendentals=0
+        ),
+    )(flags, *pieces, gain.reshape(1, width), adapter)
+
+
+def score_block(embed, caption, images, place, scale, shift):
+    scores = scale * dot_f32(embed, images, 1, 1) + shift
+    matched = caption == place
     decay = jnp.exp(-jnp.abs(scores))
-    loss = jnp.maximum(scores, 0.0) + jnp.log1p(decay) - jnp.where(matched, scores, 0.0)
     ratio = 1.0 / (1.0 + decay)
-    above = jnp.where((scores >= 0.0) != matched, ratio, decay * ratio)
-    return loss, jnp.where(matched, -above, above)
+    weight = jnp.where((scores >= 0.0) != matched, ratio, decay * ratio)
+    weight = jnp.where(matched, -weight, weight).astype(jnp.bfloat16)
+    grads = jnp.dot(weight, images, preferred_element_type=jnp.float32)
+    linear = jnp.maximum(scores, 0.0) - jnp.where(matched, scores, 0.0)
+    grown = decay
+    while grown.shape[0] > 16:
+        half = grown.shape[0] // 2
+        low, high = grown[:half], grown[half:]
+        grown = low + high + low * high
+    loss = jnp.sum(linear, axis=0, keepdims=True) + jnp.sum(jnp.log1p(grown), axis=0, keepdims=True)
+    return grads, jnp.sum(loss, axis=1, keepdims=True)
+
+
+def gather_parts(offsets_ref, parts, places, images, place):
+    at = 0
+    for k, (part, row) in enumerate(zip(parts, places)):
+        count = part.shape[0]
+        images[at : at + count, :] = part[...]
+        place[:, at : at + count] = row[...] + offsets_ref[k]
+        at += count
+
+
+def early_kernel(parts, knobs_ref, offsets_ref, embed_ref, caption_ref, *refs):
+    grads_ref, loss_ref, images, place = refs[2 * parts :]
+
+    @pl.when(pl.program_id(0) == 0)
+    def _():
+        gather_parts(offsets_ref, refs[:parts], refs[parts : 2 * parts], images, place)
+        loss_ref[...] = jnp.zeros_like(loss_ref)
+
+    grads, loss = score_block(
+        embed_ref[...], caption_ref[...], images[...], place[...], knobs_ref[0], knobs_ref[1]
+    )
+    grads_ref[...] = grads
+    loss_ref[...] += jnp.broadcast_to(loss, loss_ref.shape)
+
+
+def late_kernel(
+    parts, knobs_ref, offsets_ref, embed_ref, caption_ref,
+    early_ref, early_loss, unit_ref, inverse_ref, turned_ref, *refs,
+):
+    out_ref, images, place = refs[2 * parts :]
+    half = turned_ref.shape[0]
+
+    @pl.when(pl.program_id(0) == 0)
+    def _():
+        gather_parts(offsets_ref, refs[:parts], refs[parts : 2 * parts], images, place)
+        out_ref[:half, :] = jnp.zeros((half, out_ref.shape[1]), jnp.float32)
+        out_ref[half:, :] = jnp.broadcast_to(early_loss[0:1, 0:1], (EXTRA, out_ref.shape[1]))
+
+    grads, loss = score_block(
+        embed_ref[...], caption_ref[...], images[...], place[...], knobs_ref[0], knobs_ref[1]
+    )
+    unit = unit_ref[...]
+    scaled = (grads + early_ref[...]) * knobs_ref[2]
+    along = jnp.sum(unit * scaled, axis=-1, keepdims=True)
+    resid = (scaled - unit * along) * inverse_ref[...]
+    top = resid.astype(jnp.bfloat16)
+    rest = (resid - top.astype(jnp.float32)).astype(jnp.bfloat16)
+    turned = turned_ref[...]
+    out_ref[:half, :] += jnp.dot(turned, top, preferred_element_type=jnp.float32) + jnp.dot(
+        turned, rest, preferred_element_type=jnp.float32
+    )
+    out_ref[half:, :] += jnp.broadcast_to(loss, (EXTRA, out_ref.shape[1]))
+
+
+def score_specs(embed, images, places):
+    count, width = embed.shape
+    total = sum(part.shape[0] for part in images)
+    specs = [SMEM, SMEM, rows_spec(BLOCK, width), rows_spec(BLOCK, 1)]
+    tail = [whole_spec(part.shape) for part in images] + [whole_spec(row.shape) for row in places]
+    scratch = [pltpu.VMEM((total, width), jnp.bfloat16), pltpu.VMEM((1, total), jnp.int32)]
+    return count, width, total, specs, tail, scratch
+
+
+def early_scores(knobs, offsets, embed, caption, images, places):
+    count, width, total, specs, tail, scratch = score_specs(embed, images, places)
+    return pl.pallas_call(
+        functools.partial(early_kernel, len(images)),
+        grid=(count // BLOCK,),
+        in_specs=specs + tail,
+        out_specs=[rows_spec(BLOCK, width), whole_spec((8, 128))],
+        out_shape=[
+            jax.ShapeDtypeStruct((count, width), jnp.float32),
+            jax.ShapeDtypeStruct((8, 128), jnp.float32),
+        ],
+        scratch_shapes=scratch,
+        compiler_params=pltpu.CompilerParams(vmem_limit_bytes=40 * MIB),
+        cost_estimate=pl.CostEstimate(
+            flops=8 * count * width * total, bytes_accessed=8 * count * width, transcendentals=0
+        ),
+    )(knobs, offsets, embed, caption, *images, *places)
+
+
+def late_scores(knobs, offsets, embed, caption, early, early_loss, unit, inverse, turned, images, places):
+    count, width, total, specs, tail, scratch = score_specs(embed, images, places)
+    half = turned.shape[0]
+    return pl.pallas_call(
+        functools.partial(late_kernel, len(images)),
+        grid=(count // BLOCK,),
+        in_specs=specs
+        + [
+            rows_spec(BLOCK, width),
+            whole_spec((8, 128)),
+            rows_spec(BLOCK, width),
+            rows_spec(BLOCK, 1),
+            pl.BlockSpec((half, BLOCK), lambda i: (0, i)),
+        ]
+        + tail,
+        out_specs=whole_spec((half + EXTRA, width)),
+        out_shape=jax.ShapeDtypeStruct((half + EXTRA, width), jnp.float32),
+        scratch_shapes=scratch,
+        compiler_params=pltpu.CompilerParams(vmem_limit_bytes=48 * MIB),
+        cost_estimate=pl.CostEstimate(
+            flops=8 * count * width * (total + half), bytes_accessed=16 * count * width, transcendentals=0
+        ),
+    )(knobs, offsets, embed, caption, early, early_loss, unit, inverse, turned, *images, *places)
 
 
 def slice_plan(
@@ -149,34 +362,28 @@
     logit_scale,
     logit_bias,
 ):
-    rows = image_pooled.shape[0]
+    rows, width = image_pooled.shape
     half_rows = rows // 2
     quarter = rows // 4
     dp = lax.axis_index("dp")
     mp = lax.axis_index("mp")
-    dp_count = lax.axis_size("dp")
-    pair_count = rows * dp_count
-    width = image_pooled.shape[1]
-    own_c, own_y, own_z1, own_z2 = (bit_of(dp, b) for b in (CORE, Y, Z_LOW, Z_HIGH))
+    pair_count = rows * lax.axis_size("dp")
+    own_c = bit_of(dp, CORE)
     own_x = bit_of(mp, 1)
-    upper_of = {Y: own_y, Z_LOW: own_z1, Z_HIGH: own_z2}
-
-    def grow(values, bit, *held):
-        other = swap(values, "dp", bit)
-        if held:
-            other = after(other, *held)
-        return join(values, other, upper_of[bit])
-
-    parts = jnp.concatenate([caption_of // 128, caption_of % 128]).astype(jnp.bfloat16)
-    extra = jnp.pad(parts[None, :], ((0, 7), (0, width - 2 * rows)))
-    text_a = jnp.concatenate([text_last[:half_rows], extra], axis=0)
-    text_b = text_last[half_rows:]
-    image_pooled = after(image_pooled, text_a)
+
+    def grow(values, bit):
+        return join(values, swap(values, "dp", bit), bit_of(dp, bit))
+
+    parts = jnp.stack([caption_of // CAPTION_BASE, caption_of % CAPTION_BASE]).astype(jnp.bfloat16)
+    parts = parts.reshape(2, 2, half_rows).transpose(1, 0, 2).reshape(2, 1, rows)
+    extra = jnp.pad(parts, ((0, 0), (0, EXTRA - 1), (0, width - rows)))
+    packed = jnp.concatenate([text_last.reshape(2, half_rows, width), extra], axis=1)
+    text_a, text_b = packed[:1], packed[1:]
+    image_pooled = after(image_pooled, text_a, text_b)
     text_a = grow(text_a, Z_HIGH)
     text_b = grow(text_b, Y)
 
-    in_width = adapter.shape[0]
-    in_half = in_width // 2
+    in_half = adapter.shape[0] // 2
     piece = swap_x(half_of(adapter, own_c, in_half))
 
     image_norm = layer_norm(image_pooled, image_gain).astype(jnp.bfloat16)
@@ -197,6 +404,7 @@
     text_a = grow(text_a, Z_LOW)
     text_b = grow(text_b, Z_HIGH)
     other_adapter = join(piece, swap_core(piece), own_c)
+    full_adapter = join(adapter, other_adapter, own_x)
 
     image_a = image_unit[:quarter]
     image_b = image_unit[quarter:]
@@ -204,8 +412,7 @@
     image_b = join(image_b, swap_x(image_b), own_x)
     text_a = after(text_a, image_unit)
     text_b = after(text_b, image_unit)
-    text_a = grow(text_a, Y)
-    text_b = grow(text_b, Z_LOW)
+    pieces = [text_a, swap(text_a, "dp", Y), text_b, swap(text_b, "dp", Z_LOW)]
     image_a = grow(image_a, Z_LOW)
     image_b = grow(image_b, Z_HIGH)
     image_a = grow(image_a, Y)
@@ -213,72 +420,39 @@
     far_a = swap_x(image_a)
     far_b = swap(image_b, "dp", Y)
 
-    blocks = text_a.reshape(-1, half_rows + 8, width)
-    parts = blocks[:, half_rows, : 2 * rows].astype(jnp.int32)
-    captions = (parts[:, :rows] * 128 + parts[:, rows:]).reshape(2, 2, 2, 2, half_rows)
-    cap_a = captions[:, :, :, 0].reshape(-1)
-    cap_b = captions[:, :, :, 1].transpose(1, 2, 0, 3).reshape(-1)
-    caption = jnp.concatenate([cap_a, cap_b])
-    texts_raw = jnp.concatenate([blocks[:, :half_rows].reshape(-1, width), text_b], axis=0)
-
-    text_norm = layer_norm(texts_raw, text_gain).astype(jnp.bfloat16)
-    low, high = text_norm[:, :in_width], text_norm[:, in_width:]
-    text_part = jnp.where(own_x, high, low)
-    text_rest = jnp.where(own_x, low, high)
-    texts = dot_f32(text_part, adapter, 1, 0) + dot_f32(text_rest, other_adapter, 1, 0)
-    inverse = lax.rsqrt(jnp.sum(texts * texts, axis=-1, keepdims=True) + EPS)
-    text_unit = texts * inverse
-    text_embed = text_unit.astype(jnp.bfloat16)
-    scale = logit_scale[0]
-    shift = logit_bias[0]
+    flags = jnp.stack([mp, (dp & Y) // Y, (dp & Z_LOW) // Z_LOW]).astype(jnp.int32)
+    embed, unit, inverse, caption, turned = text_side(flags, pieces, text_gain, full_adapter)
 
     def places(bits):
         place = np.arange(quarter)
         for step in bits:
             place = np.concatenate([place, place + step])
-        return place
+        return place.astype(np.int32)[None, :]
 
     where_a = places((Z_HIGH * rows, Z_LOW * rows, Y * rows))
     where_b = places((half_rows, Z_HIGH * rows, Z_LOW * rows)) + quarter
+    where = [where_a, where_a, where_b, where_b]
     core_at = (dp & CORE) * rows
+    core_far = rows - core_at
     y_at = (dp & Y) * rows
     x_at = mp * half_rows
-
-    def score(images, place, offset):
-        partner = swap_core(images)
-        loss = 0.0
-        weights = []
-        for part, at in ((images, core_at), (partner, rows - core_at)):
-            scores = scale * dot_f32(text_embed, part, 1, 1) + shift
-            matched = (caption - (offset + at))[:, None] == place.astype(np.int32)[None, :]
-            terms, weight = pair_terms(scores, matched)
-            loss = loss + jnp.sum(terms)
-            weights.append(weight.astype(jnp.bfloat16))
-        return loss, dot_f32(jnp.concatenate(weights, 1), jnp.concatenate([images, partner]), 1, 0)
-
-    loss_a, grads_a = score(image_a, where_a, x_at)
-    loss_b, grads_b = score(image_b, where_b, y_at)
-    loss_c, grads_c = score(far_a, where_a, half_rows - x_at)
-    loss_d, grads_d = score(far_b, where_b, Y * rows - y_at)
-    loss = (loss_a + loss_c) + (loss_b + loss_d)
-    grads = (grads_a + grads_c) + (grads_b + grads_d)
-
-    resid = text_resid(grads, text_unit, inverse, scale / pair_count)
-    top = lax.reduce_precision(resid, 8, 7)
-    rest = (resid - top).astype(jnp.bfloat16)
-    top = top.astype(jnp.bfloat16)
-
-    def outer(part):
-        return dot_f32(part, top, 0, 0) + dot_f32(part, rest, 0, 0)
-
-    first, second = text_part[:, :in_half], text_part[:, in_half:]
-    given = outer(jnp.where(own_c, first, second))
-    kept = outer(jnp.where(own_c, second, first))
-    total = (kept + swap_core(given)).astype(jnp.bfloat16)
-    grad_adapter = join(total, swap_core(total), own_c)
-    loss = loss.reshape(1)
-    mean_loss = (loss + swap_core(loss)) / (pair_count * pair_count)
-    return grad_adapter, mean_loss
+    x_far = half_rows - x_at
+    y_far = Y * rows - y_at
+    near = jnp.stack([x_at + core_at, x_at + core_far, y_at + core_at, y_at + core_far])
+    far = jnp.stack([x_far + core_at, x_far + core_far, y_far + core_at, y_far + core_far])
+    scale = logit_scale[0]
+    knobs = jnp.stack([scale, logit_bias[0], scale / pair_count])
+
+    images = [image_a, swap_core(image_a), image_b, swap_core(image_b)]
+    early, early_loss = early_scores(knobs, near.astype(jnp.int32), embed, caption, images, where)
+    images = [far_a, swap_core(far_a), far_b, swap_core(far_b)]
+    part = late_scores(
+        knobs, far.astype(jnp.int32), embed, caption, early, early_loss, unit, inverse, turned, images, where
+    )
+    total = part + swap_core(part)
+    in_width = adapter.shape[0]
+    mean_loss = total[in_width, :1] / (pair_count * pair_count)
+    return total[:in_width].astype(jnp.bfloat16), mean_loss
 
 
 def solution(mesh):

time: 150 us -> 132 us (0.88); the launches traced: 148 us -> 132 us
  matrix products: 49.7 us -> 7.65 us
  Pallas kernels: 0 us -> 33.1 us
  other arithmetic: 15 us -> 9.13 us
  between operations: 9.48 us -> 4.03 us
  waiting for transfers between devices: 45.9 us -> 50.3 us
    dot_general x18 -> x0, matrix products: 42.2 us -> none  [dot_f32(): lax.dot_general(left, right, (((left_axis,), (right_axis,)), ((), ())), p...]
    pallas_call x0 -> x3, Pallas kernels: none -> 33.1 us  [the longest x1 16 us: late_scores(): pl.pallas_call(functools.partial(late_kernel, len(images)), grid=(count /...]
    ppermute x24 -> x22, waiting for transfers between devices: 45.9 us -> 50.3 us  [swap(): return lax.ppermute(values, axis, [(i, i ^ bit) for i in range(count)])]
    concatenate x12 -> x10, other arithmetic: 3.29 us -> 0.6 us  [join(): jnp.concatenate([jnp.where(upper, other, mine), jnp.where(upper, mine, ot...]
    convert_element_type x3 -> x0, other arithmetic: 2.43 us -> none  [the longest x1 2.09 us: slice_plan(): text_norm = layer_norm(texts_raw, text_gain).astype(jnp.bfloat16)]
    reduce_sum x2 -> x1, other arithmetic: 2.54 us -> 0.23 us  [layer_norm(): spread = jnp.mean(center * center, axis=-1, keepdims=True)]
    add x1, other arithmetic: 0.01 us -> 2.02 us  [slice_plan(): total = part + swap_core(part)]
    unnamed x23 -> x16, local copies, waits for them, and re-layouts: 3.05 us -> 2.21 us
  transfers between devices with their start and end apart: 24 -> 22, of which waited for: 8 -> 9; matrix products, arithmetic and copies ran while one was open for 30% -> 10% of each run, Pallas kernels for 0% -> 13%
where the time goes in v1:
time: 132 us
  waiting for transfers between devices  50.3 us (38%)
  Pallas kernels  33.1 us (25%)
  starting transfers between devices  23 us (17%)
  other arithmetic  9.13 us (7%)
  matrix products  7.65 us (6%)
  local copies, waits for them, and re-layouts  4.96 us (4%)
  between operations  4.03 us (3%)
    ppermute x22, waiting for transfers between devices, swap(): return lax.ppermute(values, axis, [(i, i ^ bit) for i in range(count)])  50.3 us
    ppermute x22, starting transfers between devices, swap(): return lax.ppermute(values, axis, [(i, i ^ bit) for i in range(count)])  23 us
    pallas_call x1, Pallas kernels, late_scores(): pl.pallas_call(functools.partial(late_kernel, len(images)), grid=(count /...  16 us
    pallas_call x1, Pallas kernels, early_scores(): pl.pallas_call(functools.partial(early_kernel, len(images)), grid=(count...  9.09 us
    pallas_call x1, Pallas kernels, text_side(): pl.pallas_call(text_kernel, grid=(4,), in_specs=[SMEM] + [whole_spec(piec...  7.99 us
    dot_general x1, matrix products, slice_plan(): branch = jnp.dot(hidden, mlp_down, preferred_element_type=jnp.float32)  7.65 us
  transfers between devices with their start and end apart: 22, of which 9 were waited for; matrix products, arithmetic and copies ran while one was open for 10% of the time, Pallas kernels for 13%

profile of v1, /device:TPU:0, one launch (start us, length us, event | category | flops | bytes accessed | tf_op | source)
XLA Modules:
  0.0 132.2 jit_solution(4871825417369488071)
XLA Ops:
  0.6 0.7 fusion.34
  1.6 1.0 fusion.20
  2.6 0.8 fusion.39
  3.4 4.0 %collective-permute-start = (bf16[1,72,1152]{2,1,0:T(8,128)(2,1)}, bf16[1,72,1152]{2,1,0:T(8,128)(2,1)}, u32[]{:S(2)}, u32[]{:S(2)}) collective-permute-start(bf16[1,72,1152]{2,1,0:T(8,128)(2,1)} %get-tuple-element.47), channel_id=1, source_target_pairs={{0,16},{2,18},{4,20},{6,22},{8,24},{10,26},{12,28},{14,30},{16,0},... | collective-permute-start | bytes 497672 | tf_op jit(solution)/shard_map/ppermute | solution.py:108
  7.4 1.5 %collective-permute-start.4 = (bf16[1,72,1152]{2,1,0:T(8,128)(2,1)}, bf16[1,72,1152]{2,1,0:T(8,128)(2,1)}, u32[]{:S(2)}, u32[]{:S(2)}) collective-permute-start(bf16[1,72,1152]{2,1,0:T(8,128)(2,1)} %get-tuple-element.46), channel_id=1, source_target_pairs={{0,4},{2,6},{4,0},{6,2},{8,12},{10,14},{12,8},{14,10},{16,20},{18,... | collective-permute-start | bytes 497672 | tf_op jit(solution)/shard_map/ppermute | solution.py:108
  9.3 7.6 %fusion.14 = f32[128,1152]{1,0:T(8,128)S(1)} fusion(bf16[2152,1152]{1,0:T(8,128)(2,1)} %param.18, bf16[1152,2152]{0,1:T(8,128)(2,1)} %param.17, bf16[128,1152]{1,0:T(8,128)(2,1)S(1)} %copy-done.5, f32[1152]{0:T(1024)S(1)} %copy-done.7, f32[128]{0:T(128)S(1)} %add_rsqrt_fusion.1, f32[128]{0:T(128)S(1)} %broadcast_multiply_fusion), kind=kOutput, calls=%fused_computation.30 | convolution fusion | flops 1272517632 | bytes 10806784 | tf_op jit(solution)/shard_map/dot_general | solution.py:393
  17.0 0.7 slice_select_fusion.1
  17.7 1.5 %collective-permute-start.2 = (f32[64,1152]{1,0:T(8,128)}, f32[64,1152]{1,0:T(8,128)S(1)}, u32[]{:S(2)}, u32[]{:S(2)}) collective-permute-start(f32[64,1152]{1,0:T(8,128)} %slice_select_fusion.1), channel_id=1, source_target_pairs={{0,1},{1,0},{2,3},{3,2},{4,5},{5,4},{6,7},{7,6},{8,9},{9,8},{10,11... | collective-permute-start | bytes 884744 | tf_op jit(solution)/shard_map/ppermute | solution.py:108
  19.2 0.9 slice_select_fusion
  22.3 1.1 broadcast_select_fusion.13
  23.4 4.5 %collective-permute-done.2 = f32[64,1152]{1,0:T(8,128)S(1)} collective-permute-done((f32[64,1152]{1,0:T(8,128)}, f32[64,1152]{1,0:T(8,128)S(1)}, u32[]{:S(2)}, u32[]{:S(2)}) %collective-permute-start.2) | collective-permute-done | bytes 294944 | tf_op jit(solution)/shard_map/ppermute | solution.py:108
  28.2 1.6 %collective-permute-start.13 = (bf16[32,1152]{1,0:T(8,128)(2,1)S(1)}, bf16[32,1152]{1,0:T(8,128)(2,1)S(1)}, u32[]{:S(2)}, u32[]{:S(2)}) collective-permute-start(bf16[32,1152]{1,0:T(8,128)(2,1)S(1)} %get-tuple-element.58), channel_id=1, source_target_pairs={{0,1},{1,0},{2,3},{3,2},{4,5},{5,4},{6,7},{7,6},{8,9},{9,8},{10,11... | collective-permute-start | bytes 221192 | tf_op jit(solution)/shard_map/ppermute | solution.py:108
  30.2 2.7 %collective-permute-start.5 = (bf16[2,72,1152]{2,1,0:T(8,128)(2,1)S(1)}, bf16[2,72,1152]{2,1,0:T(8,128)(2,1)S(1)}, u32[]{:S(2)}, u32[]{:S(2)}) collective-permute-start(bf16[2,72,1152]{2,1,0:T(8,128)(2,1)S(1)} %get-tuple-element.17), channel_id=1, source_target_pairs={{0,16},{2,18},{4,20},{6,22},{8,24},{10,26},{12,28},{14,30},{16,0},... | collective-permute-start | bytes 995336 | tf_op jit(solution)/shard_map/ppermute | solution.py:108
  32.9 1.6 %collective-permute-start.1 = (bf16[2,72,1152]{2,1,0:T(8,128)(2,1)S(1)}, bf16[2,72,1152]{2,1,0:T(8,128)(2,1)S(1)}, u32[]{:S(2)}, u32[]{:S(2)}) collective-permute-start(bf16[2,72,1152]{2,1,0:T(8,128)(2,1)S(1)} %get-tuple-element.15), channel_id=1, source_target_pairs={{0,8},{2,10},{4,12},{6,14},{8,0},{10,2},{12,4},{14,6},{16,24},{18,... | collective-permute-start | bytes 995336 | tf_op jit(solution)/shard_map/ppermute | solution.py:108
  34.4 7.5 %collective-permute-done.13 = bf16[32,1152]{1,0:T(8,128)(2,1)S(1)} collective-permute-done((bf16[32,1152]{1,0:T(8,128)(2,1)S(1)}, bf16[32,1152]{1,0:T(8,128)(2,1)S(1)}, u32[]{:S(2)}, u32[]{:S(2)}) %collective-permute-start.13) | collective-permute-done | bytes 73760 | tf_op jit(solution)/shard_map/ppermute | solution.py:108
  42.0 1.6 %collective-permute-start.10 = (bf16[64,1152]{1,0:T(8,128)(2,1)S(1)}, bf16[64,1152]{1,0:T(8,128)(2,1)S(1)}, u32[]{:S(2)}, u32[]{:S(2)}) collective-permute-start(bf16[64,1152]{1,0:T(8,128)(2,1)S(1)} %pad_maximum_fusion.10), channel_id=1, source_target_pairs={{0,8},{2,10},{4,12},{6,14},{8,0},{10,2},{12,4},{14,6},{16,24},{18,... | collective-permute-start | bytes 442376 | tf_op jit(solution)/shard_map/ppermute | solution.py:108
  44.1 5.7 %collective-permute-done.5 = bf16[2,72,1152]{2,1,0:T(8,128)(2,1)S(1)} collective-permute-done((bf16[2,72,1152]{2,1,0:T(8,128)(2,1)S(1)}, bf16[2,72,1152]{2,1,0:T(8,128)(2,1)S(1)}, u32[]{:S(2)}, u32[]{:S(2)}) %collective-permute-start.5) | collective-permute-done | bytes 331808 | tf_op jit(solution)/shard_map/ppermute | solution.py:108
  50.1 3.2 %collective-permute-done.10 = bf16[64,1152]{1,0:T(8,128)(2,1)S(1)} collective-permute-done((bf16[64,1152]{1,0:T(8,128)(2,1)S(1)}, bf16[64,1152]{1,0:T(8,128)(2,1)S(1)}, u32[]{:S(2)}, u32[]{:S(2)}) %collective-permute-start.10) | collective-permute-done | bytes 147488 | tf_op jit(solution)/shard_map/ppermute | solution.py:108
  53.5 3.3 %collective-permute-start.15 = (bf16[128,1152]{1,0:T(8,128)(2,1)S(1)}, bf16[128,1152]{1,0:T(8,128)(2,1)S(1)}, u32[]{:S(2)}, u32[]{:S(2)}) collective-permute-start(bf16[128,1152]{1,0:T(8,128)(2,1)S(1)} %pad_maximum_fusion.9), channel_id=1, source_target_pairs={{0,8},{2,10},{4,12},{6,14},{8,0},{10,2},{12,4},{14,6},{16,24},{18,... | collective-permute-start | bytes 884744 | tf_op jit(solution)/shard_map/ppermute | solution.py:108
  57.5 1.6 %collective-permute-start.11 = (bf16[128,1152]{1,0:T(8,128)(2,1)S(1)}, bf16[128,1152]{1,0:T(8,128)(2,1)S(1)}, u32[]{:S(2)}, u32[]{:S(2)}) collective-permute-start(bf16[128,1152]{1,0:T(8,128)(2,1)S(1)} %pad_maximum_fusion.8), channel_id=1, source_target_pairs={{0,4},{2,6},{4,0},{6,2},{8,12},{10,14},{12,8},{14,10},{16,20},{18,... | collective-permute-start | bytes 884744 | tf_op jit(solution)/shard_map/ppermute | solution.py:108
  59.1 14.7 %collective-permute-done.15 = bf16[128,1152]{1,0:T(8,128)(2,1)S(1)} collective-permute-done((bf16[128,1152]{1,0:T(8,128)(2,1)S(1)}, bf16[128,1152]{1,0:T(8,128)(2,1)S(1)}, u32[]{:S(2)}, u32[]{:S(2)}) %collective-permute-start.15) | collective-permute-done | bytes 294944 | tf_op jit(solution)/shard_map/ppermute | solution.py:108
  74.1 2.7 %collective-permute-done.11 = bf16[128,1152]{1,0:T(8,128)(2,1)S(1)} collective-permute-done((bf16[128,1152]{1,0:T(8,128)(2,1)S(1)}, bf16[128,1152]{1,0:T(8,128)(2,1)S(1)}, u32[]{:S(2)}, u32[]{:S(2)}) %collective-permute-start.11) | collective-permute-done | bytes 294944 | tf_op jit(solution)/shard_map/ppermute | solution.py:108
  78.2 0.6 collective-permute-start.17
  79.1 8.0 %shard_map.131 = (bf16[1024,1152]{1,0:T(8,128)(2,1)S(1)}, f32[1024,1152]{1,0:T(8,128)}, f32[1024,1]{1,0:T(8,128)S(1)}, s32[1024,1]{1,0:T(8,128)S(1)}, bf16[576,1024]{1,0:T(8,128)(2,1)S(1)}) custom-call(s32[3]{0:T(128)S(1)} %pad_add_fusion.1.flags_ref, bf16[4,72,1152]{2,1,0:T(8,128)(2,1)S(1)} %pad_maximum_fusion.2.mine_a, ...), custom_call_target="tpu_custom_call" | custom-call | flops 5435817984 | bytes 11796480 | tf_op jit(solution)/shard_map/pallas_call | solution.py:201
  87.1 2.7 %collective-permute-done.19.refs_2_ = bf16[256,1152]{1,0:T(8,128)(2,1)S(1)} collective-permute-done((bf16[256,1152]{1,0:T(8,128)(2,1)S(1)}, bf16[256,1152]{1,0:T(8,128)(2,1)S(1)}, u32[]{:S(2)}, u32[]{:S(2)}) %collective-permute-start.19) | collective-permute-done | bytes 589856 | tf_op jit(solution)/shard_map/ppermute | solution.py:108
  89.8 4.2 %collective-permute-done.17.refs_0_ = bf16[256,1152]{1,0:T(8,128)(2,1)S(1)} collective-permute-done((bf16[256,1152]{1,0:T(8,128)(2,1)S(1)}, bf16[256,1152]{1,0:T(8,128)(2,1)S(1)}, u32[]{:S(2)}, u32[]{:S(2)}) %collective-permute-start.17) | collective-permute-done | bytes 589856 | tf_op jit(solution)/shard_map/ppermute | solution.py:108
  94.0 9.1 %shard_map.132 = (f32[1024,1152]{1,0:T(8,128)S(1)}, f32[8,128]{1,0:T(8,128)S(1)}) custom-call(f32[3]{0:T(128)S(1)} %pad_maximum_fusion.12.knobs_ref, s32[4]{0:T(128)S(1)} %pad_add_fusion.2.offsets_ref, bf16[1024,1152]{1,0:T(8,128)(2,1)S(1)} %get-tuple-element.19.embed_ref, s32[1024,1]{1,0:T(8,128)S(1)} %get-tuple-element.20.caption_ref, ...), custom_call_target="tpu_custom_call" | custom-call | flops 9663676416 | bytes 9437184 | tf_op jit(solution)/shard_map/pallas_call | solution.py:311
  103.2 2.2 %copy-done.3 = f32[1024,1152]{1,0:T(8,128)} copy-done((f32[1024,1152]{1,0:T(8,128)}, f32[1024,1152]{1,0:T(8,128)S(1)}, u32[]{:S(2)}) %copy-start.3) | copy-done | bytes 4718616
  105.3 16.0 %shard_map.133 = f32[584,1152]{1,0:T(8,128)} custom-call(f32[3]{0:T(128)S(1)} %pad_maximum_fusion.12.knobs_ref, s32[4]{0:T(128)S(1)} %pad_add_fusion.offsets_ref, bf16[1024,1152]{1,0:T(8,128)(2,1)} %copy-done.2, s32[1024,1]{1,0:T(8,128)S(1)} %get-tuple-element.20.caption_ref, f32[1024,1152]{1,0:T(8,128)} %copy-done.3, ...), custom_call_target="tpu_custom_call" | custom-call | flops 15099494400 | bytes 18874368 | tf_op jit(solution)/shard_map/pallas_call | solution.py:331
  121.9 4.8 %collective-permute-done.21 = f32[584,1152]{1,0:T(8,128)S(1)} collective-permute-done((f32[584,1152]{1,0:T(8,128)}, f32[584,1152]{1,0:T(8,128)S(1)}, u32[]{:S(2)}, u32[]{:S(2)}) %collective-permute-start.21) | collective-permute-done | bytes 2691104 | tf_op jit(solution)/shard_map/ppermute | solution.py:108
  126.7 2.0 %add.93 = f32[584,1152]{1,0:T(8,128)S(1)} add(f32[584,1152]{1,0:T(8,128)} %shard_map.133, f32[584,1152]{1,0:T(8,128)S(1)} %collective-permute-done.21) | non-fusion elementwise | flops 672768 | bytes 8073216 | tf_op jit(solution)/shard_map/add | solution.py:452
  128.7 1.2 slice.76
  (77 shorter events, 6.6 us)
Async XLA Ops:
  0.6 8.3 %copy-start.5 = (bf16[128,1152]{1,0:T(8,128)(2,1)S(1)}, bf16[128,1152]{1,0:T(8,128)(2,1)}, u32[]{:S(2)}) copy-start(bf16[128,1152]{1,0:T(8,128)(2,1)} %param.12) | copy-start | bytes 884740
  0.6 8.7 %copy-start.7 = (f32[1152]{0:T(1024)S(1)}, f32[1152]{0:T(1024)}, u32[]{:S(2)}) copy-start(f32[1152]{0:T(1024)} %param.15) | copy-start | bytes 13828
  3.4 18.9 %collective-permute-start = (bf16[1,72,1152]{2,1,0:T(8,128)(2,1)}, bf16[1,72,1152]{2,1,0:T(8,128)(2,1)}, u32[]{:S(2)}, u32[]{:S(2)}) collective-permute-start(bf16[1,72,1152]{2,1,0:T(8,128)(2,1)} %get-tuple-element.47), channel_id=1, source_target_pairs={{0,16},{2,18},{4,20},{6,22},{8,24},{10,26},{12,28},{14,30},{16,0},... | collective-permute-start | bytes 497672 | tf_op jit(solution)/shard_map/ppermute | solution.py:108
  7.4 14.9 %collective-permute-start.4 = (bf16[1,72,1152]{2,1,0:T(8,128)(2,1)}, bf16[1,72,1152]{2,1,0:T(8,128)(2,1)}, u32[]{:S(2)}, u32[]{:S(2)}) collective-permute-start(bf16[1,72,1152]{2,1,0:T(8,128)(2,1)} %get-tuple-element.46), channel_id=1, source_target_pairs={{0,4},{2,6},{4,0},{6,2},{8,12},{10,14},{12,8},{14,10},{16,20},{18,... | collective-permute-start | bytes 497672 | tf_op jit(solution)/shard_map/ppermute | solution.py:108
  9.3 9.9 %copy-start.4 = (bf16[576,1152]{1,0:T(8,128)(2,1)S(1)}, bf16[576,1152]{1,0:T(8,128)(2,1)}, u32[]{:S(2)}) copy-start(bf16[576,1152]{1,0:T(8,128)(2,1)} %param.19) | copy-start | bytes 3981316
  17.0 5.2 %copy-start.6 = (f32[1152]{0:T(1024)S(1)}, f32[1152]{0:T(1024)}, u32[]{:S(2)}) copy-start(f32[1152]{0:T(1024)} %param.16) | copy-start | bytes 13828
  17.7 10.2 %collective-permute-start.2 = (f32[64,1152]{1,0:T(8,128)}, f32[64,1152]{1,0:T(8,128)S(1)}, u32[]{:S(2)}, u32[]{:S(2)}) collective-permute-start(f32[64,1152]{1,0:T(8,128)} %slice_select_fusion.1), channel_id=1, source_target_pairs={{0,1},{1,0},{2,3},{3,2},{4,5},{5,4},{6,7},{7,6},{8,9},{9,8},{10,11... | collective-permute-start | bytes 884744 | tf_op jit(solution)/shard_map/ppermute | solution.py:108
  20.2 38.9 %collective-permute-start.7 = (bf16[288,1152]{1,0:T(8,128)(2,1)}, bf16[288,1152]{1,0:T(8,128)(2,1)S(1)}, u32[]{:S(2)}, u32[]{:S(2)}) collective-permute-start(bf16[288,1152]{1,0:T(8,128)(2,1)} %slice_select_fusion), channel_id=1, source_target_pairs={{0,1},{1,0},{2,3},{3,2},{4,5},{5,4},{6,7},{7,6},{8,9},{9,8},{10,11... | collective-permute-start | bytes 1990664 | tf_op jit(solution)/shard_map/ppermute | solution.py:108
  28.2 13.7 %collective-permute-start.13 = (bf16[32,1152]{1,0:T(8,128)(2,1)S(1)}, bf16[32,1152]{1,0:T(8,128)(2,1)S(1)}, u32[]{:S(2)}, u32[]{:S(2)}) collective-permute-start(bf16[32,1152]{1,0:T(8,128)(2,1)S(1)} %get-tuple-element.58), channel_id=1, source_target_pairs={{0,1},{1,0},{2,3},{3,2},{4,5},{5,4},{6,7},{7,6},{8,9},{9,8},{10,11... | collective-permute-start | bytes 221192 | tf_op jit(solution)/shard_map/ppermute | solution.py:108
  29.8 12.2 %collective-permute-start.9 = (bf16[32,1152]{1,0:T(8,128)(2,1)S(1)}, bf16[32,1152]{1,0:T(8,128)(2,1)S(1)}, u32[]{:S(2)}, u32[]{:S(2)}) collective-permute-start(bf16[32,1152]{1,0:T(8,128)(2,1)S(1)} %get-tuple-element.59), channel_id=1, source_target_pairs={{0,16},{2,18},{4,20},{6,22},{8,24},{10,26},{12,28},{14,30},{16,0},... | collective-permute-start | bytes 221192 | tf_op jit(solution)/shard_map/ppermute | solution.py:108
  30.2 19.6 %collective-permute-start.5 = (bf16[2,72,1152]{2,1,0:T(8,128)(2,1)S(1)}, bf16[2,72,1152]{2,1,0:T(8,128)(2,1)S(1)}, u32[]{:S(2)}, u32[]{:S(2)}) collective-permute-start(bf16[2,72,1152]{2,1,0:T(8,128)(2,1)S(1)} %get-tuple-element.17), channel_id=1, source_target_pairs={{0,16},{2,18},{4,20},{6,22},{8,24},{10,26},{12,28},{14,30},{16,0},... | collective-permute-start | bytes 995336 | tf_op jit(solution)/shard_map/ppermute | solution.py:108
  32.9 17.2 %collective-permute-start.1 = (bf16[2,72,1152]{2,1,0:T(8,128)(2,1)S(1)}, bf16[2,72,1152]{2,1,0:T(8,128)(2,1)S(1)}, u32[]{:S(2)}, u32[]{:S(2)}) collective-permute-start(bf16[2,72,1152]{2,1,0:T(8,128)(2,1)S(1)} %get-tuple-element.15), channel_id=1, source_target_pairs={{0,8},{2,10},{4,12},{6,14},{8,0},{10,2},{12,4},{14,6},{16,24},{18,... | collective-permute-start | bytes 995336 | tf_op jit(solution)/shard_map/ppermute | solution.py:108
  42.0 11.4 %collective-permute-start.10 = (bf16[64,1152]{1,0:T(8,128)(2,1)S(1)}, bf16[64,1152]{1,0:T(8,128)(2,1)S(1)}, u32[]{:S(2)}, u32[]{:S(2)}) collective-permute-start(bf16[64,1152]{1,0:T(8,128)(2,1)S(1)} %pad_maximum_fusion.10), channel_id=1, source_target_pairs={{0,8},{2,10},{4,12},{6,14},{8,0},{10,2},{12,4},{14,6},{16,24},{18,... | collective-permute-start | bytes 442376 | tf_op jit(solution)/shard_map/ppermute | solution.py:108
  43.7 9.7 %collective-permute-start.14 = (bf16[64,1152]{1,0:T(8,128)(2,1)S(1)}, bf16[64,1152]{1,0:T(8,128)(2,1)S(1)}, u32[]{:S(2)}, u32[]{:S(2)}) collective-permute-start(bf16[64,1152]{1,0:T(8,128)(2,1)S(1)} %pad_maximum_fusion.11), channel_id=1, source_target_pairs={{0,16},{2,18},{4,20},{6,22},{8,24},{10,26},{12,28},{14,30},{16,0},... | collective-permute-start | bytes 442376 | tf_op jit(solution)/shard_map/ppermute | solution.py:108
  50.0 28.2 %collective-permute-start.6 = (bf16[4,72,1152]{2,1,0:T(8,128)(2,1)S(1)}, bf16[4,72,1152]{2,1,0:T(8,128)(2,1)S(1)}, u32[]{:S(2)}, u32[]{:S(2)}) collective-permute-start(bf16[4,72,1152]{2,1,0:T(8,128)(2,1)S(1)} %pad_maximum_fusion.3.mine_b), channel_id=1, source_target_pairs={{0,8},{2,10},{4,12},{6,14},{8,0},{10,2},{12,4},{14,6},{16,24},{18,... | collective-permute-start | bytes 1990664 | tf_op jit(solution)/shard_map/ppermute | solution.py:108
  53.5 20.3 %collective-permute-start.15 = (bf16[128,1152]{1,0:T(8,128)(2,1)S(1)}, bf16[128,1152]{1,0:T(8,128)(2,1)S(1)}, u32[]{:S(2)}, u32[]{:S(2)}) collective-permute-start(bf16[128,1152]{1,0:T(8,128)(2,1)S(1)} %pad_maximum_fusion.9), channel_id=1, source_target_pairs={{0,8},{2,10},{4,12},{6,14},{8,0},{10,2},{12,4},{14,6},{16,24},{18,... | collective-permute-start | bytes 884744 | tf_op jit(solution)/shard_map/ppermute | solution.py:108
  56.9 22.2 %collective-permute-start.3 = (bf16[4,72,1152]{2,1,0:T(8,128)(2,1)S(1)}, bf16[4,72,1152]{2,1,0:T(8,128)(2,1)S(1)}, u32[]{:S(2)}, u32[]{:S(2)}) collective-permute-start(bf16[4,72,1152]{2,1,0:T(8,128)(2,1)S(1)} %pad_maximum_fusion.2.mine_a), channel_id=1, source_target_pairs={{0,4},{2,6},{4,0},{6,2},{8,12},{10,14},{12,8},{14,10},{16,20},{18,... | collective-permute-start | bytes 1990664 | tf_op jit(solution)/shard_map/ppermute | solution.py:108
  57.5 19.3 %collective-permute-start.11 = (bf16[128,1152]{1,0:T(8,128)(2,1)S(1)}, bf16[128,1152]{1,0:T(8,128)(2,1)S(1)}, u32[]{:S(2)}, u32[]{:S(2)}) collective-permute-start(bf16[128,1152]{1,0:T(8,128)(2,1)S(1)} %pad_maximum_fusion.8), channel_id=1, source_target_pairs={{0,4},{2,6},{4,0},{6,2},{8,12},{10,14},{12,8},{14,10},{16,20},{18,... | collective-permute-start | bytes 884744 | tf_op jit(solution)/shard_map/ppermute | solution.py:108
  59.1 18.4 %collective-permute-start.8 = (bf16[288,1152]{1,0:T(8,128)(2,1)S(1)}, bf16[288,1152]{1,0:T(8,128)(2,1)S(1)}, u32[]{:S(2)}, u32[]{:S(2)}) collective-permute-start(bf16[288,1152]{1,0:T(8,128)(2,1)S(1)} %collective-permute-done.7), channel_id=1, source_target_pairs={{0,2},{2,0},{4,6},{6,4},{8,10},{10,8},{12,14},{14,12},{16,18},{18,... | collective-permute-start | bytes 1990664 | tf_op jit(solution)/shard_map/ppermute | solution.py:108
  74.0 20.0 %collective-permute-start.16 = (bf16[256,1152]{1,0:T(8,128)(2,1)S(1)}, bf16[256,1152]{1,0:T(8,128)(2,1)S(1)}, u32[]{:S(2)}, u32[]{:S(2)}) collective-permute-start(bf16[256,1152]{1,0:T(8,128)(2,1)S(1)} %pad_maximum_fusion.5.refs_2_), channel_id=1, source_target_pairs={{0,2},{2,0},{4,6},{6,4},{8,10},{10,8},{12,14},{14,12},{16,18},{18,... | collective-permute-start | bytes 1769480 | tf_op jit(solution)/shard_map/ppermute | solution.py:108
  76.8 13.0 %collective-permute-start.19 = (bf16[256,1152]{1,0:T(8,128)(2,1)S(1)}, bf16[256,1152]{1,0:T(8,128)(2,1)S(1)}, u32[]{:S(2)}, u32[]{:S(2)}) collective-permute-start(bf16[256,1152]{1,0:T(8,128)(2,1)S(1)} %pad_maximum_fusion.5.refs_2_), channel_id=1, source_target_pairs={{0,4},{2,6},{4,0},{6,2},{8,12},{10,14},{12,8},{14,10},{16,20},{18,... | collective-permute-start | bytes 1769480 | tf_op jit(solution)/shard_map/ppermute | solution.py:108
  77.5 16.5 %collective-permute-start.12 = (bf16[256,1152]{1,0:T(8,128)(2,1)S(1)}, bf16[256,1152]{1,0:T(8,128)(2,1)S(1)}, u32[]{:S(2)}, u32[]{:S(2)}) collective-permute-start(bf16[256,1152]{1,0:T(8,128)(2,1)S(1)} %pad_maximum_fusion.4.refs_0_), channel_id=1, source_target_pairs={{0,2},{2,0},{4,6},{6,4},{8,10},{10,8},{12,14},{14,12},{16,18},{18,... | collective-permute-start | bytes 1769480 | tf_op jit(solution)/shard_map/ppermute | solution.py:108
  78.2 15.8 %collective-permute-start.17 = (bf16[256,1152]{1,0:T(8,128)(2,1)S(1)}, bf16[256,1152]{1,0:T(8,128)(2,1)S(1)}, u32[]{:S(2)}, u32[]{:S(2)}) collective-permute-start(bf16[256,1152]{1,0:T(8,128)(2,1)S(1)} %pad_maximum_fusion.4.refs_0_), channel_id=1, source_target_pairs={{0,1},{1,0},{2,3},{3,2},{4,5},{5,4},{6,7},{7,6},{8,9},{9,8},{10,11... | collective-permute-start | bytes 1769480 | tf_op jit(solution)/shard_map/ppermute | solution.py:108
  79.0 15.0 %copy-start = (s32[1,256]{1,0:T(1,128)S(1)}, s32[1,256]{1,0:T(1,128)}, u32[]{:S(2)}) copy-start(s32[1,256]{1,0:T(1,128)} %constant.98.clone.refs_4_.refs_5_) | copy-start | bytes 3076
  79.0 15.0 %copy-start.1 = (s32[1,256]{1,0:T(1,128)S(1)}, s32[1,256]{1,0:T(1,128)}, u32[]{:S(2)}) copy-start(s32[1,256]{1,0:T(1,128)} %constant.99.clone.refs_6_.refs_7_) | copy-start | bytes 3076
  87.1 16.1 %copy-start.2 = (bf16[1024,1152]{1,0:T(8,128)(2,1)}, bf16[1024,1152]{1,0:T(8,128)(2,1)S(1)}, u32[]{:S(2)}) copy-start(bf16[1024,1152]{1,0:T(8,128)(2,1)S(1)} %get-tuple-element.19.embed_ref) | copy-start | bytes 7077892
  89.8 15.5 %collective-permute-start.20 = (bf16[256,1152]{1,0:T(8,128)(2,1)S(1)}, bf16[256,1152]{1,0:T(8,128)(2,1)S(1)}, u32[]{:S(2)}, u32[]{:S(2)}) collective-permute-start(bf16[256,1152]{1,0:T(8,128)(2,1)S(1)} %collective-permute-done.19.refs_2_), channel_id=1, source_target_pairs={{0,2},{2,0},{4,6},{6,4},{8,10},{10,8},{12,14},{14,12},{16,18},{18,... | collective-permute-start | bytes 1769480 | tf_op jit(solution)/shard_map/ppermute | solution.py:108
  94.0 11.3 %collective-permute-start.18 = (bf16[256,1152]{1,0:T(8,128)(2,1)S(1)}, bf16[256,1152]{1,0:T(8,128)(2,1)S(1)}, u32[]{:S(2)}, u32[]{:S(2)}) collective-permute-start(bf16[256,1152]{1,0:T(8,128)(2,1)S(1)} %collective-permute-done.17.refs_0_), channel_id=1, source_target_pairs={{0,2},{2,0},{4,6},{6,4},{8,10},{10,8},{12,14},{14,12},{16,18},{18,... | collective-permute-start | bytes 1769480 | tf_op jit(solution)/shard_map/ppermute | solution.py:108
  103.1 2.2 %copy-start.3 = (f32[1024,1152]{1,0:T(8,128)}, f32[1024,1152]{1,0:T(8,128)S(1)}, u32[]{:S(2)}) copy-start(f32[1024,1152]{1,0:T(8,128)S(1)} %get-tuple-element.21.early_ref) | copy-start | bytes 14155780
  121.4 5.3 %collective-permute-start.21 = (f32[584,1152]{1,0:T(8,128)}, f32[584,1152]{1,0:T(8,128)S(1)}, u32[]{:S(2)}, u32[]{:S(2)}) collective-permute-start(f32[584,1152]{1,0:T(8,128)} %shard_map.133), channel_id=1, source_target_pairs={{0,2},{2,0},{4,6},{6,4},{8,10},{10,8},{12,14},{14,12},{16,18},{18,... | collective-permute-start | bytes 8073224 | tf_op jit(solution)/shard_map/ppermute | solution.py:108

commit v2 on v1

--- a/solution.py
+++ b/solution.py
@@ -13,7 +13,7 @@
 CAPTION_BASE = 128
 EXTRA = 8
 BLOCK = 256
-MIB = 1024 * 1024
+VMEM_LIMIT = 40 * 1024 * 1024
 SMEM = pl.BlockSpec(memory_space=pltpu.SMEM)
 
 
@@ -147,21 +147,28 @@
 
 
 def text_kernel(
-    flags_ref, mine_a, other_a, mine_b, other_b, gain_ref, adapter_ref,
+    flags_ref, own_ref, near_0, near_1, far_0, far_1, gain_ref, adapter_ref,
     embed_ref, unit_ref, inverse_ref, caption_ref, turned_ref, held,
 ):
     step = pl.program_id(0)
+    count = held.shape[0]
     rows = held.shape[1] - EXTRA
-    for color, (mine, other) in enumerate(((mine_a, other_a), (mine_b, other_b))):
-        upper = flags_ref[1 + color]
-
-        @pl.when(step == 2 * color + upper)
+    own, other = 2 * flags_ref[1], 2 - 2 * flags_ref[1]
+    for k in range(2):
+
+        @pl.when(step == own + k)
         def _():
-            held[...] = mine[...]
-
-        @pl.when(step == 2 * color + 1 - upper)
-        def _():
-            held[...] = other[...]
+            held[...] = own_ref[k * count : (k + 1) * count]
+
+    @pl.when(step == other + flags_ref[0])
+    def _():
+        held[0] = near_0[0]
+        held[1] = near_1[0]
+
+    @pl.when(step == other + 1 - flags_ref[0])
+    def _():
+        held[0] = far_0[0]
+        held[1] = far_1[0]
 
     block = held[...]
     values = block[:, :rows].reshape(-1, block.shape[-1]).astype(jnp.float32)
@@ -194,7 +201,8 @@
 
 
 def text_side(flags, pieces, gain, adapter):
-    parts, padded, width = pieces[0].shape
+    padded, width = pieces[1].shape[1:]
+    parts = 2
     block = parts * (padded - EXTRA)
     count = 4 * block
     half = width // 2
@@ -218,8 +226,8 @@
             jax.ShapeDtypeStruct((count, 1), jnp.int32),
             jax.ShapeDtypeStruct((half, count), jnp.bfloat16),
         ],
-        scratch_shapes=[pltpu.VMEM(pieces[0].shape, jnp.bfloat16)],
-        compiler_params=pltpu.CompilerParams(vmem_limit_bytes=40 * MIB),
+        scratch_shapes=[pltpu.VMEM((parts, padded, width), jnp.bfloat16)],
+        compiler_params=pltpu.CompilerParams(vmem_limit_bytes=VMEM_LIMIT),
         cost_estimate=pl.CostEstimate(
             flops=4 * count * width * width, bytes_accessed=10 * count * width, transcendentals=0
         ),
@@ -272,14 +280,13 @@
     parts, knobs_ref, offsets_ref, embed_ref, caption_ref,
     early_ref, early_loss, unit_ref, inverse_ref, turned_ref, *refs,
 ):
-    out_ref, images, place = refs[2 * parts :]
-    half = turned_ref.shape[0]
+    out_ref, loss_ref, images, place = refs[2 * parts :]
 
     @pl.when(pl.program_id(0) == 0)
     def _():
         gather_parts(offsets_ref, refs[:parts], refs[parts : 2 * parts], images, place)
-        out_ref[:half, :] = jnp.zeros((half, out_ref.shape[1]), jnp.float32)
-        out_ref[half:, :] = jnp.broadcast_to(early_loss[0:1, 0:1], (EXTRA, out_ref.shape[1]))
+        out_ref[...] = jnp.zeros_like(out_ref)
+        loss_ref[...] = early_loss[...]
 
     grads, loss = score_block(
         embed_ref[...], caption_ref[...], images[...], place[...], knobs_ref[0], knobs_ref[1]
@@ -291,10 +298,10 @@
     top = resid.astype(jnp.bfloat16)
     rest = (resid - top.astype(jnp.float32)).astype(jnp.bfloat16)
     turned = turned_ref[...]
-    out_ref[:half, :] += jnp.dot(turned, top, preferred_element_type=jnp.float32) + jnp.dot(
+    out_ref[...] += jnp.dot(turned, top, preferred_element_type=jnp.float32) + jnp.dot(
         turned, rest, preferred_element_type=jnp.float32
     )
-    out_ref[half:, :] += jnp.broadcast_to(loss, (EXTRA, out_ref.shape[1]))
+    loss_ref[...] += jnp.broadcast_to(loss, loss_ref.shape)
 
 
 def score_specs(embed, images, places):
@@ -318,7 +325,7 @@
             jax.ShapeDtypeStruct((8, 128), jnp.float32),
         ],
         scratch_shapes=scratch,
-        compiler_params=pltpu.CompilerParams(vmem_limit_bytes=40 * MIB),
+        compiler_params=pltpu.CompilerParams(vmem_limit_bytes=VMEM_LIMIT),
         cost_estimate=pl.CostEstimate(
             flops=8 * count * width * total, bytes_accessed=8 * count * width, transcendentals=0
         ),
@@ -340,10 +347,13 @@
             pl.BlockSpec((half, BLOCK), lambda i: (0, i)),
         ]
         + tail,
-        out_specs=whole_spec((half + EXTRA, width)),
-        out_shape=jax.ShapeDtypeStruct((half + EXTRA, width), jnp.float32),
+        out_specs=[whole_spec((half, width)), whole_spec((8, 128))],
+        out_shape=[
+            jax.ShapeDtypeStruct((half, width), jnp.float32),
+            jax.ShapeDtypeStruct((8, 128), jnp.float32),
+        ],
         scratch_shapes=scratch,
-        compiler_params=pltpu.CompilerParams(vmem_limit_bytes=48 * MIB),
+        compiler_params=pltpu.CompilerParams(vmem_limit_bytes=VMEM_LIMIT),
         cost_estimate=pl.CostEstimate(
             flops=8 * count * width * (total + half), bytes_accessed=16 * count * width, transcendentals=0
         ),
@@ -374,23 +384,25 @@
     def grow(values, bit):
         return join(values, swap(values, "dp", bit), bit_of(dp, bit))
 
-    parts = jnp.stack([caption_of // CAPTION_BASE, caption_of % CAPTION_BASE]).astype(jnp.bfloat16)
-    parts = parts.reshape(2, 2, half_rows).transpose(1, 0, 2).reshape(2, 1, rows)
-    extra = jnp.pad(parts, ((0, 0), (0, EXTRA - 1), (0, width - rows)))
-    packed = jnp.concatenate([text_last.reshape(2, half_rows, width), extra], axis=1)
-    text_a, text_b = packed[:1], packed[1:]
-    image_pooled = after(image_pooled, text_a, text_b)
-    text_a = grow(text_a, Z_HIGH)
-    text_b = grow(text_b, Y)
-
+    parts = jnp.concatenate([caption_of // CAPTION_BASE, caption_of % CAPTION_BASE])
+    extra = jnp.pad(parts.astype(jnp.bfloat16)[None, :], ((0, EXTRA - 1), (0, width - 2 * rows)))
+    packed = jnp.concatenate([text_last, extra], axis=0)[None]
     in_half = adapter.shape[0] // 2
-    piece = swap_x(half_of(adapter, own_c, in_half))
+    in_part = in_half // 2
+    sent = half_of(adapter, own_c, in_half)
+    image_pooled = after(image_pooled, packed, sent)
+    z_high, z_low = bit_of(dp, Z_HIGH), bit_of(dp, Z_LOW)
+    from_low = swap(packed, "dp", Z_LOW)
+    from_high = swap(packed, "dp", Z_HIGH)
+    piece_0 = swap_x(sent[:in_part])
 
     image_norm = layer_norm(image_pooled, image_gain).astype(jnp.bfloat16)
     hidden = jax.nn.gelu(
         jnp.dot(image_norm, mlp_up, preferred_element_type=jnp.float32), approximate=True
     ).astype(jnp.bfloat16)
     branch = jnp.dot(hidden, mlp_down, preferred_element_type=jnp.float32)
+    branch, from_low, from_high, piece_0 = lax.optimization_barrier((branch, from_low, from_high, piece_0))
+    from_both = swap(from_high, "dp", Z_LOW)
     arrived = swap_x(half_of(branch, ~own_x, half_rows))
     feature = half_of(image_pooled, own_x, half_rows).astype(jnp.float32) + (
         half_of(branch, own_x, half_rows) + arrived
@@ -399,28 +411,34 @@
         feature * lax.rsqrt(jnp.sum(feature * feature, axis=-1, keepdims=True) + EPS)
     ).astype(jnp.bfloat16)
 
-    text_a = after(text_a, branch)
-    text_b = after(text_b, branch)
-    text_a = grow(text_a, Z_LOW)
-    text_b = grow(text_b, Z_HIGH)
+    image_unit, from_both = lax.optimization_barrier((image_unit, from_both))
+    texts = join(join(packed, from_low, z_low), join(from_high, from_both, z_low), z_high)
+    given = half_of(texts, own_x, 2)
+
+    image_a = image_unit[:quarter]
+    image_b = image_unit[quarter:]
+    near_0 = swap(given[:1], "dp", Y)
+    piece_1 = swap_x(sent[in_part:])
+    image_a = grow(image_a, Z_HIGH)
+    image_b = join(image_b, swap_x(image_b), own_x)
+    image_a, image_b, near_0, piece_1 = lax.optimization_barrier((image_a, image_b, near_0, piece_1))
+    piece = jnp.concatenate([piece_0, piece_1])
     other_adapter = join(piece, swap_core(piece), own_c)
     full_adapter = join(adapter, other_adapter, own_x)
-
-    image_a = image_unit[:quarter]
-    image_b = image_unit[quarter:]
-    image_a = grow(image_a, Z_HIGH)
-    image_b = join(image_b, swap_x(image_b), own_x)
-    text_a = after(text_a, image_unit)
-    text_b = after(text_b, image_unit)
-    pieces = [text_a, swap(text_a, "dp", Y), text_b, swap(text_b, "dp", Z_LOW)]
+    near_1 = swap(given[1:], "dp", Y)
+    far_0 = swap_x(near_0)
     image_a = grow(image_a, Z_LOW)
     image_b = grow(image_b, Z_HIGH)
+    image_a, image_b, near_1, far_0 = lax.optimization_barrier((image_a, image_b, near_1, far_0))
+    far_1 = swap_x(near_1)
     image_a = grow(image_a, Y)
     image_b = grow(image_b, Z_LOW)
+    image_a, image_b, far_1, full_adapter = lax.optimization_barrier((image_a, image_b, far_1, full_adapter))
     far_a = swap_x(image_a)
     far_b = swap(image_b, "dp", Y)
 
-    flags = jnp.stack([mp, (dp & Y) // Y, (dp & Z_LOW) // Z_LOW]).astype(jnp.int32)
+    flags = jnp.stack([mp, (dp & Y) // Y]).astype(jnp.int32)
+    pieces = [texts, near_0, near_1, far_0, far_1]
     embed, unit, inverse, caption, turned = text_side(flags, pieces, text_gain, full_adapter)
 
     def places(bits):
@@ -446,13 +464,12 @@
     images = [image_a, swap_core(image_a), image_b, swap_core(image_b)]
     early, early_loss = early_scores(knobs, near.astype(jnp.int32), embed, caption, images, where)
     images = [far_a, swap_core(far_a), far_b, swap_core(far_b)]
-    part = late_scores(
+    part, loss = late_scores(
         knobs, far.astype(jnp.int32), embed, caption, early, early_loss, unit, inverse, turned, images, where
     )
-    total = part + swap_core(part)
-    in_width = adapter.shape[0]
-    mean_loss = total[in_width, :1] / (pair_count * pair_count)
-    return total[:in_width].astype(jnp.bfloat16), mean_loss
+    grad_adapter = (part + swap_core(part)).astype(jnp.bfloat16)
+    mean_loss = (loss + swap_core(loss))[0, :1] / (pair_count * pair_count)
+    return grad_adapter, mean_loss
 
 
 def solution(mesh):

time: 132 us -> 116 us (0.88)
  waiting for transfers between devices: 50.3 us -> 38.8 us
  Pallas kernels: 33.1 us -> 30.6 us
  other arithmetic: 9.13 us -> 7.32 us
    ppermute x22 -> x25, waiting for transfers between devices: 50.3 us -> 38.8 us  [swap(): return lax.ppermute(values, axis, [(i, i ^ bit) for i in range(count)])]
    add x1, other arithmetic: 2.02 us -> 0.01 us  [slice_plan(): mean_loss = (loss + swap_core(loss))[0, :1] / (pair_count * pair_count)]
    slice x3, local copies, waits for them, and re-layouts: 2.46 us -> 0.62 us  [the longest x1 0.51 us: slice_plan(): mean_loss = (loss + swap_core(loss))[0, :1] / (pair_count * pair_count)]
    pallas_call x1, Pallas kernels: 16 us -> 14.3 us  [late_scores(): pl.pallas_call(functools.partial(late_kernel, len(images)), grid=(count /...]
    convert_element_type x0 -> x1, other arithmetic: none -> 1.43 us  [slice_plan(): grad_adapter = (part + swap_core(part)).astype(jnp.bfloat16)]
    unnamed x16 -> x17, local copies, waits for them, and re-layouts: 2.21 us -> 3.36 us
    ppermute x22 -> x25, starting transfers between devices: 23 us -> 23.3 us  [swap(): return lax.ppermute(values, axis, [(i, i ^ bit) for i in range(count)])]
  transfers between devices with their start and end apart: 22 -> 25, of which waited for: 9 -> 12; matrix products, arithmetic and copies ran while one was open for 10% -> 11% of each run, Pallas kernels for 13% -> 14%
where the time goes in v2:
time: 116 us
  waiting for transfers between devices  38.8 us (33%)
  Pallas kernels  30.6 us (26%)
  starting transfers between devices  23.3 us (20%)
  matrix products  7.59 us (7%)
  other arithmetic  7.32 us (6%)
  between operations  4.11 us (4%)
  local copies, waits for them, and re-layouts  4.03 us (3%)
    ppermute x25, waiting for transfers between devices, swap(): return lax.ppermute(values, axis, [(i, i ^ bit) for i in range(count)])  38.8 us
    ppermute x25, starting transfers between devices, swap(): return lax.ppermute(values, axis, [(i, i ^ bit) for i in range(count)])  23.3 us
    pallas_call x1, Pallas kernels, late_scores(): pl.pallas_call(functools.partial(late_kernel, len(images)), grid=(count /...  14.3 us
    pallas_call x1, Pallas kernels, early_scores(): pl.pallas_call(functools.partial(early_kernel, len(images)), grid=(count...  9.1 us
    dot_general x1, matrix products, slice_plan(): branch = jnp.dot(hidden, mlp_down, preferred_element_type=jnp.float32)  7.59 us
    pallas_call x1, Pallas kernels, text_side(): pl.pallas_call(text_kernel, grid=(4,), in_specs=[SMEM] + [whole_spec(piec...  7.13 us
    unnamed x17, local copies, waits for them, and re-layouts  3.36 us
  transfers between devices with their start and end apart: 25, of which 12 were waited for; matrix products, arithmetic and copies ran while one was open for 11% of the time, Pallas kernels for 14%

profile of v2, /device:TPU:0, one launch (start us, length us, event | category | flops | bytes accessed | tf_op | source)
XLA Modules:
  0.0 115.7 jit_solution(333767678498154139)
XLA Ops:
  0.6 0.7 convert_bitcast_fusion
  1.3 1.0 maximum_bitcast_fusion
  2.3 3.1 %collective-permute-start = (bf16[1,136,1152]{2,1,0:T(8,128)(2,1)S(1)}, bf16[1,136,1152]{2,1,0:T(8,128)(2,1)S(1)}, u32[]{:S(2)}, u32[]{:S(2)}) collective-permute-start(bf16[1,136,1152]{2,1,0:T(8,128)(2,1)S(1)} %maximum_bitcast_fusion), channel_id=1, source_target_pairs={{0,8},{2,10},{4,12},{6,14},{8,0},{10,2},{12,4},{14,6},{16,24},{18,... | collective-permute-start | bytes 940040 | tf_op jit(solution)/shard_map/ppermute | solution.py:108
  5.4 2.6 %collective-permute-start.1 = (bf16[1,136,1152]{2,1,0:T(8,128)(2,1)S(1)}, bf16[1,136,1152]{2,1,0:T(8,128)(2,1)S(1)}, u32[]{:S(2)}, u32[]{:S(2)}) collective-permute-start(bf16[1,136,1152]{2,1,0:T(8,128)(2,1)S(1)} %maximum_bitcast_fusion), channel_id=1, source_target_pairs={{0,16},{2,18},{4,20},{6,22},{8,24},{10,26},{12,28},{14,30},{16,0},... | collective-permute-start | bytes 940040 | tf_op jit(solution)/shard_map/ppermute | solution.py:108
  8.0 1.4 %slice_select_fusion = bf16[288,1152]{1,0:T(8,128)(2,1)S(1)} fusion(bf16[576,1152]{1,0:T(8,128)(2,1)} %param.19, pred[]{:T(512)S(6)} %ne.55), kind=kLoop, calls=%fused_computation.19 | loop fusion | flops 331776 | bytes 1990657 | tf_op jit(solution)/shard_map/jit(_where)/select_n | solution.py:132
  9.5 1.6 %collective-permute-start.2 = (bf16[144,1152]{1,0:T(8,128)(2,1)S(1)}, bf16[144,1152]{1,0:T(8,128)(2,1)S(1)}, u32[]{:S(2)}, u32[]{:S(2)}) collective-permute-start(bf16[144,1152]{1,0:T(8,128)(2,1)S(1)} %get-tuple-element.68), channel_id=1, source_target_pairs={{0,1},{1,0},{2,3},{3,2},{4,5},{5,4},{6,7},{7,6},{8,9},{9,8},{10,11... | collective-permute-start | bytes 995336 | tf_op jit(solution)/shard_map/ppermute | solution.py:108
  12.0 7.6 %fusion.13 = f32[128,1152]{1,0:T(8,128)S(1)} fusion(bf16[2152,1152]{1,0:T(8,128)(2,1)} %param.18, bf16[1152,2152]{0,1:T(8,128)(2,1)} %param.17, bf16[128,1152]{1,0:T(8,128)(2,1)S(1)} %copy-done.4, f32[1152]{0:T(1024)S(1)} %copy-done.7, f32[128]{0:T(128)S(1)} %add_rsqrt_fusion.1, f32[128]{0:T(128)S(1)} %broadcast_multiply_fusion), kind=kOutput, calls=%fused_computation.32 | convolution fusion | flops 1272517632 | bytes 10806784 | tf_op jit(solution)/shard_map/dot_general | solution.py:403
  21.0 0.9 collective-permute-done.1
  22.0 1.6 %collective-permute-start.3 = (f32[64,1152]{1,0:T(8,128)S(1)}, f32[64,1152]{1,0:T(8,128)S(1)}, u32[]{:S(2)}, u32[]{:S(2)}) collective-permute-start(f32[64,1152]{1,0:T(8,128)S(1)} %slice_select_fusion.1), channel_id=1, source_target_pairs={{0,1},{1,0},{2,3},{3,2},{4,5},{5,4},{6,7},{7,6},{8,9},{9,8},{10,11... | collective-permute-start | bytes 884744 | tf_op jit(solution)/shard_map/ppermute | solution.py:108
  24.1 7.9 %collective-permute-done.3 = f32[64,1152]{1,0:T(8,128)S(1)} collective-permute-done((f32[64,1152]{1,0:T(8,128)S(1)}, f32[64,1152]{1,0:T(8,128)S(1)}, u32[]{:S(2)}, u32[]{:S(2)}) %collective-permute-start.3) | collective-permute-done | bytes 294944 | tf_op jit(solution)/shard_map/ppermute | solution.py:108
  32.7 1.5 %collective-permute-start.6 = (bf16[32,1152]{1,0:T(8,128)(2,1)S(1)}, bf16[32,1152]{1,0:T(8,128)(2,1)S(1)}, u32[]{:S(2)}, u32[]{:S(2)}) collective-permute-start(bf16[32,1152]{1,0:T(8,128)(2,1)S(1)} %get-tuple-element.89), channel_id=1, source_target_pairs={{0,1},{1,0},{2,3},{3,2},{4,5},{5,4},{6,7},{7,6},{8,9},{9,8},{10,11... | collective-permute-start | bytes 221192 | tf_op jit(solution)/shard_map/ppermute | solution.py:108
  34.6 1.6 %collective-permute-start.7 = (bf16[1,136,1152]{2,1,0:T(8,128)(2,1)S(1)}, bf16[1,136,1152]{2,1,0:T(8,128)(2,1)S(1)}, u32[]{:S(2)}, u32[]{:S(2)}) collective-permute-start(bf16[1,136,1152]{2,1,0:T(8,128)(2,1)S(1)} %get-tuple-element.70), channel_id=1, source_target_pairs={{0,4},{2,6},{4,0},{6,2},{8,12},{10,14},{12,8},{14,10},{16,20},{18,... | collective-permute-start | bytes 940040 | tf_op jit(solution)/shard_map/ppermute | solution.py:108
  36.2 2.1 %collective-permute-done.5 = bf16[32,1152]{1,0:T(8,128)(2,1)S(1)} collective-permute-done((bf16[32,1152]{1,0:T(8,128)(2,1)S(1)}, bf16[32,1152]{1,0:T(8,128)(2,1)S(1)}, u32[]{:S(2)}, u32[]{:S(2)}) %collective-permute-start.5) | collective-permute-done | bytes 73760 | tf_op jit(solution)/shard_map/ppermute | solution.py:108
  38.4 3.4 %collective-permute-done.7.near_0 = bf16[1,136,1152]{2,1,0:T(8,128)(2,1)S(1)} collective-permute-done((bf16[1,136,1152]{2,1,0:T(8,128)(2,1)S(1)}, bf16[1,136,1152]{2,1,0:T(8,128)(2,1)S(1)}, u32[]{:S(2)}, u32[]{:S(2)}) %collective-permute-start.7) | collective-permute-done | bytes 313376 | tf_op jit(solution)/shard_map/ppermute | solution.py:108
  41.8 2.8 %collective-permute-start.10 = (bf16[64,1152]{1,0:T(8,128)(2,1)S(1)}, bf16[64,1152]{1,0:T(8,128)(2,1)S(1)}, u32[]{:S(2)}, u32[]{:S(2)}) collective-permute-start(bf16[64,1152]{1,0:T(8,128)(2,1)S(1)} %get-tuple-element.38), channel_id=1, source_target_pairs={{0,16},{2,18},{4,20},{6,22},{8,24},{10,26},{12,28},{14,30},{16,0},... | collective-permute-start | bytes 442376 | tf_op jit(solution)/shard_map/ppermute | solution.py:108
  44.7 1.5 %collective-permute-start.11 = (bf16[1,136,1152]{2,1,0:T(8,128)(2,1)S(1)}, bf16[1,136,1152]{2,1,0:T(8,128)(2,1)S(1)}, u32[]{:S(2)}, u32[]{:S(2)}) collective-permute-start(bf16[1,136,1152]{2,1,0:T(8,128)(2,1)S(1)} %get-tuple-element.69), channel_id=1, source_target_pairs={{0,4},{2,6},{4,0},{6,2},{8,12},{10,14},{12,8},{14,10},{16,20},{18,... | collective-permute-start | bytes 940040 | tf_op jit(solution)/shard_map/ppermute | solution.py:108
  46.7 0.6 collective-permute-start.12
  47.3 2.0 %collective-permute-done.10 = bf16[64,1152]{1,0:T(8,128)(2,1)S(1)} collective-permute-done((bf16[64,1152]{1,0:T(8,128)(2,1)S(1)}, bf16[64,1152]{1,0:T(8,128)(2,1)S(1)}, u32[]{:S(2)}, u32[]{:S(2)}) %collective-permute-start.10) | collective-permute-done | bytes 147488 | tf_op jit(solution)/shard_map/ppermute | solution.py:108
  49.4 2.1 %collective-permute-done.9 = bf16[64,1152]{1,0:T(8,128)(2,1)S(1)} collective-permute-done((bf16[64,1152]{1,0:T(8,128)(2,1)S(1)}, bf16[64,1152]{1,0:T(8,128)(2,1)S(1)}, u32[]{:S(2)}, u32[]{:S(2)}) %collective-permute-start.9) | collective-permute-done | bytes 147488 | tf_op jit(solution)/shard_map/ppermute | solution.py:108
  51.6 2.0 %collective-permute-done.12.far_0 = bf16[1,136,1152]{2,1,0:T(8,128)(2,1)S(1)} collective-permute-done((bf16[1,136,1152]{2,1,0:T(8,128)(2,1)S(1)}, bf16[1,136,1152]{2,1,0:T(8,128)(2,1)S(1)}, u32[]{:S(2)}, u32[]{:S(2)}) %collective-permute-start.12) | collective-permute-done | bytes 313376 | tf_op jit(solution)/shard_map/ppermute | solution.py:108
  53.6 1.6 %collective-permute-start.14 = (bf16[128,1152]{1,0:T(8,128)(2,1)S(1)}, bf16[128,1152]{1,0:T(8,128)(2,1)S(1)}, u32[]{:S(2)}, u32[]{:S(2)}) collective-permute-start(bf16[128,1152]{1,0:T(8,128)(2,1)S(1)} %pad_maximum_fusion.8), channel_id=1, source_target_pairs={{0,8},{2,10},{4,12},{6,14},{8,0},{10,2},{12,4},{14,6},{16,24},{18,... | collective-permute-start | bytes 884744 | tf_op jit(solution)/shard_map/ppermute | solution.py:108
  56.4 3.9 %collective-permute-done.14 = bf16[128,1152]{1,0:T(8,128)(2,1)S(1)} collective-permute-done((bf16[128,1152]{1,0:T(8,128)(2,1)S(1)}, bf16[128,1152]{1,0:T(8,128)(2,1)S(1)}, u32[]{:S(2)}, u32[]{:S(2)}) %collective-permute-start.14) | collective-permute-done | bytes 294944 | tf_op jit(solution)/shard_map/ppermute | solution.py:108
  60.4 4.3 %collective-permute-done.13 = bf16[128,1152]{1,0:T(8,128)(2,1)S(1)} collective-permute-done((bf16[128,1152]{1,0:T(8,128)(2,1)S(1)}, bf16[128,1152]{1,0:T(8,128)(2,1)S(1)}, u32[]{:S(2)}, u32[]{:S(2)}) %collective-permute-start.13) | collective-permute-done | bytes 294944 | tf_op jit(solution)/shard_map/ppermute | solution.py:108
  65.0 1.2 %copy-done.3 = bf16[576,1152]{1,0:T(8,128)(2,1)S(1)} copy-done((bf16[576,1152]{1,0:T(8,128)(2,1)S(1)}, bf16[576,1152]{1,0:T(8,128)(2,1)}, u32[]{:S(2)}) %copy-start.3) | copy-done | bytes 1327128
  67.0 0.6 collective-permute-start.19
  68.4 7.1 %shard_map.131 = (bf16[1024,1152]{1,0:T(8,128)(2,1)S(1)}, f32[1024,1152]{1,0:T(8,128)S(1)}, f32[1024,1]{1,0:T(8,128)S(1)}, s32[1024,1]{1,0:T(8,128)S(1)}, bf16[576,1024]{1,0:T(8,128)(2,1)S(1)}) custom-call(s32[2]{0:T(128)S(1)} %pad_add_fusion.1.flags_ref, bf16[4,136,1152]{2,1,0:T(8,128)(2,1)S(1)} %pad_maximum_fusion.2.own_ref, ...), custom_call_target="tpu_custom_call" | custom-call | flops 5435817984 | bytes 11796480 | tf_op jit(solution)/shard_map/pallas_call | solution.py:209
  75.6 2.1 %copy-done.2 = f32[1024,1152]{1,0:T(8,128)} copy-done((f32[1024,1152]{1,0:T(8,128)}, f32[1024,1152]{1,0:T(8,128)S(1)}, u32[]{:S(2)}) %copy-start.2) | copy-done | bytes 4718616
  77.7 5.0 %collective-permute-done.19.refs_0_ = bf16[256,1152]{1,0:T(8,128)(2,1)S(1)} collective-permute-done((bf16[256,1152]{1,0:T(8,128)(2,1)S(1)}, bf16[256,1152]{1,0:T(8,128)(2,1)S(1)}, u32[]{:S(2)}, u32[]{:S(2)}) %collective-permute-start.19) | collective-permute-done | bytes 589856 | tf_op jit(solution)/shard_map/ppermute | solution.py:108
  83.4 9.1 %shard_map.132 = (f32[1024,1152]{1,0:T(8,128)S(1)}, f32[8,128]{1,0:T(8,128)S(1)}) custom-call(f32[3]{0:T(128)S(1)} %pad_maximum_fusion.11.knobs_ref, s32[4]{0:T(128)S(1)} %pad_add_fusion.2.offsets_ref, bf16[1024,1152]{1,0:T(8,128)(2,1)S(1)} %get-tuple-element.47.embed_ref, s32[1024,1]{1,0:T(8,128)S(1)} %get-tuple-element.48.caption_ref, ...), custom_call_target="tpu_custom_call" | custom-call | flops 9663676416 | bytes 9437184 | tf_op jit(solution)/shard_map/pallas_call | solution.py:318
  92.5 14.3 %shard_map.133 = (f32[576,1152]{1,0:T(8,128)S(1)}, f32[8,128]{1,0:T(8,128)S(1)}) custom-call(f32[3]{0:T(128)S(1)} %pad_maximum_fusion.11.knobs_ref, s32[4]{0:T(128)S(1)} %pad_add_fusion.offsets_ref, bf16[1024,1152]{1,0:T(8,128)(2,1)S(1)} %get-tuple-element.47.embed_ref, s32[1024,1]{1,0:T(8,128)S(1)} %get-tuple-element.48.caption_ref, ...), custom_call_target="tpu_custom_call" | custom-call | flops 15099494400 | bytes 18874368 | tf_op jit(solution)/shard_map/pallas_call | solution.py:338
  107.5 4.5 %collective-permute-done.24 = f32[8,128]{1,0:T(8,128)S(1)} collective-permute-done((f32[8,128]{1,0:T(8,128)S(1)}, f32[8,128]{1,0:T(8,128)S(1)}, u32[]{:S(2)}, u32[]{:S(2)}) %collective-permute-start.24) | collective-permute-done | bytes 4128 | tf_op jit(solution)/shard_map/ppermute | solution.py:108
  113.2 1.4 %add_convert_fusion = bf16[576,1152]{1,0:T(8,128)(2,1)} fusion(f32[576,1152]{1,0:T(8,128)S(1)} %get-tuple-element.56, f32[576,1152]{1,0:T(8,128)S(1)} %collective-permute-done.23), kind=kLoop, calls=%fused_computation.1 | loop fusion | flops 1327104 | bytes 6635520 | tf_op jit(solution)/shard_map/convert_element_type | solution.py:470
  (80 shorter events, 8.6 us)
Async XLA Ops:
  2.3 18.7 %collective-permute-start = (bf16[1,136,1152]{2,1,0:T(8,128)(2,1)S(1)}, bf16[1,136,1152]{2,1,0:T(8,128)(2,1)S(1)}, u32[]{:S(2)}, u32[]{:S(2)}) collective-permute-start(bf16[1,136,1152]{2,1,0:T(8,128)(2,1)S(1)} %maximum_bitcast_fusion), channel_id=1, source_target_pairs={{0,8},{2,10},{4,12},{6,14},{8,0},{10,2},{12,4},{14,6},{16,24},{18,... | collective-permute-start | bytes 940040 | tf_op jit(solution)/shard_map/ppermute | solution.py:108
  5.4 16.5 %collective-permute-start.1 = (bf16[1,136,1152]{2,1,0:T(8,128)(2,1)S(1)}, bf16[1,136,1152]{2,1,0:T(8,128)(2,1)S(1)}, u32[]{:S(2)}, u32[]{:S(2)}) collective-permute-start(bf16[1,136,1152]{2,1,0:T(8,128)(2,1)S(1)} %maximum_bitcast_fusion), channel_id=1, source_target_pairs={{0,16},{2,18},{4,20},{6,22},{8,24},{10,26},{12,28},{14,30},{16,0},... | collective-permute-start | bytes 940040 | tf_op jit(solution)/shard_map/ppermute | solution.py:108
  8.0 3.6 %copy-start.4 = (bf16[128,1152]{1,0:T(8,128)(2,1)S(1)}, bf16[128,1152]{1,0:T(8,128)(2,1)}, u32[]{:S(2)}) copy-start(bf16[128,1152]{1,0:T(8,128)(2,1)} %param.12) | copy-start | bytes 884740
  9.4 2.5 %copy-start.7 = (f32[1152]{0:T(1024)S(1)}, f32[1152]{0:T(1024)}, u32[]{:S(2)}) copy-start(f32[1152]{0:T(1024)} %param.15) | copy-start | bytes 13828
  9.5 12.4 %collective-permute-start.2 = (bf16[144,1152]{1,0:T(8,128)(2,1)S(1)}, bf16[144,1152]{1,0:T(8,128)(2,1)S(1)}, u32[]{:S(2)}, u32[]{:S(2)}) collective-permute-start(bf16[144,1152]{1,0:T(8,128)(2,1)S(1)} %get-tuple-element.68), channel_id=1, source_target_pairs={{0,1},{1,0},{2,3},{3,2},{4,5},{5,4},{6,7},{7,6},{8,9},{9,8},{10,11... | collective-permute-start | bytes 995336 | tf_op jit(solution)/shard_map/ppermute | solution.py:108
  11.0 27.3 %collective-permute-start.8 = (bf16[144,1152]{1,0:T(8,128)(2,1)S(1)}, bf16[144,1152]{1,0:T(8,128)(2,1)S(1)}, u32[]{:S(2)}, u32[]{:S(2)}) collective-permute-start(bf16[144,1152]{1,0:T(8,128)(2,1)S(1)} %get-tuple-element.67), channel_id=1, source_target_pairs={{0,1},{1,0},{2,3},{3,2},{4,5},{5,4},{6,7},{7,6},{8,9},{9,8},{10,11... | collective-permute-start | bytes 995336 | tf_op jit(solution)/shard_map/ppermute | solution.py:108
  11.9 12.0 %copy-start.5 = (bf16[128,1152]{1,0:T(8,128)(2,1)S(1)}, bf16[128,1152]{1,0:T(8,128)(2,1)}, u32[]{:S(2)}) copy-start(bf16[128,1152]{1,0:T(8,128)(2,1)} %param.13) | copy-start | bytes 884740
  22.0 10.0 %collective-permute-start.3 = (f32[64,1152]{1,0:T(8,128)S(1)}, f32[64,1152]{1,0:T(8,128)S(1)}, u32[]{:S(2)}, u32[]{:S(2)}) collective-permute-start(f32[64,1152]{1,0:T(8,128)S(1)} %slice_select_fusion.1), channel_id=1, source_target_pairs={{0,1},{1,0},{2,3},{3,2},{4,5},{5,4},{6,7},{7,6},{8,9},{9,8},{10,11... | collective-permute-start | bytes 884744 | tf_op jit(solution)/shard_map/ppermute | solution.py:108
  23.5 8.8 %collective-permute-start.4 = (bf16[1,136,1152]{2,1,0:T(8,128)(2,1)S(1)}, bf16[1,136,1152]{2,1,0:T(8,128)(2,1)S(1)}, u32[]{:S(2)}, u32[]{:S(2)}) collective-permute-start(bf16[1,136,1152]{2,1,0:T(8,128)(2,1)S(1)} %collective-permute-done.1), channel_id=1, source_target_pairs={{0,8},{2,10},{4,12},{6,14},{8,0},{10,2},{12,4},{14,6},{16,24},{18,... | collective-permute-start | bytes 940040 | tf_op jit(solution)/shard_map/ppermute | solution.py:108
  32.3 6.0 %collective-permute-start.5 = (bf16[32,1152]{1,0:T(8,128)(2,1)S(1)}, bf16[32,1152]{1,0:T(8,128)(2,1)S(1)}, u32[]{:S(2)}, u32[]{:S(2)}) collective-permute-start(bf16[32,1152]{1,0:T(8,128)(2,1)S(1)} %get-tuple-element.90), channel_id=1, source_target_pairs={{0,16},{2,18},{4,20},{6,22},{8,24},{10,26},{12,28},{14,30},{16,0},... | collective-permute-start | bytes 221192 | tf_op jit(solution)/shard_map/ppermute | solution.py:108
  32.7 5.6 %collective-permute-start.6 = (bf16[32,1152]{1,0:T(8,128)(2,1)S(1)}, bf16[32,1152]{1,0:T(8,128)(2,1)S(1)}, u32[]{:S(2)}, u32[]{:S(2)}) collective-permute-start(bf16[32,1152]{1,0:T(8,128)(2,1)S(1)} %get-tuple-element.89), channel_id=1, source_target_pairs={{0,1},{1,0},{2,3},{3,2},{4,5},{5,4},{6,7},{7,6},{8,9},{9,8},{10,11... | collective-permute-start | bytes 221192 | tf_op jit(solution)/shard_map/ppermute | solution.py:108
  34.5 10.1 %copy-start.6 = (f32[1152]{0:T(1024)S(1)}, f32[1152]{0:T(1024)}, u32[]{:S(2)}) copy-start(f32[1152]{0:T(1024)} %param.16) | copy-start | bytes 13828
  34.6 7.2 %collective-permute-start.7 = (bf16[1,136,1152]{2,1,0:T(8,128)(2,1)S(1)}, bf16[1,136,1152]{2,1,0:T(8,128)(2,1)S(1)}, u32[]{:S(2)}, u32[]{:S(2)}) collective-permute-start(bf16[1,136,1152]{2,1,0:T(8,128)(2,1)S(1)} %get-tuple-element.70), channel_id=1, source_target_pairs={{0,4},{2,6},{4,0},{6,2},{8,12},{10,14},{12,8},{14,10},{16,20},{18,... | collective-permute-start | bytes 940040 | tf_op jit(solution)/shard_map/ppermute | solution.py:108
  41.8 7.6 %collective-permute-start.10 = (bf16[64,1152]{1,0:T(8,128)(2,1)S(1)}, bf16[64,1152]{1,0:T(8,128)(2,1)S(1)}, u32[]{:S(2)}, u32[]{:S(2)}) collective-permute-start(bf16[64,1152]{1,0:T(8,128)(2,1)S(1)} %get-tuple-element.38), channel_id=1, source_target_pairs={{0,16},{2,18},{4,20},{6,22},{8,24},{10,26},{12,28},{14,30},{16,0},... | collective-permute-start | bytes 442376 | tf_op jit(solution)/shard_map/ppermute | solution.py:108
  44.7 6.9 %collective-permute-start.11 = (bf16[1,136,1152]{2,1,0:T(8,128)(2,1)S(1)}, bf16[1,136,1152]{2,1,0:T(8,128)(2,1)S(1)}, u32[]{:S(2)}, u32[]{:S(2)}) collective-permute-start(bf16[1,136,1152]{2,1,0:T(8,128)(2,1)S(1)} %get-tuple-element.69), channel_id=1, source_target_pairs={{0,4},{2,6},{4,0},{6,2},{8,12},{10,14},{12,8},{14,10},{16,20},{18,... | collective-permute-start | bytes 940040 | tf_op jit(solution)/shard_map/ppermute | solution.py:108
  46.2 5.3 %collective-permute-start.9 = (bf16[64,1152]{1,0:T(8,128)(2,1)S(1)}, bf16[64,1152]{1,0:T(8,128)(2,1)S(1)}, u32[]{:S(2)}, u32[]{:S(2)}) collective-permute-start(bf16[64,1152]{1,0:T(8,128)(2,1)S(1)} %get-tuple-element.37), channel_id=1, source_target_pairs={{0,8},{2,10},{4,12},{6,14},{8,0},{10,2},{12,4},{14,6},{16,24},{18,... | collective-permute-start | bytes 442376 | tf_op jit(solution)/shard_map/ppermute | solution.py:108
  46.7 6.9 %collective-permute-start.12 = (bf16[1,136,1152]{2,1,0:T(8,128)(2,1)S(1)}, bf16[1,136,1152]{2,1,0:T(8,128)(2,1)S(1)}, u32[]{:S(2)}, u32[]{:S(2)}) collective-permute-start(bf16[1,136,1152]{2,1,0:T(8,128)(2,1)S(1)} %collective-permute-done.7.near_0), channel_id=1, source_target_pairs={{0,1},{1,0},{2,3},{3,2},{4,5},{5,4},{6,7},{7,6},{8,9},{9,8},{10,11... | collective-permute-start | bytes 940040 | tf_op jit(solution)/shard_map/ppermute | solution.py:108
  53.6 6.7 %collective-permute-start.14 = (bf16[128,1152]{1,0:T(8,128)(2,1)S(1)}, bf16[128,1152]{1,0:T(8,128)(2,1)S(1)}, u32[]{:S(2)}, u32[]{:S(2)}) collective-permute-start(bf16[128,1152]{1,0:T(8,128)(2,1)S(1)} %pad_maximum_fusion.8), channel_id=1, source_target_pairs={{0,8},{2,10},{4,12},{6,14},{8,0},{10,2},{12,4},{14,6},{16,24},{18,... | collective-permute-start | bytes 884744 | tf_op jit(solution)/shard_map/ppermute | solution.py:108
  55.2 9.6 %collective-permute-start.16 = (bf16[288,1152]{1,0:T(8,128)(2,1)S(1)}, bf16[288,1152]{1,0:T(8,128)(2,1)S(1)}, u32[]{:S(2)}, u32[]{:S(2)}) collective-permute-start(bf16[288,1152]{1,0:T(8,128)(2,1)S(1)} %constant_dynamic-update-slice_fusion), channel_id=1, source_target_pairs={{0,2},{2,0},{4,6},{6,4},{8,10},{10,8},{12,14},{14,12},{16,18},{18,... | collective-permute-start | bytes 1990664 | tf_op jit(solution)/shard_map/ppermute | solution.py:108
  55.3 9.4 %collective-permute-start.13 = (bf16[128,1152]{1,0:T(8,128)(2,1)S(1)}, bf16[128,1152]{1,0:T(8,128)(2,1)S(1)}, u32[]{:S(2)}, u32[]{:S(2)}) collective-permute-start(bf16[128,1152]{1,0:T(8,128)(2,1)S(1)} %pad_maximum_fusion.7), channel_id=1, source_target_pairs={{0,4},{2,6},{4,0},{6,2},{8,12},{10,14},{12,8},{14,10},{16,20},{18,... | collective-permute-start | bytes 884744 | tf_op jit(solution)/shard_map/ppermute | solution.py:108
  55.9 11.0 %collective-permute-start.15 = (bf16[1,136,1152]{2,1,0:T(8,128)(2,1)S(1)}, bf16[1,136,1152]{2,1,0:T(8,128)(2,1)S(1)}, u32[]{:S(2)}, u32[]{:S(2)}) collective-permute-start(bf16[1,136,1152]{2,1,0:T(8,128)(2,1)S(1)} %collective-permute-done.11.near_1), channel_id=1, source_target_pairs={{0,1},{1,0},{2,3},{3,2},{4,5},{5,4},{6,7},{7,6},{8,9},{9,8},{10,11... | collective-permute-start | bytes 940040 | tf_op jit(solution)/shard_map/ppermute | solution.py:108
  66.9 16.4 %collective-permute-start.17 = (bf16[256,1152]{1,0:T(8,128)(2,1)S(1)}, bf16[256,1152]{1,0:T(8,128)(2,1)S(1)}, u32[]{:S(2)}, u32[]{:S(2)}) collective-permute-start(bf16[256,1152]{1,0:T(8,128)(2,1)S(1)} %pad_maximum_fusion.5.refs_0_), channel_id=1, source_target_pairs={{0,2},{2,0},{4,6},{6,4},{8,10},{10,8},{12,14},{14,12},{16,18},{18,... | collective-permute-start | bytes 1769480 | tf_op jit(solution)/shard_map/ppermute | solution.py:108
  67.0 15.7 %collective-permute-start.19 = (bf16[256,1152]{1,0:T(8,128)(2,1)S(1)}, bf16[256,1152]{1,0:T(8,128)(2,1)S(1)}, u32[]{:S(2)}, u32[]{:S(2)}) collective-permute-start(bf16[256,1152]{1,0:T(8,128)(2,1)S(1)} %pad_maximum_fusion.5.refs_0_), channel_id=1, source_target_pairs={{0,1},{1,0},{2,3},{3,2},{4,5},{5,4},{6,7},{7,6},{8,9},{9,8},{10,11... | collective-permute-start | bytes 1769480 | tf_op jit(solution)/shard_map/ppermute | solution.py:108
  67.6 15.8 %collective-permute-start.18 = (bf16[256,1152]{1,0:T(8,128)(2,1)S(1)}, bf16[256,1152]{1,0:T(8,128)(2,1)S(1)}, u32[]{:S(2)}, u32[]{:S(2)}) collective-permute-start(bf16[256,1152]{1,0:T(8,128)(2,1)S(1)} %pad_maximum_fusion.6.refs_2_), channel_id=1, source_target_pairs={{0,2},{2,0},{4,6},{6,4},{8,10},{10,8},{12,14},{14,12},{16,18},{18,... | collective-permute-start | bytes 1769480 | tf_op jit(solution)/shard_map/ppermute | solution.py:108
  67.8 15.6 %collective-permute-start.21 = (bf16[256,1152]{1,0:T(8,128)(2,1)S(1)}, bf16[256,1152]{1,0:T(8,128)(2,1)S(1)}, u32[]{:S(2)}, u32[]{:S(2)}) collective-permute-start(bf16[256,1152]{1,0:T(8,128)(2,1)S(1)} %pad_maximum_fusion.6.refs_2_), channel_id=1, source_target_pairs={{0,4},{2,6},{4,0},{6,2},{8,12},{10,14},{12,8},{14,10},{16,20},{18,... | collective-permute-start | bytes 1769480 | tf_op jit(solution)/shard_map/ppermute | solution.py:108
  68.4 15.0 %copy-start = (s32[1,256]{1,0:T(1,128)S(1)}, s32[1,256]{1,0:T(1,128)}, u32[]{:S(2)}) copy-start(s32[1,256]{1,0:T(1,128)} %constant.89.clone.refs_4_.refs_5_) | copy-start | bytes 3076
  68.4 15.0 %copy-start.1 = (s32[1,256]{1,0:T(1,128)S(1)}, s32[1,256]{1,0:T(1,128)}, u32[]{:S(2)}) copy-start(s32[1,256]{1,0:T(1,128)} %constant.90.clone.refs_6_.refs_7_) | copy-start | bytes 3076
  75.6 2.1 %copy-start.2 = (f32[1024,1152]{1,0:T(8,128)}, f32[1024,1152]{1,0:T(8,128)S(1)}, u32[]{:S(2)}) copy-start(f32[1024,1152]{1,0:T(8,128)S(1)} %get-tuple-element.53.unit_ref) | copy-start | bytes 14155780
  82.7 9.7 %collective-permute-start.20 = (bf16[256,1152]{1,0:T(8,128)(2,1)S(1)}, bf16[256,1152]{1,0:T(8,128)(2,1)S(1)}, u32[]{:S(2)}, u32[]{:S(2)}) collective-permute-start(bf16[256,1152]{1,0:T(8,128)(2,1)S(1)} %collective-permute-done.19.refs_0_), channel_id=1, source_target_pairs={{0,2},{2,0},{4,6},{6,4},{8,10},{10,8},{12,14},{14,12},{16,18},{18,... | collective-permute-start | bytes 1769480 | tf_op jit(solution)/shard_map/ppermute | solution.py:108
  83.3 9.2 %collective-permute-start.22 = (bf16[256,1152]{1,0:T(8,128)(2,1)S(1)}, bf16[256,1152]{1,0:T(8,128)(2,1)S(1)}, u32[]{:S(2)}, u32[]{:S(2)}) collective-permute-start(bf16[256,1152]{1,0:T(8,128)(2,1)S(1)} %collective-permute-done.21.refs_2_), channel_id=1, source_target_pairs={{0,2},{2,0},{4,6},{6,4},{8,10},{10,8},{12,14},{14,12},{16,18},{18,... | collective-permute-start | bytes 1769480 | tf_op jit(solution)/shard_map/ppermute | solution.py:108
  106.9 6.3 %collective-permute-start.23 = (f32[576,1152]{1,0:T(8,128)S(1)}, f32[576,1152]{1,0:T(8,128)S(1)}, u32[]{:S(2)}, u32[]{:S(2)}) collective-permute-start(f32[576,1152]{1,0:T(8,128)S(1)} %get-tuple-element.56), channel_id=1, source_target_pairs={{0,2},{2,0},{4,6},{6,4},{8,10},{10,8},{12,14},{14,12},{16,18},{18,... | collective-permute-start | bytes 7962632 | tf_op jit(solution)/shard_map/ppermute | solution.py:108
  107.4 4.6 %collective-permute-start.24 = (f32[8,128]{1,0:T(8,128)S(1)}, f32[8,128]{1,0:T(8,128)S(1)}, u32[]{:S(2)}, u32[]{:S(2)}) collective-permute-start(f32[8,128]{1,0:T(8,128)S(1)} %get-tuple-element.57), channel_id=1, source_target_pairs={{0,2},{2,0},{4,6},{6,4},{8,10},{10,8},{12,14},{14,12},{16,18},{18,... | collective-permute-start | bytes 12296 | tf_op jit(solution)/shard_map/ppermute | solution.py:108
  (1 other events, 1.3 us)

commit v3 on v2

--- a/solution.py
+++ b/solution.py
@@ -146,29 +146,17 @@
     return pl.BlockSpec(shape, lambda i: (0,) * len(shape))
 
 
-def text_kernel(
-    flags_ref, own_ref, near_0, near_1, far_0, far_1, gain_ref, adapter_ref,
-    embed_ref, unit_ref, inverse_ref, caption_ref, turned_ref, held,
-):
+def text_kernel(flags_ref, *refs):
+    pieces, (gain_ref, adapter_ref) = refs[:8], refs[8:10]
+    embed_ref, unit_ref, inverse_ref, caption_ref, turned_ref, held = refs[10:]
     step = pl.program_id(0)
-    count = held.shape[0]
     rows = held.shape[1] - EXTRA
-    own, other = 2 * flags_ref[1], 2 - 2 * flags_ref[1]
-    for k in range(2):
-
-        @pl.when(step == own + k)
+    for k in range(4):
+
+        @pl.when(step == k)
         def _():
-            held[...] = own_ref[k * count : (k + 1) * count]
-
-    @pl.when(step == other + flags_ref[0])
-    def _():
-        held[0] = near_0[0]
-        held[1] = near_1[0]
-
-    @pl.when(step == other + 1 - flags_ref[0])
-    def _():
-        held[0] = far_0[0]
-        held[1] = far_1[0]
+            held[0] = pieces[2 * k][...]
+            held[1] = pieces[2 * k + 1][...]
 
     block = held[...]
     values = block[:, :rows].reshape(-1, block.shape[-1]).astype(jnp.float32)
@@ -201,7 +189,7 @@
 
 
 def text_side(flags, pieces, gain, adapter):
-    padded, width = pieces[1].shape[1:]
+    padded, width = pieces[0].shape
     parts = 2
     block = parts * (padded - EXTRA)
     count = 4 * block
@@ -220,11 +208,11 @@
             pl.BlockSpec((half, block), lambda i: (0, i)),
         ],
         out_shape=[
-            jax.ShapeDtypeStruct((count, width), jnp.bfloat16),
-            jax.ShapeDtypeStruct((count, width), jnp.float32),
-            jax.ShapeDtypeStruct((count, 1), jnp.float32),
-            jax.ShapeDtypeStruct((count, 1), jnp.int32),
-            jax.ShapeDtypeStruct((half, count), jnp.bfloat16),
+            pltpu.HBM((count, width), jnp.bfloat16),
+            pltpu.HBM((count, width), jnp.float32),
+            pltpu.HBM((count, 1), jnp.float32),
+            pltpu.HBM((count, 1), jnp.int32),
+            pltpu.HBM((half, count), jnp.bfloat16),
         ],
         scratch_shapes=[pltpu.VMEM((parts, padded, width), jnp.bfloat16)],
         compiler_params=pltpu.CompilerParams(vmem_limit_bytes=VMEM_LIMIT),
@@ -313,6 +301,10 @@
     return count, width, total, specs, tail, scratch
 
 
+def in_hbm(values):
+    return pltpu.with_memory_space_constraint(values, pltpu.HBM)
+
+
 def early_scores(knobs, offsets, embed, caption, images, places):
     count, width, total, specs, tail, scratch = score_specs(embed, images, places)
     return pl.pallas_call(
@@ -321,15 +313,15 @@
         in_specs=specs + tail,
         out_specs=[rows_spec(BLOCK, width), whole_spec((8, 128))],
         out_shape=[
-            jax.ShapeDtypeStruct((count, width), jnp.float32),
-            jax.ShapeDtypeStruct((8, 128), jnp.float32),
+            pltpu.HBM((count, width), jnp.float32),
+            pltpu.HBM((8, 128), jnp.float32),
         ],
         scratch_shapes=scratch,
         compiler_params=pltpu.CompilerParams(vmem_limit_bytes=VMEM_LIMIT),
         cost_estimate=pl.CostEstimate(
             flops=8 * count * width * total, bytes_accessed=8 * count * width, transcendentals=0
         ),
-    )(knobs, offsets, embed, caption, *images, *places)
+    )(knobs, offsets, in_hbm(embed), in_hbm(caption), *images, *places)
 
 
 def late_scores(knobs, offsets, embed, caption, early, early_loss, unit, inverse, turned, images, places):
@@ -357,7 +349,10 @@
         cost_estimate=pl.CostEstimate(
             flops=8 * count * width * (total + half), bytes_accessed=16 * count * width, transcendentals=0
         ),
-    )(knobs, offsets, embed, caption, early, early_loss, unit, inverse, turned, *images, *places)
+    )(
+        knobs, offsets, in_hbm(embed), in_hbm(caption), in_hbm(early), early_loss,
+        in_hbm(unit), in_hbm(inverse), in_hbm(turned), *images, *places,
+    )
 
 
 def slice_plan(
@@ -386,23 +381,22 @@
 
     parts = jnp.concatenate([caption_of // CAPTION_BASE, caption_of % CAPTION_BASE])
     extra = jnp.pad(parts.astype(jnp.bfloat16)[None, :], ((0, EXTRA - 1), (0, width - 2 * rows)))
-    packed = jnp.concatenate([text_last, extra], axis=0)[None]
+    packed = jnp.concatenate([text_last, extra], axis=0)
     in_half = adapter.shape[0] // 2
-    in_part = in_half // 2
-    sent = half_of(adapter, own_c, in_half)
+    sent = lax.dynamic_slice_in_dim(adapter, (dp & CORE) * in_half, in_half, 0)
     image_pooled = after(image_pooled, packed, sent)
-    z_high, z_low = bit_of(dp, Z_HIGH), bit_of(dp, Z_LOW)
+    from_high = swap(packed, "dp", Z_HIGH)
     from_low = swap(packed, "dp", Z_LOW)
-    from_high = swap(packed, "dp", Z_HIGH)
-    piece_0 = swap_x(sent[:in_part])
+    piece = swap_x(sent)
 
     image_norm = layer_norm(image_pooled, image_gain).astype(jnp.bfloat16)
     hidden = jax.nn.gelu(
         jnp.dot(image_norm, mlp_up, preferred_element_type=jnp.float32), approximate=True
     ).astype(jnp.bfloat16)
     branch = jnp.dot(hidden, mlp_down, preferred_element_type=jnp.float32)
-    branch, from_low, from_high, piece_0 = lax.optimization_barrier((branch, from_low, from_high, piece_0))
+    branch, from_low, from_high, piece = lax.optimization_barrier((branch, from_low, from_high, piece))
     from_both = swap(from_high, "dp", Z_LOW)
+    near_0 = swap(jnp.where(own_x, from_high, packed), "dp", Y)
     arrived = swap_x(half_of(branch, ~own_x, half_rows))
     feature = half_of(image_pooled, own_x, half_rows).astype(jnp.float32) + (
         half_of(branch, own_x, half_rows) + arrived
@@ -411,35 +405,29 @@
         feature * lax.rsqrt(jnp.sum(feature * feature, axis=-1, keepdims=True) + EPS)
     ).astype(jnp.bfloat16)
 
-    image_unit, from_both = lax.optimization_barrier((image_unit, from_both))
-    texts = join(join(packed, from_low, z_low), join(from_high, from_both, z_low), z_high)
-    given = half_of(texts, own_x, 2)
+    image_unit, from_both, near_0 = lax.optimization_barrier((image_unit, from_both, near_0))
+    near_1 = swap(jnp.where(own_x, from_both, from_low), "dp", Y)
+    far_0 = swap_x(near_0)
+    other_adapter = join(piece, swap_core(piece), own_c)
+    full_adapter = join(adapter, other_adapter, own_x)
 
     image_a = image_unit[:quarter]
     image_b = image_unit[quarter:]
-    near_0 = swap(given[:1], "dp", Y)
-    piece_1 = swap_x(sent[in_part:])
     image_a = grow(image_a, Z_HIGH)
     image_b = join(image_b, swap_x(image_b), own_x)
-    image_a, image_b, near_0, piece_1 = lax.optimization_barrier((image_a, image_b, near_0, piece_1))
-    piece = jnp.concatenate([piece_0, piece_1])
-    other_adapter = join(piece, swap_core(piece), own_c)
-    full_adapter = join(adapter, other_adapter, own_x)
-    near_1 = swap(given[1:], "dp", Y)
-    far_0 = swap_x(near_0)
+    image_a, image_b, near_1, far_0 = lax.optimization_barrier((image_a, image_b, near_1, far_0))
+    far_1 = swap_x(near_1)
     image_a = grow(image_a, Z_LOW)
     image_b = grow(image_b, Z_HIGH)
-    image_a, image_b, near_1, far_0 = lax.optimization_barrier((image_a, image_b, near_1, far_0))
-    far_1 = swap_x(near_1)
+    image_a, image_b, far_1, full_adapter = lax.optimization_barrier((image_a, image_b, far_1, full_adapter))
+    flags = mp.astype(jnp.int32).reshape(1)
+    pieces = [packed, from_low, from_high, from_both, near_0, near_1, far_0, far_1]
+    embed, unit, inverse, caption, turned = text_side(flags, pieces, text_gain, full_adapter)
     image_a = grow(image_a, Y)
     image_b = grow(image_b, Z_LOW)
-    image_a, image_b, far_1, full_adapter = lax.optimization_barrier((image_a, image_b, far_1, full_adapter))
+    image_a, image_b, caption = lax.optimization_barrier((image_a, image_b, caption))
     far_a = swap_x(image_a)
     far_b = swap(image_b, "dp", Y)
-
-    flags = jnp.stack([mp, (dp & Y) // Y]).astype(jnp.int32)
-    pieces = [texts, near_0, near_1, far_0, far_1]
-    embed, unit, inverse, caption, turned = text_side(flags, pieces, text_gain, full_adapter)
 
     def places(bits):
         place = np.arange(quarter)
@@ -463,6 +451,7 @@
 
     images = [image_a, swap_core(image_a), image_b, swap_core(image_b)]
     early, early_loss = early_scores(knobs, near.astype(jnp.int32), embed, caption, images, where)
+    far_a, far_b, early_loss = lax.optimization_barrier((far_a, far_b, early_loss))
     images = [far_a, swap_core(far_a), far_b, swap_core(far_b)]
     part, loss = late_scores(
         knobs, far.astype(jnp.int32), embed, caption, early, early_loss, unit, inverse, turned, images, where

time: 116 us -> 110 us (0.948)
  waiting for transfers between devices: 38.8 us -> 31.3 us
  starting transfers between devices: 23.3 us -> 26.4 us
  Pallas kernels: 30.6 us -> 32.9 us
  other arithmetic: 7.32 us -> 5.39 us
  local copies, waits for them, and re-layouts: 4.03 us -> 2.38 us
    ppermute x25 -> x24, waiting for transfers between devices: 38.8 us -> 31.3 us  [swap(): return lax.ppermute(values, axis, [(i, i ^ bit) for i in range(count)])]
    ppermute x25 -> x24, starting transfers between devices: 23.3 us -> 26.4 us  [swap(): return lax.ppermute(values, axis, [(i, i ^ bit) for i in range(count)])]
    unnamed x17 -> x16, local copies, waits for them, and re-layouts: 3.36 us -> 0.71 us
    select_n x3 -> x1, other arithmetic: 1.66 us -> 0.03 us  [half_of(): return jnp.where(upper, values[half:], values[:half])]
    pallas_call x1, Pallas kernels: 9.1 us -> 10.7 us  [early_scores(): pl.pallas_call(functools.partial(early_kernel, len(images)), grid=(count...]
  transfers between devices with their start and end apart: 25 -> 24, of which waited for: 12 -> 16; matrix products, arithmetic and copies ran while one was open for 11% -> 10% of each run, Pallas kernels for 14% -> 17%
where the time goes in v3:
time: 110 us
  Pallas kernels  32.9 us (30%)
  waiting for transfers between devices  31.3 us (28%)
  starting transfers between devices  26.4 us (24%)
  matrix products  7.59 us (7%)
  other arithmetic  5.39 us (5%)
  between operations  4.01 us (4%)
  local copies, waits for them, and re-layouts  2.38 us (2%)
    ppermute x24, waiting for transfers between devices, swap(): return lax.ppermute(values, axis, [(i, i ^ bit) for i in range(count)])  31.3 us
    ppermute x24, starting transfers between devices, swap(): return lax.ppermute(values, axis, [(i, i ^ bit) for i in range(count)])  26.4 us
    pallas_call x1, Pallas kernels, late_scores(): pl.pallas_call(functools.partial(late_kernel, len(images)), grid=(count /...  14.6 us
    pallas_call x1, Pallas kernels, early_scores(): pl.pallas_call(functools.partial(early_kernel, len(images)), grid=(count...  10.7 us
    pallas_call x1, Pallas kernels, text_side(): pl.pallas_call(text_kernel, grid=(4,), in_specs=[SMEM] + [whole_spec(piec...  7.61 us
    dot_general x1, matrix products, slice_plan(): branch = jnp.dot(hidden, mlp_down, preferred_element_type=jnp.float32)  7.59 us
  transfers between devices with their start and end apart: 24, of which 16 were waited for; matrix products, arithmetic and copies ran while one was open for 10% of the time, Pallas kernels for 17%

profile of v3, /device:TPU:0, one launch (start us, length us, event | category | flops | bytes accessed | tf_op | source)
XLA Modules:
  0.0 110.0 jit_solution(8716357086691061249)
XLA Ops:
  1.4 1.0 pad_maximum_fusion.4.refs_0_
  2.4 4.1 %collective-permute-start.1 = (bf16[136,1152]{1,0:T(8,128)(2,1)S(1)}, bf16[136,1152]{1,0:T(8,128)(2,1)S(1)}, u32[]{:S(2)}, u32[]{:S(2)}) collective-permute-start(bf16[136,1152]{1,0:T(8,128)(2,1)S(1)} %pad_maximum_fusion.4.refs_0_), channel_id=1, source_target_pairs={{0,16},{2,18},{4,20},{6,22},{8,24},{10,26},{12,28},{14,30},{16,0},... | collective-permute-start | bytes 940040 | tf_op jit(solution)/shard_map/ppermute | solution.py:108
  6.5 1.6 %collective-permute-start = (bf16[136,1152]{1,0:T(8,128)(2,1)S(1)}, bf16[136,1152]{1,0:T(8,128)(2,1)S(1)}, u32[]{:S(2)}, u32[]{:S(2)}) collective-permute-start(bf16[136,1152]{1,0:T(8,128)(2,1)S(1)} %pad_maximum_fusion.4.refs_0_), channel_id=1, source_target_pairs={{0,8},{2,10},{4,12},{6,14},{8,0},{10,2},{12,4},{14,6},{16,24},{18,... | collective-permute-start | bytes 940040 | tf_op jit(solution)/shard_map/ppermute | solution.py:108
  8.0 1.1 %constant_dynamic-slice_fusion = bf16[288,1152]{1,0:T(8,128)(2,1)S(1)} fusion(bf16[576,1152]{1,0:T(8,128)(2,1)} %param.19, s32[]{:T(128)S(6)} %select_n.137), kind=kLoop, calls=%fused_computation.79 | loop fusion | bytes 1327108 | tf_op jit(solution)/shard_map/dynamic_slice | solution.py:386
  9.2 1.6 %collective-permute-start.2 = (bf16[288,1152]{1,0:T(8,128)(2,1)S(1)}, bf16[288,1152]{1,0:T(8,128)(2,1)S(1)}, u32[]{:S(2)}, u32[]{:S(2)}) collective-permute-start(bf16[288,1152]{1,0:T(8,128)(2,1)S(1)} %constant_dynamic-slice_fusion), channel_id=1, source_target_pairs={{0,1},{1,0},{2,3},{3,2},{4,5},{5,4},{6,7},{7,6},{8,9},{9,8},{10,11... | collective-permute-start | bytes 1990664 | tf_op jit(solution)/shard_map/ppermute | solution.py:108
  11.1 7.6 %fusion.13 = f32[128,1152]{1,0:T(8,128)S(1)} fusion(bf16[2152,1152]{1,0:T(8,128)(2,1)} %param.18, bf16[1152,2152]{0,1:T(8,128)(2,1)} %param.17, bf16[128,1152]{1,0:T(8,128)(2,1)S(1)} %copy-done.4, f32[1152]{0:T(1024)S(1)} %copy-done.7, f32[128]{0:T(128)S(1)} %add_rsqrt_fusion.1, f32[128]{0:T(128)S(1)} %broadcast_multiply_fusion), kind=kOutput, calls=%fused_computation.25 | convolution fusion | flops 1272517632 | bytes 10806784 | tf_op jit(solution)/shard_map/dot_general | solution.py:396
  18.8 1.9 %collective-permute-done.1.refs_2_ = bf16[136,1152]{1,0:T(8,128)(2,1)S(1)} collective-permute-done((bf16[136,1152]{1,0:T(8,128)(2,1)S(1)}, bf16[136,1152]{1,0:T(8,128)(2,1)S(1)}, u32[]{:S(2)}, u32[]{:S(2)}) %collective-permute-start.1) | collective-permute-done | bytes 313376 | tf_op jit(solution)/shard_map/ppermute | solution.py:108
  20.9 4.5 %collective-permute-done.2 = bf16[288,1152]{1,0:T(8,128)(2,1)S(1)} collective-permute-done((bf16[288,1152]{1,0:T(8,128)(2,1)S(1)}, bf16[288,1152]{1,0:T(8,128)(2,1)S(1)}, u32[]{:S(2)}, u32[]{:S(2)}) %collective-permute-start.2) | collective-permute-done | bytes 663584 | tf_op jit(solution)/shard_map/ppermute | solution.py:108
  25.4 1.6 %collective-permute-start.3 = (f32[64,1152]{1,0:T(8,128)S(1)}, f32[64,1152]{1,0:T(8,128)S(1)}, u32[]{:S(2)}, u32[]{:S(2)}) collective-permute-start(f32[64,1152]{1,0:T(8,128)S(1)} %slice_select_fusion), channel_id=1, source_target_pairs={{0,1},{1,0},{2,3},{3,2},{4,5},{5,4},{6,7},{7,6},{8,9},{9,8},{10,11... | collective-permute-start | bytes 884744 | tf_op jit(solution)/shard_map/ppermute | solution.py:108
  27.5 1.6 %collective-permute-start.5 = (bf16[136,1152]{1,0:T(8,128)(2,1)S(1)}, bf16[136,1152]{1,0:T(8,128)(2,1)S(1)}, u32[]{:S(2)}, u32[]{:S(2)}) collective-permute-start(bf16[136,1152]{1,0:T(8,128)(2,1)S(1)} %broadcast_select_fusion.5), channel_id=1, source_target_pairs={{0,4},{2,6},{4,0},{6,2},{8,12},{10,14},{12,8},{14,10},{16,20},{18,... | collective-permute-start | bytes 940040 | tf_op jit(solution)/shard_map/ppermute | solution.py:108
  29.1 3.6 %collective-permute-done.3 = f32[64,1152]{1,0:T(8,128)S(1)} collective-permute-done((f32[64,1152]{1,0:T(8,128)S(1)}, f32[64,1152]{1,0:T(8,128)S(1)}, u32[]{:S(2)}, u32[]{:S(2)}) %collective-permute-start.3) | collective-permute-done | bytes 294944 | tf_op jit(solution)/shard_map/ppermute | solution.py:108
  33.0 1.6 %collective-permute-done.5.refs_4_ = bf16[136,1152]{1,0:T(8,128)(2,1)S(1)} collective-permute-done((bf16[136,1152]{1,0:T(8,128)(2,1)S(1)}, bf16[136,1152]{1,0:T(8,128)(2,1)S(1)}, u32[]{:S(2)}, u32[]{:S(2)}) %collective-permute-start.5) | collective-permute-done | bytes 313376 | tf_op jit(solution)/shard_map/ppermute | solution.py:108
  36.0 1.5 %collective-permute-start.8 = (bf16[136,1152]{1,0:T(8,128)(2,1)S(1)}, bf16[136,1152]{1,0:T(8,128)(2,1)S(1)}, u32[]{:S(2)}, u32[]{:S(2)}) collective-permute-start(bf16[136,1152]{1,0:T(8,128)(2,1)S(1)} %broadcast_select_fusion.4), channel_id=1, source_target_pairs={{0,4},{2,6},{4,0},{6,2},{8,12},{10,14},{12,8},{14,10},{16,20},{18,... | collective-permute-start | bytes 940040 | tf_op jit(solution)/shard_map/ppermute | solution.py:108
  37.5 1.5 %collective-permute-start.9 = (bf16[136,1152]{1,0:T(8,128)(2,1)S(1)}, bf16[136,1152]{1,0:T(8,128)(2,1)S(1)}, u32[]{:S(2)}, u32[]{:S(2)}) collective-permute-start(bf16[136,1152]{1,0:T(8,128)(2,1)S(1)} %collective-permute-done.5.refs_4_), channel_id=1, source_target_pairs={{0,1},{1,0},{2,3},{3,2},{4,5},{5,4},{6,7},{7,6},{8,9},{9,8},{10,11... | collective-permute-start | bytes 940040 | tf_op jit(solution)/shard_map/ppermute | solution.py:108
  38.9 1.0 collective-permute-done.7
  40.6 2.4 %collective-permute-done.8.refs_5_ = bf16[136,1152]{1,0:T(8,128)(2,1)S(1)} collective-permute-done((bf16[136,1152]{1,0:T(8,128)(2,1)S(1)}, bf16[136,1152]{1,0:T(8,128)(2,1)S(1)}, u32[]{:S(2)}, u32[]{:S(2)}) %collective-permute-start.8) | collective-permute-done | bytes 313376 | tf_op jit(solution)/shard_map/ppermute | solution.py:108
  42.9 1.4 %collective-permute-done.9.refs_6_ = bf16[136,1152]{1,0:T(8,128)(2,1)S(1)} collective-permute-done((bf16[136,1152]{1,0:T(8,128)(2,1)S(1)}, bf16[136,1152]{1,0:T(8,128)(2,1)S(1)}, u32[]{:S(2)}, u32[]{:S(2)}) %collective-permute-start.9) | collective-permute-done | bytes 313376 | tf_op jit(solution)/shard_map/ppermute | solution.py:108
  44.4 1.4 %collective-permute-start.10 = (bf16[64,1152]{1,0:T(8,128)(2,1)S(1)}, bf16[64,1152]{1,0:T(8,128)(2,1)S(1)}, u32[]{:S(2)}, u32[]{:S(2)}) collective-permute-start(bf16[64,1152]{1,0:T(8,128)(2,1)S(1)} %get-tuple-element.42), channel_id=1, source_target_pairs={{0,8},{2,10},{4,12},{6,14},{8,0},{10,2},{12,4},{14,6},{16,24},{18,... | collective-permute-start | bytes 442376 | tf_op jit(solution)/shard_map/ppermute | solution.py:108
  45.8 3.2 %collective-permute-start.11 = (bf16[64,1152]{1,0:T(8,128)(2,1)S(1)}, bf16[64,1152]{1,0:T(8,128)(2,1)S(1)}, u32[]{:S(2)}, u32[]{:S(2)}) collective-permute-start(bf16[64,1152]{1,0:T(8,128)(2,1)S(1)} %get-tuple-element.43), channel_id=1, source_target_pairs={{0,16},{2,18},{4,20},{6,22},{8,24},{10,26},{12,28},{14,30},{16,0},... | collective-permute-start | bytes 442376 | tf_op jit(solution)/shard_map/ppermute | solution.py:108
  49.0 1.5 %collective-permute-start.12 = (bf16[136,1152]{1,0:T(8,128)(2,1)S(1)}, bf16[136,1152]{1,0:T(8,128)(2,1)S(1)}, u32[]{:S(2)}, u32[]{:S(2)}) collective-permute-start(bf16[136,1152]{1,0:T(8,128)(2,1)S(1)} %collective-permute-done.8.refs_5_), channel_id=1, source_target_pairs={{0,1},{1,0},{2,3},{3,2},{4,5},{5,4},{6,7},{7,6},{8,9},{9,8},{10,11... | collective-permute-start | bytes 940040 | tf_op jit(solution)/shard_map/ppermute | solution.py:108
  51.4 1.9 %collective-permute-done.11 = bf16[64,1152]{1,0:T(8,128)(2,1)S(1)} collective-permute-done((bf16[64,1152]{1,0:T(8,128)(2,1)S(1)}, bf16[64,1152]{1,0:T(8,128)(2,1)S(1)}, u32[]{:S(2)}, u32[]{:S(2)}) %collective-permute-start.11) | collective-permute-done | bytes 147488 | tf_op jit(solution)/shard_map/ppermute | solution.py:108
  53.5 2.4 %collective-permute-done.12.refs_7_ = bf16[136,1152]{1,0:T(8,128)(2,1)S(1)} collective-permute-done((bf16[136,1152]{1,0:T(8,128)(2,1)S(1)}, bf16[136,1152]{1,0:T(8,128)(2,1)S(1)}, u32[]{:S(2)}, u32[]{:S(2)}) %collective-permute-start.12) | collective-permute-done | bytes 313376 | tf_op jit(solution)/shard_map/ppermute | solution.py:108
  56.6 7.6 %shard_map.131 = (bf16[1024,1152]{1,0:T(8,128)(2,1)}, f32[1024,1152]{1,0:T(8,128)}, f32[1024,1]{1,0:T(8,128)}, s32[1024,1]{1,0:T(8,128)}, bf16[576,1024]{1,0:T(8,128)(2,1)}) custom-call(s32[1]{0:T(128)} %bitcast.4.flags_ref, bf16[136,1152]{1,0:T(8,128)(2,1)S(1)} %pad_maximum_fusion.4.refs_0_, bf16[136,1152]{1,0:T(8,128)(2,1)S(1)} %collective-permute-done.refs_1_, ...), custom_call_target="tpu_custom_call" | custom-call | flops 5435817984 | bytes 11796480 | tf_op jit(solution)/shard_map/pallas_call | solution.py:197
  66.6 1.6 %collective-permute-start.18 = (bf16[256,1152]{1,0:T(8,128)(2,1)S(1)}, bf16[256,1152]{1,0:T(8,128)(2,1)S(1)}, u32[]{:S(2)}, u32[]{:S(2)}) collective-permute-start(bf16[256,1152]{1,0:T(8,128)(2,1)S(1)} %pad_maximum_fusion.2.refs_0_), channel_id=1, source_target_pairs={{0,1},{1,0},{2,3},{3,2},{4,5},{5,4},{6,7},{7,6},{8,9},{9,8},{10,11... | collective-permute-start | bytes 1769480 | tf_op jit(solution)/shard_map/ppermute | solution.py:108
  68.2 1.2 %collective-permute-start.19 = (bf16[256,1152]{1,0:T(8,128)(2,1)S(1)}, bf16[256,1152]{1,0:T(8,128)(2,1)S(1)}, u32[]{:S(2)}, u32[]{:S(2)}) collective-permute-start(bf16[256,1152]{1,0:T(8,128)(2,1)S(1)} %pad_maximum_fusion.3.refs_2_), channel_id=1, source_target_pairs={{0,4},{2,6},{4,0},{6,2},{8,12},{10,14},{12,8},{14,10},{16,20},{18,... | collective-permute-start | bytes 1769480 | tf_op jit(solution)/shard_map/ppermute | solution.py:108
  69.4 10.7 %shard_map.132 = (f32[1024,1152]{1,0:T(8,128)}, f32[8,128]{1,0:T(8,128)}) custom-call(f32[3]{0:T(128)S(1)} %pad_maximum_fusion.9.knobs_ref, s32[4]{0:T(128)S(1)} %pad_add_fusion.1.offsets_ref, bf16[1024,1152]{1,0:T(8,128)(2,1)} %get-tuple-element.47.embed_ref, s32[1024,1]{1,0:T(8,128)} %get-tuple-element.51.caption_ref, ...), custom_call_target="tpu_custom_call" | custom-call | flops 9663676416 | bytes 9437184 | tf_op jit(solution)/shard_map/pallas_call | solution.py:310
  80.1 1.8 %collective-permute-done.18.refs_0_ = bf16[256,1152]{1,0:T(8,128)(2,1)S(1)} collective-permute-done((bf16[256,1152]{1,0:T(8,128)(2,1)S(1)}, bf16[256,1152]{1,0:T(8,128)(2,1)S(1)}, u32[]{:S(2)}, u32[]{:S(2)}) %collective-permute-start.18) | collective-permute-done | bytes 589856 | tf_op jit(solution)/shard_map/ppermute | solution.py:108
  81.9 1.3 %collective-permute-done.19.refs_2_ = bf16[256,1152]{1,0:T(8,128)(2,1)S(1)} collective-permute-done((bf16[256,1152]{1,0:T(8,128)(2,1)S(1)}, bf16[256,1152]{1,0:T(8,128)(2,1)S(1)}, u32[]{:S(2)}, u32[]{:S(2)}) %collective-permute-start.19) | collective-permute-done | bytes 589856 | tf_op jit(solution)/shard_map/ppermute | solution.py:108
  83.8 1.4 %collective-permute-done.20.refs_1_ = bf16[256,1152]{1,0:T(8,128)(2,1)S(1)} collective-permute-done((bf16[256,1152]{1,0:T(8,128)(2,1)S(1)}, bf16[256,1152]{1,0:T(8,128)(2,1)S(1)}, u32[]{:S(2)}, u32[]{:S(2)}) %collective-permute-start.20) | collective-permute-done | bytes 589856 | tf_op jit(solution)/shard_map/ppermute | solution.py:108
  86.7 14.6 %shard_map.133 = (f32[576,1152]{1,0:T(8,128)S(1)}, f32[8,128]{1,0:T(8,128)S(1)}) custom-call(f32[3]{0:T(128)S(1)} %pad_maximum_fusion.9.knobs_ref, s32[4]{0:T(128)S(1)} %pad_add_fusion.offsets_ref, bf16[1024,1152]{1,0:T(8,128)(2,1)} %get-tuple-element.47.embed_ref, s32[1024,1]{1,0:T(8,128)} %get-tuple-element.51.caption_ref, ...), custom_call_target="tpu_custom_call" | custom-call | flops 15099494400 | bytes 18874368 | tf_op jit(solution)/shard_map/pallas_call | solution.py:330
  101.9 4.5 %collective-permute-done.23 = f32[8,128]{1,0:T(8,128)S(1)} collective-permute-done((f32[8,128]{1,0:T(8,128)S(1)}, f32[8,128]{1,0:T(8,128)S(1)}, u32[]{:S(2)}, u32[]{:S(2)}) %collective-permute-start.23) | collective-permute-done | bytes 4128 | tf_op jit(solution)/shard_map/ppermute | solution.py:108
  107.6 1.3 %add_convert_fusion = bf16[576,1152]{1,0:T(8,128)(2,1)} fusion(f32[576,1152]{1,0:T(8,128)S(1)} %get-tuple-element.62, f32[576,1152]{1,0:T(8,128)S(1)} %collective-permute-done.22), kind=kLoop, calls=%fused_computation.1 | loop fusion | flops 1327104 | bytes 6635520 | tf_op jit(solution)/shard_map/convert_element_type | solution.py:459
  (71 shorter events, 10.0 us)
Async XLA Ops:
  0.6 10.1 %copy-start.4 = (bf16[128,1152]{1,0:T(8,128)(2,1)S(1)}, bf16[128,1152]{1,0:T(8,128)(2,1)}, u32[]{:S(2)}) copy-start(bf16[128,1152]{1,0:T(8,128)(2,1)} %param.12) | copy-start | bytes 884740
  0.6 10.5 %copy-start.7 = (f32[1152]{0:T(1024)S(1)}, f32[1152]{0:T(1024)}, u32[]{:S(2)}) copy-start(f32[1152]{0:T(1024)} %param.15) | copy-start | bytes 13828
  2.4 18.3 %collective-permute-start.1 = (bf16[136,1152]{1,0:T(8,128)(2,1)S(1)}, bf16[136,1152]{1,0:T(8,128)(2,1)S(1)}, u32[]{:S(2)}, u32[]{:S(2)}) collective-permute-start(bf16[136,1152]{1,0:T(8,128)(2,1)S(1)} %pad_maximum_fusion.4.refs_0_), channel_id=1, source_target_pairs={{0,16},{2,18},{4,20},{6,22},{8,24},{10,26},{12,28},{14,30},{16,0},... | collective-permute-start | bytes 940040 | tf_op jit(solution)/shard_map/ppermute | solution.py:108
  6.5 14.4 %collective-permute-start = (bf16[136,1152]{1,0:T(8,128)(2,1)S(1)}, bf16[136,1152]{1,0:T(8,128)(2,1)S(1)}, u32[]{:S(2)}, u32[]{:S(2)}) collective-permute-start(bf16[136,1152]{1,0:T(8,128)(2,1)S(1)} %pad_maximum_fusion.4.refs_0_), channel_id=1, source_target_pairs={{0,8},{2,10},{4,12},{6,14},{8,0},{10,2},{12,4},{14,6},{16,24},{18,... | collective-permute-start | bytes 940040 | tf_op jit(solution)/shard_map/ppermute | solution.py:108
  9.2 16.2 %collective-permute-start.2 = (bf16[288,1152]{1,0:T(8,128)(2,1)S(1)}, bf16[288,1152]{1,0:T(8,128)(2,1)S(1)}, u32[]{:S(2)}, u32[]{:S(2)}) collective-permute-start(bf16[288,1152]{1,0:T(8,128)(2,1)S(1)} %constant_dynamic-slice_fusion), channel_id=1, source_target_pairs={{0,1},{1,0},{2,3},{3,2},{4,5},{5,4},{6,7},{7,6},{8,9},{9,8},{10,11... | collective-permute-start | bytes 1990664 | tf_op jit(solution)/shard_map/ppermute | solution.py:108
  11.1 7.6 %copy-start.6 = (f32[1152]{0:T(1024)S(1)}, f32[1152]{0:T(1024)}, u32[]{:S(2)}) copy-start(f32[1152]{0:T(1024)} %param.16) | copy-start | bytes 13828
  11.1 16.2 %copy-start.5 = (bf16[128,1152]{1,0:T(8,128)(2,1)S(1)}, bf16[128,1152]{1,0:T(8,128)(2,1)}, u32[]{:S(2)}) copy-start(bf16[128,1152]{1,0:T(8,128)(2,1)} %param.13) | copy-start | bytes 884740
  25.4 7.3 %collective-permute-start.3 = (f32[64,1152]{1,0:T(8,128)S(1)}, f32[64,1152]{1,0:T(8,128)S(1)}, u32[]{:S(2)}, u32[]{:S(2)}) collective-permute-start(f32[64,1152]{1,0:T(8,128)S(1)} %slice_select_fusion), channel_id=1, source_target_pairs={{0,1},{1,0},{2,3},{3,2},{4,5},{5,4},{6,7},{7,6},{8,9},{9,8},{10,11... | collective-permute-start | bytes 884744 | tf_op jit(solution)/shard_map/ppermute | solution.py:108
  26.9 7.7 %collective-permute-start.4 = (bf16[136,1152]{1,0:T(8,128)(2,1)S(1)}, bf16[136,1152]{1,0:T(8,128)(2,1)S(1)}, u32[]{:S(2)}, u32[]{:S(2)}) collective-permute-start(bf16[136,1152]{1,0:T(8,128)(2,1)S(1)} %collective-permute-done.1.refs_2_), channel_id=1, source_target_pairs={{0,8},{2,10},{4,12},{6,14},{8,0},{10,2},{12,4},{14,6},{16,24},{18,... | collective-permute-start | bytes 940040 | tf_op jit(solution)/shard_map/ppermute | solution.py:108
  27.5 7.2 %collective-permute-start.5 = (bf16[136,1152]{1,0:T(8,128)(2,1)S(1)}, bf16[136,1152]{1,0:T(8,128)(2,1)S(1)}, u32[]{:S(2)}, u32[]{:S(2)}) collective-permute-start(bf16[136,1152]{1,0:T(8,128)(2,1)S(1)} %broadcast_select_fusion.5), channel_id=1, source_target_pairs={{0,4},{2,6},{4,0},{6,2},{8,12},{10,14},{12,8},{14,10},{16,20},{18,... | collective-permute-start | bytes 940040 | tf_op jit(solution)/shard_map/ppermute | solution.py:108
  29.1 21.4 %collective-permute-start.13 = (bf16[288,1152]{1,0:T(8,128)(2,1)S(1)}, bf16[288,1152]{1,0:T(8,128)(2,1)S(1)}, u32[]{:S(2)}, u32[]{:S(2)}) collective-permute-start(bf16[288,1152]{1,0:T(8,128)(2,1)S(1)} %collective-permute-done.2), channel_id=1, source_target_pairs={{0,2},{2,0},{4,6},{6,4},{8,10},{10,8},{12,14},{14,12},{16,18},{18,... | collective-permute-start | bytes 1990664 | tf_op jit(solution)/shard_map/ppermute | solution.py:108
  34.7 5.3 %collective-permute-start.7 = (bf16[32,1152]{1,0:T(8,128)(2,1)S(1)}, bf16[32,1152]{1,0:T(8,128)(2,1)S(1)}, u32[]{:S(2)}, u32[]{:S(2)}) collective-permute-start(bf16[32,1152]{1,0:T(8,128)(2,1)S(1)} %get-tuple-element.84), channel_id=1, source_target_pairs={{0,1},{1,0},{2,3},{3,2},{4,5},{5,4},{6,7},{7,6},{8,9},{9,8},{10,11... | collective-permute-start | bytes 221192 | tf_op jit(solution)/shard_map/ppermute | solution.py:108
  35.3 5.3 %collective-permute-start.6 = (bf16[32,1152]{1,0:T(8,128)(2,1)S(1)}, bf16[32,1152]{1,0:T(8,128)(2,1)S(1)}, u32[]{:S(2)}, u32[]{:S(2)}) collective-permute-start(bf16[32,1152]{1,0:T(8,128)(2,1)S(1)} %get-tuple-element.85), channel_id=1, source_target_pairs={{0,16},{2,18},{4,20},{6,22},{8,24},{10,26},{12,28},{14,30},{16,0},... | collective-permute-start | bytes 221192 | tf_op jit(solution)/shard_map/ppermute | solution.py:108
  36.0 7.0 %collective-permute-start.8 = (bf16[136,1152]{1,0:T(8,128)(2,1)S(1)}, bf16[136,1152]{1,0:T(8,128)(2,1)S(1)}, u32[]{:S(2)}, u32[]{:S(2)}) collective-permute-start(bf16[136,1152]{1,0:T(8,128)(2,1)S(1)} %broadcast_select_fusion.4), channel_id=1, source_target_pairs={{0,4},{2,6},{4,0},{6,2},{8,12},{10,14},{12,8},{14,10},{16,20},{18,... | collective-permute-start | bytes 940040 | tf_op jit(solution)/shard_map/ppermute | solution.py:108
  37.5 6.9 %collective-permute-start.9 = (bf16[136,1152]{1,0:T(8,128)(2,1)S(1)}, bf16[136,1152]{1,0:T(8,128)(2,1)S(1)}, u32[]{:S(2)}, u32[]{:S(2)}) collective-permute-start(bf16[136,1152]{1,0:T(8,128)(2,1)S(1)} %collective-permute-done.5.refs_4_), channel_id=1, source_target_pairs={{0,1},{1,0},{2,3},{3,2},{4,5},{5,4},{6,7},{7,6},{8,9},{9,8},{10,11... | collective-permute-start | bytes 940040 | tf_op jit(solution)/shard_map/ppermute | solution.py:108
  44.4 6.3 %copy-start.3 = (bf16[576,1152]{1,0:T(8,128)(2,1)S(1)}, bf16[576,1152]{1,0:T(8,128)(2,1)}, u32[]{:S(2)}) copy-start(bf16[576,1152]{1,0:T(8,128)(2,1)} %param.19) | copy-start | bytes 3981316
  44.4 9.0 %collective-permute-start.10 = (bf16[64,1152]{1,0:T(8,128)(2,1)S(1)}, bf16[64,1152]{1,0:T(8,128)(2,1)S(1)}, u32[]{:S(2)}, u32[]{:S(2)}) collective-permute-start(bf16[64,1152]{1,0:T(8,128)(2,1)S(1)} %get-tuple-element.42), channel_id=1, source_target_pairs={{0,8},{2,10},{4,12},{6,14},{8,0},{10,2},{12,4},{14,6},{16,24},{18,... | collective-permute-start | bytes 442376 | tf_op jit(solution)/shard_map/ppermute | solution.py:108
  45.8 7.6 %collective-permute-start.11 = (bf16[64,1152]{1,0:T(8,128)(2,1)S(1)}, bf16[64,1152]{1,0:T(8,128)(2,1)S(1)}, u32[]{:S(2)}, u32[]{:S(2)}) collective-permute-start(bf16[64,1152]{1,0:T(8,128)(2,1)S(1)} %get-tuple-element.43), channel_id=1, source_target_pairs={{0,16},{2,18},{4,20},{6,22},{8,24},{10,26},{12,28},{14,30},{16,0},... | collective-permute-start | bytes 442376 | tf_op jit(solution)/shard_map/ppermute | solution.py:108
  49.0 6.9 %collective-permute-start.12 = (bf16[136,1152]{1,0:T(8,128)(2,1)S(1)}, bf16[136,1152]{1,0:T(8,128)(2,1)S(1)}, u32[]{:S(2)}, u32[]{:S(2)}) collective-permute-start(bf16[136,1152]{1,0:T(8,128)(2,1)S(1)} %collective-permute-done.8.refs_5_), channel_id=1, source_target_pairs={{0,1},{1,0},{2,3},{3,2},{4,5},{5,4},{6,7},{7,6},{8,9},{9,8},{10,11... | collective-permute-start | bytes 940040 | tf_op jit(solution)/shard_map/ppermute | solution.py:108
  55.9 8.3 %collective-permute-start.14 = (bf16[128,1152]{1,0:T(8,128)(2,1)S(1)}, bf16[128,1152]{1,0:T(8,128)(2,1)S(1)}, u32[]{:S(2)}, u32[]{:S(2)}) collective-permute-start(bf16[128,1152]{1,0:T(8,128)(2,1)S(1)} %pad_maximum_fusion.5), channel_id=1, source_target_pairs={{0,4},{2,6},{4,0},{6,2},{8,12},{10,14},{12,8},{14,10},{16,20},{18,... | collective-permute-start | bytes 884744 | tf_op jit(solution)/shard_map/ppermute | solution.py:108
  56.6 7.8 %collective-permute-start.15 = (bf16[128,1152]{1,0:T(8,128)(2,1)S(1)}, bf16[128,1152]{1,0:T(8,128)(2,1)S(1)}, u32[]{:S(2)}, u32[]{:S(2)}) collective-permute-start(bf16[128,1152]{1,0:T(8,128)(2,1)S(1)} %pad_maximum_fusion.6), channel_id=1, source_target_pairs={{0,8},{2,10},{4,12},{6,14},{8,0},{10,2},{12,4},{14,6},{16,24},{18,... | collective-permute-start | bytes 884744 | tf_op jit(solution)/shard_map/ppermute | solution.py:108
  64.4 5.0 %copy-start = (s32[1,256]{1,0:T(1,128)S(1)}, s32[1,256]{1,0:T(1,128)}, u32[]{:S(2)}) copy-start(s32[1,256]{1,0:T(1,128)} %constant.84.clone.refs_6_.refs_7_) | copy-start | bytes 3076
  64.4 5.0 %copy-start.1 = (s32[1,256]{1,0:T(1,128)S(1)}, s32[1,256]{1,0:T(1,128)}, u32[]{:S(2)}) copy-start(s32[1,256]{1,0:T(1,128)} %constant.83.clone.refs_4_.refs_5_) | copy-start | bytes 3076
  64.5 4.9 %collective-permute-start.16 = (bf16[256,1152]{1,0:T(8,128)(2,1)S(1)}, bf16[256,1152]{1,0:T(8,128)(2,1)S(1)}, u32[]{:S(2)}, u32[]{:S(2)}) collective-permute-start(bf16[256,1152]{1,0:T(8,128)(2,1)S(1)} %pad_maximum_fusion.2.refs_0_), channel_id=1, source_target_pairs={{0,2},{2,0},{4,6},{6,4},{8,10},{10,8},{12,14},{14,12},{16,18},{18,... | collective-permute-start | bytes 1769480 | tf_op jit(solution)/shard_map/ppermute | solution.py:108
  64.6 4.8 %collective-permute-start.17 = (bf16[256,1152]{1,0:T(8,128)(2,1)S(1)}, bf16[256,1152]{1,0:T(8,128)(2,1)S(1)}, u32[]{:S(2)}, u32[]{:S(2)}) collective-permute-start(bf16[256,1152]{1,0:T(8,128)(2,1)S(1)} %pad_maximum_fusion.3.refs_2_), channel_id=1, source_target_pairs={{0,2},{2,0},{4,6},{6,4},{8,10},{10,8},{12,14},{14,12},{16,18},{18,... | collective-permute-start | bytes 1769480 | tf_op jit(solution)/shard_map/ppermute | solution.py:108
  66.6 15.3 %collective-permute-start.18 = (bf16[256,1152]{1,0:T(8,128)(2,1)S(1)}, bf16[256,1152]{1,0:T(8,128)(2,1)S(1)}, u32[]{:S(2)}, u32[]{:S(2)}) collective-permute-start(bf16[256,1152]{1,0:T(8,128)(2,1)S(1)} %pad_maximum_fusion.2.refs_0_), channel_id=1, source_target_pairs={{0,1},{1,0},{2,3},{3,2},{4,5},{5,4},{6,7},{7,6},{8,9},{9,8},{10,11... | collective-permute-start | bytes 1769480 | tf_op jit(solution)/shard_map/ppermute | solution.py:108
  68.2 15.0 %collective-permute-start.19 = (bf16[256,1152]{1,0:T(8,128)(2,1)S(1)}, bf16[256,1152]{1,0:T(8,128)(2,1)S(1)}, u32[]{:S(2)}, u32[]{:S(2)}) collective-permute-start(bf16[256,1152]{1,0:T(8,128)(2,1)S(1)} %pad_maximum_fusion.3.refs_2_), channel_id=1, source_target_pairs={{0,4},{2,6},{4,0},{6,2},{8,12},{10,14},{12,8},{14,10},{16,20},{18,... | collective-permute-start | bytes 1769480 | tf_op jit(solution)/shard_map/ppermute | solution.py:108
  83.2 2.0 %collective-permute-start.20 = (bf16[256,1152]{1,0:T(8,128)(2,1)S(1)}, bf16[256,1152]{1,0:T(8,128)(2,1)S(1)}, u32[]{:S(2)}, u32[]{:S(2)}) collective-permute-start(bf16[256,1152]{1,0:T(8,128)(2,1)S(1)} %collective-permute-done.18.refs_0_), channel_id=1, source_target_pairs={{0,2},{2,0},{4,6},{6,4},{8,10},{10,8},{12,14},{14,12},{16,18},{18,... | collective-permute-start | bytes 1769480 | tf_op jit(solution)/shard_map/ppermute | solution.py:108
  83.2 2.8 %collective-permute-start.21 = (bf16[256,1152]{1,0:T(8,128)(2,1)S(1)}, bf16[256,1152]{1,0:T(8,128)(2,1)S(1)}, u32[]{:S(2)}, u32[]{:S(2)}) collective-permute-start(bf16[256,1152]{1,0:T(8,128)(2,1)S(1)} %collective-permute-done.19.refs_2_), channel_id=1, source_target_pairs={{0,2},{2,0},{4,6},{6,4},{8,10},{10,8},{12,14},{14,12},{16,18},{18,... | collective-permute-start | bytes 1769480 | tf_op jit(solution)/shard_map/ppermute | solution.py:108
  86.1 0.7 copy-start.2
  101.4 6.2 %collective-permute-start.22 = (f32[576,1152]{1,0:T(8,128)S(1)}, f32[576,1152]{1,0:T(8,128)S(1)}, u32[]{:S(2)}, u32[]{:S(2)}) collective-permute-start(f32[576,1152]{1,0:T(8,128)S(1)} %get-tuple-element.62), channel_id=1, source_target_pairs={{0,2},{2,0},{4,6},{6,4},{8,10},{10,8},{12,14},{14,12},{16,18},{18,... | collective-permute-start | bytes 7962632 | tf_op jit(solution)/shard_map/ppermute | solution.py:108
  101.6 4.8 %collective-permute-start.23 = (f32[8,128]{1,0:T(8,128)S(1)}, f32[8,128]{1,0:T(8,128)S(1)}, u32[]{:S(2)}, u32[]{:S(2)}) collective-permute-start(f32[8,128]{1,0:T(8,128)S(1)} %get-tuple-element.63), channel_id=1, source_target_pairs={{0,2},{2,0},{4,6},{6,4},{8,10},{10,8},{12,14},{14,12},{16,18},{18,... | collective-permute-start | bytes 12296 | tf_op jit(solution)/shard_map/ppermute | solution.py:108

commit v4 on v3

--- a/solution.py
+++ b/solution.py
@@ -384,17 +384,19 @@
     packed = jnp.concatenate([text_last, extra], axis=0)
     in_half = adapter.shape[0] // 2
     sent = lax.dynamic_slice_in_dim(adapter, (dp & CORE) * in_half, in_half, 0)
-    image_pooled = after(image_pooled, packed, sent)
+    image_pooled = after(image_pooled, sent)
+    piece = swap_x(sent)
+
+    image_norm = layer_norm(image_pooled, image_gain).astype(jnp.bfloat16)
+    image_norm, packed = lax.optimization_barrier((image_norm, packed))
     from_high = swap(packed, "dp", Z_HIGH)
     from_low = swap(packed, "dp", Z_LOW)
-    piece = swap_x(sent)
-
-    image_norm = layer_norm(image_pooled, image_gain).astype(jnp.bfloat16)
     hidden = jax.nn.gelu(
         jnp.dot(image_norm, mlp_up, preferred_element_type=jnp.float32), approximate=True
     ).astype(jnp.bfloat16)
     branch = jnp.dot(hidden, mlp_down, preferred_element_type=jnp.float32)
-    branch, from_low, from_high, piece = lax.optimization_barrier((branch, from_low, from_high, piece))
+    branch, piece = lax.optimization_barrier((branch, piece))
+    branch, from_low = lax.optimization_barrier((branch, from_low))
     from_both = swap(from_high, "dp", Z_LOW)
     near_0 = swap(jnp.where(own_x, from_high, packed), "dp", Y)
     arrived = swap_x(half_of(branch, ~own_x, half_rows))
@@ -456,8 +458,9 @@
     part, loss = late_scores(
         knobs, far.astype(jnp.int32), embed, caption, early, early_loss, unit, inverse, turned, images, where
     )
-    grad_adapter = (part + swap_core(part)).astype(jnp.bfloat16)
     mean_loss = (loss + swap_core(loss))[0, :1] / (pair_count * pair_count)
+    other, mean_loss = lax.optimization_barrier((swap_core(part), mean_loss))
+    grad_adapter = (part + other).astype(jnp.bfloat16)
     return grad_adapter, mean_loss
 
 

time: 110 us -> 108 us (0.982)
  other arithmetic: 5.39 us -> 3.81 us
  transfers between devices with their start and end apart: 24 -> 24, of which waited for: 16 -> 15; matrix products, arithmetic and copies ran while one was open for 10% -> 10% of each run, Pallas kernels for 17% -> 17%
where the time goes in v4:
time: 108 us
  Pallas kernels  32.9 us (30%)
  waiting for transfers between devices  30.4 us (28%)
  starting transfers between devices  26.8 us (25%)
  matrix products  7.48 us (7%)
  between operations  4.06 us (4%)
  other arithmetic  3.81 us (4%)
  local copies, waits for them, and re-layouts  2.46 us (2%)
    ppermute x24, waiting for transfers between devices, swap(): return lax.ppermute(values, axis, [(i, i ^ bit) for i in range(count)])  30.4 us
    ppermute x24, starting transfers between devices, swap(): return lax.ppermute(values, axis, [(i, i ^ bit) for i in range(count)])  26.8 us
    pallas_call x1, Pallas kernels, late_scores(): pl.pallas_call(functools.partial(late_kernel, len(images)), grid=(count /...  14.6 us
    pallas_call x1, Pallas kernels, early_scores(): pl.pallas_call(functools.partial(early_kernel, len(images)), grid=(count...  10.7 us
    pallas_call x1, Pallas kernels, text_side(): pl.pallas_call(text_kernel, grid=(4,), in_specs=[SMEM] + [whole_spec(piec...  7.61 us
    dot_general x1, matrix products, slice_plan(): branch = jnp.dot(hidden, mlp_down, preferred_element_type=jnp.float32)  7.48 us
  transfers between devices with their start and end apart: 24, of which 15 were waited for; matrix products, arithmetic and copies ran while one was open for 10% of the time, Pallas kernels for 17%

profile of v4, /device:TPU:0, one launch (start us, length us, event | category | flops | bytes accessed | tf_op | source)
XLA Modules:
  0.0 108.0 jit_solution(9047131739490181361)
XLA Ops:
  0.7 1.2 %constant_dynamic-slice_fusion = bf16[288,1152]{1,0:T(8,128)(2,1)S(1)} fusion(bf16[576,1152]{1,0:T(8,128)(2,1)} %param.19, s32[]{:T(128)S(6)} %select_n.135), kind=kLoop, calls=%fused_computation.75 | loop fusion | bytes 1327108 | tf_op jit(solution)/shard_map/dynamic_slice | solution.py:386
  1.9 3.0 %collective-permute-start = (bf16[288,1152]{1,0:T(8,128)(2,1)S(1)}, bf16[288,1152]{1,0:T(8,128)(2,1)S(1)}, u32[]{:S(2)}, u32[]{:S(2)}) collective-permute-start(bf16[288,1152]{1,0:T(8,128)(2,1)S(1)} %constant_dynamic-slice_fusion), channel_id=1, source_target_pairs={{0,1},{1,0},{2,3},{3,2},{4,5},{5,4},{6,7},{7,6},{8,9},{9,8},{10,11... | collective-permute-start | bytes 1990664 | tf_op jit(solution)/shard_map/ppermute | solution.py:108
  5.6 2.7 %collective-permute-start.2 = (bf16[136,1152]{1,0:T(8,128)(2,1)S(1)}, bf16[136,1152]{1,0:T(8,128)(2,1)S(1)}, u32[]{:S(2)}, u32[]{:S(2)}) collective-permute-start(bf16[136,1152]{1,0:T(8,128)(2,1)S(1)} %pad_maximum_fusion.4.refs_0_), channel_id=1, source_target_pairs={{0,16},{2,18},{4,20},{6,22},{8,24},{10,26},{12,28},{14,30},{16,0},... | collective-permute-start | bytes 940040 | tf_op jit(solution)/shard_map/ppermute | solution.py:108
  8.2 1.6 %collective-permute-start.1 = (bf16[136,1152]{1,0:T(8,128)(2,1)S(1)}, bf16[136,1152]{1,0:T(8,128)(2,1)S(1)}, u32[]{:S(2)}, u32[]{:S(2)}) collective-permute-start(bf16[136,1152]{1,0:T(8,128)(2,1)S(1)} %pad_maximum_fusion.4.refs_0_), channel_id=1, source_target_pairs={{0,8},{2,10},{4,12},{6,14},{8,0},{10,2},{12,4},{14,6},{16,24},{18,... | collective-permute-start | bytes 940040 | tf_op jit(solution)/shard_map/ppermute | solution.py:108
  9.8 7.5 %fusion.13 = f32[128,1152]{1,0:T(8,128)S(1)} fusion(bf16[2152,1152]{1,0:T(8,128)(2,1)} %param.18, bf16[128,1152]{1,0:T(8,128)(2,1)S(1)} %fusion.12, bf16[1152,2152]{0,1:T(8,128)(2,1)} %param.17), kind=kOutput, calls=%fused_computation.25 | convolution fusion | flops 1271780352 | bytes 10801152 | tf_op jit(solution)/shard_map/dot_general | solution.py:397
  17.4 2.4 %collective-permute-done = bf16[288,1152]{1,0:T(8,128)(2,1)S(1)} collective-permute-done((bf16[288,1152]{1,0:T(8,128)(2,1)S(1)}, bf16[288,1152]{1,0:T(8,128)(2,1)S(1)}, u32[]{:S(2)}, u32[]{:S(2)}) %collective-permute-start) | collective-permute-done | bytes 663584 | tf_op jit(solution)/shard_map/ppermute | solution.py:108
  19.8 2.6 %collective-permute-done.1.refs_1_ = bf16[136,1152]{1,0:T(8,128)(2,1)S(1)} collective-permute-done((bf16[136,1152]{1,0:T(8,128)(2,1)S(1)}, bf16[136,1152]{1,0:T(8,128)(2,1)S(1)}, u32[]{:S(2)}, u32[]{:S(2)}) %collective-permute-start.1) | collective-permute-done | bytes 313376 | tf_op jit(solution)/shard_map/ppermute | solution.py:108
  23.1 1.6 %collective-permute-start.5 = (bf16[136,1152]{1,0:T(8,128)(2,1)S(1)}, bf16[136,1152]{1,0:T(8,128)(2,1)S(1)}, u32[]{:S(2)}, u32[]{:S(2)}) collective-permute-start(bf16[136,1152]{1,0:T(8,128)(2,1)S(1)} %broadcast_select_fusion.5), channel_id=1, source_target_pairs={{0,4},{2,6},{4,0},{6,2},{8,12},{10,14},{12,8},{14,10},{16,20},{18,... | collective-permute-start | bytes 940040 | tf_op jit(solution)/shard_map/ppermute | solution.py:108
  24.7 1.4 %collective-permute-start.4 = (bf16[136,1152]{1,0:T(8,128)(2,1)S(1)}, bf16[136,1152]{1,0:T(8,128)(2,1)S(1)}, u32[]{:S(2)}, u32[]{:S(2)}) collective-permute-start(bf16[136,1152]{1,0:T(8,128)(2,1)S(1)} %collective-permute-done.2.refs_2_), channel_id=1, source_target_pairs={{0,8},{2,10},{4,12},{6,14},{8,0},{10,2},{12,4},{14,6},{16,24},{18,... | collective-permute-start | bytes 940040 | tf_op jit(solution)/shard_map/ppermute | solution.py:108
  26.1 3.1 %collective-permute-done.3 = f32[64,1152]{1,0:T(8,128)S(1)} collective-permute-done((f32[64,1152]{1,0:T(8,128)S(1)}, f32[64,1152]{1,0:T(8,128)S(1)}, u32[]{:S(2)}, u32[]{:S(2)}) %collective-permute-start.3) | collective-permute-done | bytes 294944 | tf_op jit(solution)/shard_map/ppermute | solution.py:108
  29.5 1.0 collective-permute-done.5.refs_4_
  30.5 1.2 %collective-permute-done.4.refs_3_ = bf16[136,1152]{1,0:T(8,128)(2,1)S(1)} collective-permute-done((bf16[136,1152]{1,0:T(8,128)(2,1)S(1)}, bf16[136,1152]{1,0:T(8,128)(2,1)S(1)}, u32[]{:S(2)}, u32[]{:S(2)}) %collective-permute-start.4) | collective-permute-done | bytes 313376 | tf_op jit(solution)/shard_map/ppermute | solution.py:108
  31.8 1.6 %collective-permute-start.7 = (bf16[32,1152]{1,0:T(8,128)(2,1)S(1)}, bf16[32,1152]{1,0:T(8,128)(2,1)S(1)}, u32[]{:S(2)}, u32[]{:S(2)}) collective-permute-start(bf16[32,1152]{1,0:T(8,128)(2,1)S(1)} %get-tuple-element.92), channel_id=1, source_target_pairs={{0,1},{1,0},{2,3},{3,2},{4,5},{5,4},{6,7},{7,6},{8,9},{9,8},{10,11... | collective-permute-start | bytes 221192 | tf_op jit(solution)/shard_map/ppermute | solution.py:108
  33.4 2.4 %collective-permute-start.6 = (bf16[32,1152]{1,0:T(8,128)(2,1)S(1)}, bf16[32,1152]{1,0:T(8,128)(2,1)S(1)}, u32[]{:S(2)}, u32[]{:S(2)}) collective-permute-start(bf16[32,1152]{1,0:T(8,128)(2,1)S(1)} %get-tuple-element.93), channel_id=1, source_target_pairs={{0,16},{2,18},{4,20},{6,22},{8,24},{10,26},{12,28},{14,30},{16,0},... | collective-permute-start | bytes 221192 | tf_op jit(solution)/shard_map/ppermute | solution.py:108
  36.3 1.5 %collective-permute-start.9 = (bf16[136,1152]{1,0:T(8,128)(2,1)S(1)}, bf16[136,1152]{1,0:T(8,128)(2,1)S(1)}, u32[]{:S(2)}, u32[]{:S(2)}) collective-permute-start(bf16[136,1152]{1,0:T(8,128)(2,1)S(1)} %collective-permute-done.5.refs_4_), channel_id=1, source_target_pairs={{0,1},{1,0},{2,3},{3,2},{4,5},{5,4},{6,7},{7,6},{8,9},{9,8},{10,11... | collective-permute-start | bytes 940040 | tf_op jit(solution)/shard_map/ppermute | solution.py:108
  38.7 4.6 %collective-permute-done.8.refs_5_ = bf16[136,1152]{1,0:T(8,128)(2,1)S(1)} collective-permute-done((bf16[136,1152]{1,0:T(8,128)(2,1)S(1)}, bf16[136,1152]{1,0:T(8,128)(2,1)S(1)}, u32[]{:S(2)}, u32[]{:S(2)}) %collective-permute-start.8) | collective-permute-done | bytes 313376 | tf_op jit(solution)/shard_map/ppermute | solution.py:108
  43.5 2.0 %collective-permute-start.10 = (bf16[64,1152]{1,0:T(8,128)(2,1)S(1)}, bf16[64,1152]{1,0:T(8,128)(2,1)S(1)}, u32[]{:S(2)}, u32[]{:S(2)}) collective-permute-start(bf16[64,1152]{1,0:T(8,128)(2,1)S(1)} %get-tuple-element.48), channel_id=1, source_target_pairs={{0,8},{2,10},{4,12},{6,14},{8,0},{10,2},{12,4},{14,6},{16,24},{18,... | collective-permute-start | bytes 442376 | tf_op jit(solution)/shard_map/ppermute | solution.py:108
  45.5 1.2 %collective-permute-start.11 = (bf16[64,1152]{1,0:T(8,128)(2,1)S(1)}, bf16[64,1152]{1,0:T(8,128)(2,1)S(1)}, u32[]{:S(2)}, u32[]{:S(2)}) collective-permute-start(bf16[64,1152]{1,0:T(8,128)(2,1)S(1)} %get-tuple-element.49), channel_id=1, source_target_pairs={{0,16},{2,18},{4,20},{6,22},{8,24},{10,26},{12,28},{14,30},{16,0},... | collective-permute-start | bytes 442376 | tf_op jit(solution)/shard_map/ppermute | solution.py:108
  46.7 1.4 %collective-permute-start.12 = (bf16[136,1152]{1,0:T(8,128)(2,1)S(1)}, bf16[136,1152]{1,0:T(8,128)(2,1)S(1)}, u32[]{:S(2)}, u32[]{:S(2)}) collective-permute-start(bf16[136,1152]{1,0:T(8,128)(2,1)S(1)} %collective-permute-done.8.refs_5_), channel_id=1, source_target_pairs={{0,1},{1,0},{2,3},{3,2},{4,5},{5,4},{6,7},{7,6},{8,9},{9,8},{10,11... | collective-permute-start | bytes 940040 | tf_op jit(solution)/shard_map/ppermute | solution.py:108
  49.0 3.9 %collective-permute-done.11 = bf16[64,1152]{1,0:T(8,128)(2,1)S(1)} collective-permute-done((bf16[64,1152]{1,0:T(8,128)(2,1)S(1)}, bf16[64,1152]{1,0:T(8,128)(2,1)S(1)}, u32[]{:S(2)}, u32[]{:S(2)}) %collective-permute-start.11) | collective-permute-done | bytes 147488 | tf_op jit(solution)/shard_map/ppermute | solution.py:108
  53.6 1.3 %collective-permute-start.14 = (bf16[128,1152]{1,0:T(8,128)(2,1)S(1)}, bf16[128,1152]{1,0:T(8,128)(2,1)S(1)}, u32[]{:S(2)}, u32[]{:S(2)}) collective-permute-start(bf16[128,1152]{1,0:T(8,128)(2,1)S(1)} %pad_maximum_fusion.5), channel_id=1, source_target_pairs={{0,4},{2,6},{4,0},{6,2},{8,12},{10,14},{12,8},{14,10},{16,20},{18,... | collective-permute-start | bytes 884744 | tf_op jit(solution)/shard_map/ppermute | solution.py:108
  55.1 7.6 %shard_map.131 = (bf16[1024,1152]{1,0:T(8,128)(2,1)}, f32[1024,1152]{1,0:T(8,128)}, f32[1024,1]{1,0:T(8,128)}, s32[1024,1]{1,0:T(8,128)}, bf16[576,1024]{1,0:T(8,128)(2,1)}) custom-call(s32[1]{0:T(128)} %bitcast.4.flags_ref, bf16[136,1152]{1,0:T(8,128)(2,1)S(1)} %pad_maximum_fusion.4.refs_0_, bf16[136,1152]{1,0:T(8,128)(2,1)S(1)} %collective-permute-done.1.refs_1_, ...), custom_call_target="tpu_custom_call" | custom-call | flops 5435817984 | bytes 11796480 | tf_op jit(solution)/shard_map/pallas_call | solution.py:197
  65.0 1.2 %collective-permute-start.18 = (bf16[256,1152]{1,0:T(8,128)(2,1)S(1)}, bf16[256,1152]{1,0:T(8,128)(2,1)S(1)}, u32[]{:S(2)}, u32[]{:S(2)}) collective-permute-start(bf16[256,1152]{1,0:T(8,128)(2,1)S(1)} %pad_maximum_fusion.2.refs_0_), channel_id=1, source_target_pairs={{0,1},{1,0},{2,3},{3,2},{4,5},{5,4},{6,7},{7,6},{8,9},{9,8},{10,11... | collective-permute-start | bytes 1769480 | tf_op jit(solution)/shard_map/ppermute | solution.py:108
  66.2 1.1 %collective-permute-start.19 = (bf16[256,1152]{1,0:T(8,128)(2,1)S(1)}, bf16[256,1152]{1,0:T(8,128)(2,1)S(1)}, u32[]{:S(2)}, u32[]{:S(2)}) collective-permute-start(bf16[256,1152]{1,0:T(8,128)(2,1)S(1)} %pad_maximum_fusion.3.refs_2_), channel_id=1, source_target_pairs={{0,4},{2,6},{4,0},{6,2},{8,12},{10,14},{12,8},{14,10},{16,20},{18,... | collective-permute-start | bytes 1769480 | tf_op jit(solution)/shard_map/ppermute | solution.py:108
  67.3 10.7 %shard_map.132 = (f32[1024,1152]{1,0:T(8,128)}, f32[8,128]{1,0:T(8,128)}) custom-call(f32[3]{0:T(128)S(1)} %pad_maximum_fusion.9.knobs_ref, s32[4]{0:T(128)S(1)} %pad_add_fusion.1.offsets_ref, bf16[1024,1152]{1,0:T(8,128)(2,1)} %get-tuple-element.53.embed_ref, s32[1024,1]{1,0:T(8,128)} %get-tuple-element.57.caption_ref, ...), custom_call_target="tpu_custom_call" | custom-call | flops 9663676416 | bytes 9437184 | tf_op jit(solution)/shard_map/pallas_call | solution.py:310
  78.0 2.3 %collective-permute-done.18.refs_0_ = bf16[256,1152]{1,0:T(8,128)(2,1)S(1)} collective-permute-done((bf16[256,1152]{1,0:T(8,128)(2,1)S(1)}, bf16[256,1152]{1,0:T(8,128)(2,1)S(1)}, u32[]{:S(2)}, u32[]{:S(2)}) %collective-permute-start.18) | collective-permute-done | bytes 589856 | tf_op jit(solution)/shard_map/ppermute | solution.py:108
  80.3 0.9 collective-permute-done.19.refs_2_
  81.8 1.4 %collective-permute-done.20.refs_1_ = bf16[256,1152]{1,0:T(8,128)(2,1)S(1)} collective-permute-done((bf16[256,1152]{1,0:T(8,128)(2,1)S(1)}, bf16[256,1152]{1,0:T(8,128)(2,1)S(1)}, u32[]{:S(2)}, u32[]{:S(2)}) %collective-permute-start.20) | collective-permute-done | bytes 589856 | tf_op jit(solution)/shard_map/ppermute | solution.py:108
  83.2 0.8 collective-permute-done.21.refs_3_
  84.7 14.6 %shard_map.133 = (f32[576,1152]{1,0:T(8,128)S(1)}, f32[8,128]{1,0:T(8,128)S(1)}) custom-call(f32[3]{0:T(128)S(1)} %pad_maximum_fusion.9.knobs_ref, s32[4]{0:T(128)S(1)} %pad_add_fusion.offsets_ref, bf16[1024,1152]{1,0:T(8,128)(2,1)} %get-tuple-element.53.embed_ref, s32[1024,1]{1,0:T(8,128)} %get-tuple-element.57.caption_ref, ...), custom_call_target="tpu_custom_call" | custom-call | flops 15099494400 | bytes 18874368 | tf_op jit(solution)/shard_map/pallas_call | solution.py:330
  99.9 4.5 %collective-permute-done.23 = f32[8,128]{1,0:T(8,128)S(1)} collective-permute-done((f32[8,128]{1,0:T(8,128)S(1)}, f32[8,128]{1,0:T(8,128)S(1)}, u32[]{:S(2)}, u32[]{:S(2)}) %collective-permute-start.23) | collective-permute-done | bytes 4128 | tf_op jit(solution)/shard_map/ppermute | solution.py:108
  105.6 1.3 %add_convert_fusion = bf16[576,1152]{1,0:T(8,128)(2,1)} fusion(f32[576,1152]{1,0:T(8,128)S(1)} %get-tuple-element.68, f32[576,1152]{1,0:T(8,128)S(1)} %collective-permute-done.22), kind=kLoop, calls=%fused_computation.1 | loop fusion | flops 1327104 | bytes 6635520 | tf_op jit(solution)/shard_map/convert_element_type | solution.py:463
  (74 shorter events, 8.4 us)
Async XLA Ops:
  0.6 4.3 %copy-start.8 = (s32[128]{0:T(128)S(1)}, s32[128]{0:T(128)}, u32[]{:S(2)}) copy-start(s32[128]{0:T(128)} %param.14) | copy-start | bytes 1540
  0.6 4.3 %copy-start.3 = (bf16[128,1152]{1,0:T(8,128)(2,1)S(1)}, bf16[128,1152]{1,0:T(8,128)(2,1)}, u32[]{:S(2)}) copy-start(bf16[128,1152]{1,0:T(8,128)(2,1)} %param.12) | copy-start | bytes 884740
  0.7 4.6 %copy-start.6 = (f32[1152]{0:T(1024)S(1)}, f32[1152]{0:T(1024)}, u32[]{:S(2)}) copy-start(f32[1152]{0:T(1024)} %param.15) | copy-start | bytes 13828
  0.7 4.9 %copy-start.5 = (bf16[128,1152]{1,0:T(8,128)(2,1)S(1)}, bf16[128,1152]{1,0:T(8,128)(2,1)}, u32[]{:S(2)}) copy-start(bf16[128,1152]{1,0:T(8,128)(2,1)} %param.13) | copy-start | bytes 884740
  1.9 17.9 %collective-permute-start = (bf16[288,1152]{1,0:T(8,128)(2,1)S(1)}, bf16[288,1152]{1,0:T(8,128)(2,1)S(1)}, u32[]{:S(2)}, u32[]{:S(2)}) collective-permute-start(bf16[288,1152]{1,0:T(8,128)(2,1)S(1)} %constant_dynamic-slice_fusion), channel_id=1, source_target_pairs={{0,1},{1,0},{2,3},{3,2},{4,5},{5,4},{6,7},{7,6},{8,9},{9,8},{10,11... | collective-permute-start | bytes 1990664 | tf_op jit(solution)/shard_map/ppermute | solution.py:108
  5.6 11.8 %copy-start.7 = (f32[1152]{0:T(1024)S(1)}, f32[1152]{0:T(1024)}, u32[]{:S(2)}) copy-start(f32[1152]{0:T(1024)} %param.16) | copy-start | bytes 13828
  5.6 17.4 %collective-permute-start.2 = (bf16[136,1152]{1,0:T(8,128)(2,1)S(1)}, bf16[136,1152]{1,0:T(8,128)(2,1)S(1)}, u32[]{:S(2)}, u32[]{:S(2)}) collective-permute-start(bf16[136,1152]{1,0:T(8,128)(2,1)S(1)} %pad_maximum_fusion.4.refs_0_), channel_id=1, source_target_pairs={{0,16},{2,18},{4,20},{6,22},{8,24},{10,26},{12,28},{14,30},{16,0},... | collective-permute-start | bytes 940040 | tf_op jit(solution)/shard_map/ppermute | solution.py:108
  8.2 14.2 %collective-permute-start.1 = (bf16[136,1152]{1,0:T(8,128)(2,1)S(1)}, bf16[136,1152]{1,0:T(8,128)(2,1)S(1)}, u32[]{:S(2)}, u32[]{:S(2)}) collective-permute-start(bf16[136,1152]{1,0:T(8,128)(2,1)S(1)} %pad_maximum_fusion.4.refs_0_), channel_id=1, source_target_pairs={{0,8},{2,10},{4,12},{6,14},{8,0},{10,2},{12,4},{14,6},{16,24},{18,... | collective-permute-start | bytes 940040 | tf_op jit(solution)/shard_map/ppermute | solution.py:108
  22.5 6.8 %collective-permute-start.3 = (f32[64,1152]{1,0:T(8,128)S(1)}, f32[64,1152]{1,0:T(8,128)S(1)}, u32[]{:S(2)}, u32[]{:S(2)}) collective-permute-start(f32[64,1152]{1,0:T(8,128)S(1)} %slice_select_fusion), channel_id=1, source_target_pairs={{0,1},{1,0},{2,3},{3,2},{4,5},{5,4},{6,7},{7,6},{8,9},{9,8},{10,11... | collective-permute-start | bytes 884744 | tf_op jit(solution)/shard_map/ppermute | solution.py:108
  23.1 7.5 %collective-permute-start.5 = (bf16[136,1152]{1,0:T(8,128)(2,1)S(1)}, bf16[136,1152]{1,0:T(8,128)(2,1)S(1)}, u32[]{:S(2)}, u32[]{:S(2)}) collective-permute-start(bf16[136,1152]{1,0:T(8,128)(2,1)S(1)} %broadcast_select_fusion.5), channel_id=1, source_target_pairs={{0,4},{2,6},{4,0},{6,2},{8,12},{10,14},{12,8},{14,10},{16,20},{18,... | collective-permute-start | bytes 940040 | tf_op jit(solution)/shard_map/ppermute | solution.py:108
  24.7 7.1 %collective-permute-start.4 = (bf16[136,1152]{1,0:T(8,128)(2,1)S(1)}, bf16[136,1152]{1,0:T(8,128)(2,1)S(1)}, u32[]{:S(2)}, u32[]{:S(2)}) collective-permute-start(bf16[136,1152]{1,0:T(8,128)(2,1)S(1)} %collective-permute-done.2.refs_2_), channel_id=1, source_target_pairs={{0,8},{2,10},{4,12},{6,14},{8,0},{10,2},{12,4},{14,6},{16,24},{18,... | collective-permute-start | bytes 940040 | tf_op jit(solution)/shard_map/ppermute | solution.py:108
  26.1 21.9 %collective-permute-start.13 = (bf16[288,1152]{1,0:T(8,128)(2,1)S(1)}, bf16[288,1152]{1,0:T(8,128)(2,1)S(1)}, u32[]{:S(2)}, u32[]{:S(2)}) collective-permute-start(bf16[288,1152]{1,0:T(8,128)(2,1)S(1)} %collective-permute-done), channel_id=1, source_target_pairs={{0,2},{2,0},{4,6},{6,4},{8,10},{10,8},{12,14},{14,12},{16,18},{18,... | collective-permute-start | bytes 1990664 | tf_op jit(solution)/shard_map/ppermute | solution.py:108
  31.8 6.0 %collective-permute-start.7 = (bf16[32,1152]{1,0:T(8,128)(2,1)S(1)}, bf16[32,1152]{1,0:T(8,128)(2,1)S(1)}, u32[]{:S(2)}, u32[]{:S(2)}) collective-permute-start(bf16[32,1152]{1,0:T(8,128)(2,1)S(1)} %get-tuple-element.92), channel_id=1, source_target_pairs={{0,1},{1,0},{2,3},{3,2},{4,5},{5,4},{6,7},{7,6},{8,9},{9,8},{10,11... | collective-permute-start | bytes 221192 | tf_op jit(solution)/shard_map/ppermute | solution.py:108
  33.4 5.3 %collective-permute-start.6 = (bf16[32,1152]{1,0:T(8,128)(2,1)S(1)}, bf16[32,1152]{1,0:T(8,128)(2,1)S(1)}, u32[]{:S(2)}, u32[]{:S(2)}) collective-permute-start(bf16[32,1152]{1,0:T(8,128)(2,1)S(1)} %get-tuple-element.93), channel_id=1, source_target_pairs={{0,16},{2,18},{4,20},{6,22},{8,24},{10,26},{12,28},{14,30},{16,0},... | collective-permute-start | bytes 221192 | tf_op jit(solution)/shard_map/ppermute | solution.py:108
  35.8 7.5 %collective-permute-start.8 = (bf16[136,1152]{1,0:T(8,128)(2,1)S(1)}, bf16[136,1152]{1,0:T(8,128)(2,1)S(1)}, u32[]{:S(2)}, u32[]{:S(2)}) collective-permute-start(bf16[136,1152]{1,0:T(8,128)(2,1)S(1)} %broadcast_select_fusion.4), channel_id=1, source_target_pairs={{0,4},{2,6},{4,0},{6,2},{8,12},{10,14},{12,8},{14,10},{16,20},{18,... | collective-permute-start | bytes 940040 | tf_op jit(solution)/shard_map/ppermute | solution.py:108
  36.3 7.2 %collective-permute-start.9 = (bf16[136,1152]{1,0:T(8,128)(2,1)S(1)}, bf16[136,1152]{1,0:T(8,128)(2,1)S(1)}, u32[]{:S(2)}, u32[]{:S(2)}) collective-permute-start(bf16[136,1152]{1,0:T(8,128)(2,1)S(1)} %collective-permute-done.5.refs_4_), channel_id=1, source_target_pairs={{0,1},{1,0},{2,3},{3,2},{4,5},{5,4},{6,7},{7,6},{8,9},{9,8},{10,11... | collective-permute-start | bytes 940040 | tf_op jit(solution)/shard_map/ppermute | solution.py:108
  43.5 4.7 %copy-start.4 = (bf16[576,1152]{1,0:T(8,128)(2,1)S(1)}, bf16[576,1152]{1,0:T(8,128)(2,1)}, u32[]{:S(2)}) copy-start(bf16[576,1152]{1,0:T(8,128)(2,1)} %param.19) | copy-start | bytes 3981316
  43.5 9.3 %collective-permute-start.10 = (bf16[64,1152]{1,0:T(8,128)(2,1)S(1)}, bf16[64,1152]{1,0:T(8,128)(2,1)S(1)}, u32[]{:S(2)}, u32[]{:S(2)}) collective-permute-start(bf16[64,1152]{1,0:T(8,128)(2,1)S(1)} %get-tuple-element.48), channel_id=1, source_target_pairs={{0,8},{2,10},{4,12},{6,14},{8,0},{10,2},{12,4},{14,6},{16,24},{18,... | collective-permute-start | bytes 442376 | tf_op jit(solution)/shard_map/ppermute | solution.py:108
  45.5 7.3 %collective-permute-start.11 = (bf16[64,1152]{1,0:T(8,128)(2,1)S(1)}, bf16[64,1152]{1,0:T(8,128)(2,1)S(1)}, u32[]{:S(2)}, u32[]{:S(2)}) collective-permute-start(bf16[64,1152]{1,0:T(8,128)(2,1)S(1)} %get-tuple-element.49), channel_id=1, source_target_pairs={{0,16},{2,18},{4,20},{6,22},{8,24},{10,26},{12,28},{14,30},{16,0},... | collective-permute-start | bytes 442376 | tf_op jit(solution)/shard_map/ppermute | solution.py:108
  46.7 6.9 %collective-permute-start.12 = (bf16[136,1152]{1,0:T(8,128)(2,1)S(1)}, bf16[136,1152]{1,0:T(8,128)(2,1)S(1)}, u32[]{:S(2)}, u32[]{:S(2)}) collective-permute-start(bf16[136,1152]{1,0:T(8,128)(2,1)S(1)} %collective-permute-done.8.refs_5_), channel_id=1, source_target_pairs={{0,1},{1,0},{2,3},{3,2},{4,5},{5,4},{6,7},{7,6},{8,9},{9,8},{10,11... | collective-permute-start | bytes 940040 | tf_op jit(solution)/shard_map/ppermute | solution.py:108
  53.6 9.1 %collective-permute-start.14 = (bf16[128,1152]{1,0:T(8,128)(2,1)S(1)}, bf16[128,1152]{1,0:T(8,128)(2,1)S(1)}, u32[]{:S(2)}, u32[]{:S(2)}) collective-permute-start(bf16[128,1152]{1,0:T(8,128)(2,1)S(1)} %pad_maximum_fusion.5), channel_id=1, source_target_pairs={{0,4},{2,6},{4,0},{6,2},{8,12},{10,14},{12,8},{14,10},{16,20},{18,... | collective-permute-start | bytes 884744 | tf_op jit(solution)/shard_map/ppermute | solution.py:108
  54.9 7.9 %collective-permute-start.15 = (bf16[128,1152]{1,0:T(8,128)(2,1)S(1)}, bf16[128,1152]{1,0:T(8,128)(2,1)S(1)}, u32[]{:S(2)}, u32[]{:S(2)}) collective-permute-start(bf16[128,1152]{1,0:T(8,128)(2,1)S(1)} %pad_maximum_fusion.6), channel_id=1, source_target_pairs={{0,8},{2,10},{4,12},{6,14},{8,0},{10,2},{12,4},{14,6},{16,24},{18,... | collective-permute-start | bytes 884744 | tf_op jit(solution)/shard_map/ppermute | solution.py:108
  62.8 4.5 %copy-start = (s32[1,256]{1,0:T(1,128)S(1)}, s32[1,256]{1,0:T(1,128)}, u32[]{:S(2)}) copy-start(s32[1,256]{1,0:T(1,128)} %constant.84.clone.refs_6_.refs_7_) | copy-start | bytes 3076
  62.8 4.5 %copy-start.1 = (s32[1,256]{1,0:T(1,128)S(1)}, s32[1,256]{1,0:T(1,128)}, u32[]{:S(2)}) copy-start(s32[1,256]{1,0:T(1,128)} %constant.83.clone.refs_4_.refs_5_) | copy-start | bytes 3076
  63.0 4.3 %collective-permute-start.16 = (bf16[256,1152]{1,0:T(8,128)(2,1)S(1)}, bf16[256,1152]{1,0:T(8,128)(2,1)S(1)}, u32[]{:S(2)}, u32[]{:S(2)}) collective-permute-start(bf16[256,1152]{1,0:T(8,128)(2,1)S(1)} %pad_maximum_fusion.2.refs_0_), channel_id=1, source_target_pairs={{0,2},{2,0},{4,6},{6,4},{8,10},{10,8},{12,14},{14,12},{16,18},{18,... | collective-permute-start | bytes 1769480 | tf_op jit(solution)/shard_map/ppermute | solution.py:108
  63.1 4.2 %collective-permute-start.17 = (bf16[256,1152]{1,0:T(8,128)(2,1)S(1)}, bf16[256,1152]{1,0:T(8,128)(2,1)S(1)}, u32[]{:S(2)}, u32[]{:S(2)}) collective-permute-start(bf16[256,1152]{1,0:T(8,128)(2,1)S(1)} %pad_maximum_fusion.3.refs_2_), channel_id=1, source_target_pairs={{0,2},{2,0},{4,6},{6,4},{8,10},{10,8},{12,14},{14,12},{16,18},{18,... | collective-permute-start | bytes 1769480 | tf_op jit(solution)/shard_map/ppermute | solution.py:108
  65.0 15.3 %collective-permute-start.18 = (bf16[256,1152]{1,0:T(8,128)(2,1)S(1)}, bf16[256,1152]{1,0:T(8,128)(2,1)S(1)}, u32[]{:S(2)}, u32[]{:S(2)}) collective-permute-start(bf16[256,1152]{1,0:T(8,128)(2,1)S(1)} %pad_maximum_fusion.2.refs_0_), channel_id=1, source_target_pairs={{0,1},{1,0},{2,3},{3,2},{4,5},{5,4},{6,7},{7,6},{8,9},{9,8},{10,11... | collective-permute-start | bytes 1769480 | tf_op jit(solution)/shard_map/ppermute | solution.py:108
  66.2 15.0 %collective-permute-start.19 = (bf16[256,1152]{1,0:T(8,128)(2,1)S(1)}, bf16[256,1152]{1,0:T(8,128)(2,1)S(1)}, u32[]{:S(2)}, u32[]{:S(2)}) collective-permute-start(bf16[256,1152]{1,0:T(8,128)(2,1)S(1)} %pad_maximum_fusion.3.refs_2_), channel_id=1, source_target_pairs={{0,4},{2,6},{4,0},{6,2},{8,12},{10,14},{12,8},{14,10},{16,20},{18,... | collective-permute-start | bytes 1769480 | tf_op jit(solution)/shard_map/ppermute | solution.py:108
  81.2 2.0 %collective-permute-start.20 = (bf16[256,1152]{1,0:T(8,128)(2,1)S(1)}, bf16[256,1152]{1,0:T(8,128)(2,1)S(1)}, u32[]{:S(2)}, u32[]{:S(2)}) collective-permute-start(bf16[256,1152]{1,0:T(8,128)(2,1)S(1)} %collective-permute-done.18.refs_0_), channel_id=1, source_target_pairs={{0,2},{2,0},{4,6},{6,4},{8,10},{10,8},{12,14},{14,12},{16,18},{18,... | collective-permute-start | bytes 1769480 | tf_op jit(solution)/shard_map/ppermute | solution.py:108
  81.2 2.8 %collective-permute-start.21 = (bf16[256,1152]{1,0:T(8,128)(2,1)S(1)}, bf16[256,1152]{1,0:T(8,128)(2,1)S(1)}, u32[]{:S(2)}, u32[]{:S(2)}) collective-permute-start(bf16[256,1152]{1,0:T(8,128)(2,1)S(1)} %collective-permute-done.19.refs_2_), channel_id=1, source_target_pairs={{0,2},{2,0},{4,6},{6,4},{8,10},{10,8},{12,14},{14,12},{16,18},{18,... | collective-permute-start | bytes 1769480 | tf_op jit(solution)/shard_map/ppermute | solution.py:108
  99.4 6.2 %collective-permute-start.22 = (f32[576,1152]{1,0:T(8,128)S(1)}, f32[576,1152]{1,0:T(8,128)S(1)}, u32[]{:S(2)}, u32[]{:S(2)}) collective-permute-start(f32[576,1152]{1,0:T(8,128)S(1)} %get-tuple-element.68), channel_id=1, source_target_pairs={{0,2},{2,0},{4,6},{6,4},{8,10},{10,8},{12,14},{14,12},{16,18},{18,... | collective-permute-start | bytes 7962632 | tf_op jit(solution)/shard_map/ppermute | solution.py:108
  99.6 4.8 %collective-permute-start.23 = (f32[8,128]{1,0:T(8,128)S(1)}, f32[8,128]{1,0:T(8,128)S(1)}, u32[]{:S(2)}, u32[]{:S(2)}) collective-permute-start(f32[8,128]{1,0:T(8,128)S(1)} %get-tuple-element.69), channel_id=1, source_target_pairs={{0,2},{2,0},{4,6},{6,4},{8,10},{10,8},{12,14},{14,12},{16,18},{18,... | collective-permute-start | bytes 12296 | tf_op jit(solution)/shard_map/ppermute | solution.py:108
  (1 other events, 0.7 us)

commit v5 on v4

--- a/solution.py
+++ b/solution.py
@@ -396,7 +396,6 @@
     ).astype(jnp.bfloat16)
     branch = jnp.dot(hidden, mlp_down, preferred_element_type=jnp.float32)
     branch, piece = lax.optimization_barrier((branch, piece))
-    branch, from_low = lax.optimization_barrier((branch, from_low))
     from_both = swap(from_high, "dp", Z_LOW)
     near_0 = swap(jnp.where(own_x, from_high, packed), "dp", Y)
     arrived = swap_x(half_of(branch, ~own_x, half_rows))
@@ -407,7 +406,7 @@
         feature * lax.rsqrt(jnp.sum(feature * feature, axis=-1, keepdims=True) + EPS)
     ).astype(jnp.bfloat16)
 
-    image_unit, from_both, near_0 = lax.optimization_barrier((image_unit, from_both, near_0))
+    image_unit, from_both, near_0, from_low = lax.optimization_barrier((image_unit, from_both, near_0, from_low))
     near_1 = swap(jnp.where(own_x, from_both, from_low), "dp", Y)
     far_0 = swap_x(near_0)
     other_adapter = join(piece, swap_core(piece), own_c)
@@ -415,9 +414,11 @@
 
     image_a = image_unit[:quarter]
     image_b = image_unit[quarter:]
-    image_a = grow(image_a, Z_HIGH)
-    image_b = join(image_b, swap_x(image_b), own_x)
+    other_a = swap(image_a, "dp", Z_HIGH)
+    other_b = swap_x(image_b)
     image_a, image_b, near_1, far_0 = lax.optimization_barrier((image_a, image_b, near_1, far_0))
+    image_a = join(image_a, other_a, bit_of(dp, Z_HIGH))
+    image_b = join(image_b, other_b, own_x)
     far_1 = swap_x(near_1)
     image_a = grow(image_a, Z_LOW)
     image_b = grow(image_b, Z_HIGH)

time: 108 us -> 106 us (0.981)
  starting transfers between devices: 26.8 us -> 23.8 us
  other arithmetic: 3.81 us -> 4.96 us
    ppermute x24, starting transfers between devices: 26.8 us -> 23.8 us  [swap(): return lax.ppermute(values, axis, [(i, i ^ bit) for i in range(count)])]
    select_n x7, other arithmetic: 0.88 us -> 2.02 us  [join(): jnp.where(upper, other, mine)]
  transfers between devices with their start and end apart: 24 -> 24, of which waited for: 15 -> 16; matrix products, arithmetic and copies ran while one was open for 10% -> 11% of each run, Pallas kernels for 17% -> 17%
where the time goes in v5:
time: 106 us; the launch traced here: 105 us
  Pallas kernels  32.9 us (31%)
  waiting for transfers between devices  29.6 us (28%)
  starting transfers between devices  23.8 us (22%)
  matrix products  7.49 us (7%)
  other arithmetic  4.96 us (5%)
  between operations  4.04 us (4%)
  local copies, waits for them, and re-layouts  2.45 us (2%)
    ppermute x24, waiting for transfers between devices, swap(): return lax.ppermute(values, axis, [(i, i ^ bit) for i in range(count)])  29.6 us
    ppermute x24, starting transfers between devices, swap(): return lax.ppermute(values, axis, [(i, i ^ bit) for i in range(count)])  23.8 us
    pallas_call x1, Pallas kernels, late_scores(): pl.pallas_call(functools.partial(late_kernel, len(images)), grid=(count /...  14.6 us
    pallas_call x1, Pallas kernels, early_scores(): pl.pallas_call(functools.partial(early_kernel, len(images)), grid=(count...  10.7 us
    pallas_call x1, Pallas kernels, text_side(): pl.pallas_call(text_kernel, grid=(4,), in_specs=[SMEM] + [whole_spec(piec...  7.61 us
    dot_general x1, matrix products, slice_plan(): branch = jnp.dot(hidden, mlp_down, preferred_element_type=jnp.float32)  7.49 us
  transfers between devices with their start and end apart: 24, of which 16 were waited for; matrix products, arithmetic and copies ran while one was open for 11% of the time, Pallas kernels for 17%

profile of v5, /device:TPU:0, one launch (start us, length us, event | category | flops | bytes accessed | tf_op | source)
XLA Modules:
  0.0 105.2 jit_solution(10321425583585044394)
XLA Ops:
  0.7 1.2 %constant_dynamic-slice_fusion = bf16[288,1152]{1,0:T(8,128)(2,1)S(1)} fusion(bf16[576,1152]{1,0:T(8,128)(2,1)} %param.19, s32[]{:T(128)S(6)} %select_n.135), kind=kLoop, calls=%fused_computation.75 | loop fusion | bytes 1327108 | tf_op jit(solution)/shard_map/dynamic_slice | solution.py:386
  1.9 3.0 %collective-permute-start = (bf16[288,1152]{1,0:T(8,128)(2,1)S(1)}, bf16[288,1152]{1,0:T(8,128)(2,1)}, u32[]{:S(2)}, u32[]{:S(2)}) collective-permute-start(bf16[288,1152]{1,0:T(8,128)(2,1)S(1)} %constant_dynamic-slice_fusion), channel_id=1, source_target_pairs={{0,1},{1,0},{2,3},{3,2},{4,5},{5,4},{6,7},{7,6},{8,9},{9,8},{10,11... | collective-permute-start | bytes 1990664 | tf_op jit(solution)/shard_map/ppermute | solution.py:108
  5.6 1.6 %collective-permute-start.5 = (bf16[136,1152]{1,0:T(8,128)(2,1)S(1)}, bf16[136,1152]{1,0:T(8,128)(2,1)S(1)}, u32[]{:S(2)}, u32[]{:S(2)}) collective-permute-start(bf16[136,1152]{1,0:T(8,128)(2,1)S(1)} %pad_maximum_fusion.4.refs_0_), channel_id=1, source_target_pairs={{0,8},{2,10},{4,12},{6,14},{8,0},{10,2},{12,4},{14,6},{16,24},{18,... | collective-permute-start | bytes 940040 | tf_op jit(solution)/shard_map/ppermute | solution.py:108
  7.2 2.6 %collective-permute-start.2 = (bf16[136,1152]{1,0:T(8,128)(2,1)S(1)}, bf16[136,1152]{1,0:T(8,128)(2,1)S(1)}, u32[]{:S(2)}, u32[]{:S(2)}) collective-permute-start(bf16[136,1152]{1,0:T(8,128)(2,1)S(1)} %pad_maximum_fusion.4.refs_0_), channel_id=1, source_target_pairs={{0,16},{2,18},{4,20},{6,22},{8,24},{10,26},{12,28},{14,30},{16,0},... | collective-permute-start | bytes 940040 | tf_op jit(solution)/shard_map/ppermute | solution.py:108
  9.8 7.5 %fusion.13 = f32[128,1152]{1,0:T(8,128)S(1)} fusion(bf16[2152,1152]{1,0:T(8,128)(2,1)} %param.18, bf16[128,1152]{1,0:T(8,128)(2,1)S(1)} %fusion.12, bf16[1152,2152]{0,1:T(8,128)(2,1)} %param.17), kind=kOutput, calls=%fused_computation.25 | convolution fusion | flops 1271780352 | bytes 10801152 | tf_op jit(solution)/shard_map/dot_general | solution.py:397
  17.3 2.6 %collective-permute-done = bf16[288,1152]{1,0:T(8,128)(2,1)} collective-permute-done((bf16[288,1152]{1,0:T(8,128)(2,1)S(1)}, bf16[288,1152]{1,0:T(8,128)(2,1)}, u32[]{:S(2)}, u32[]{:S(2)}) %collective-permute-start) | collective-permute-done | bytes 663584 | tf_op jit(solution)/shard_map/ppermute | solution.py:108
  19.9 1.8 %collective-permute-start.1 = (f32[64,1152]{1,0:T(8,128)S(1)}, f32[64,1152]{1,0:T(8,128)S(1)}, u32[]{:S(2)}, u32[]{:S(2)}) collective-permute-start(f32[64,1152]{1,0:T(8,128)S(1)} %slice_select_fusion), channel_id=1, source_target_pairs={{0,1},{1,0},{2,3},{3,2},{4,5},{5,4},{6,7},{7,6},{8,9},{9,8},{10,11... | collective-permute-start | bytes 884744 | tf_op jit(solution)/shard_map/ppermute | solution.py:108
  21.7 1.7 %collective-permute-done.2.refs_2_ = bf16[136,1152]{1,0:T(8,128)(2,1)S(1)} collective-permute-done((bf16[136,1152]{1,0:T(8,128)(2,1)S(1)}, bf16[136,1152]{1,0:T(8,128)(2,1)S(1)}, u32[]{:S(2)}, u32[]{:S(2)}) %collective-permute-start.2) | collective-permute-done | bytes 313376 | tf_op jit(solution)/shard_map/ppermute | solution.py:108
  23.5 1.6 %collective-permute-start.4 = (bf16[136,1152]{1,0:T(8,128)(2,1)S(1)}, bf16[136,1152]{1,0:T(8,128)(2,1)S(1)}, u32[]{:S(2)}, u32[]{:S(2)}) collective-permute-start(bf16[136,1152]{1,0:T(8,128)(2,1)S(1)} %broadcast_select_fusion.5), channel_id=1, source_target_pairs={{0,4},{2,6},{4,0},{6,2},{8,12},{10,14},{12,8},{14,10},{16,20},{18,... | collective-permute-start | bytes 940040 | tf_op jit(solution)/shard_map/ppermute | solution.py:108
  25.6 2.6 %collective-permute-done.1 = f32[64,1152]{1,0:T(8,128)S(1)} collective-permute-done((f32[64,1152]{1,0:T(8,128)S(1)}, f32[64,1152]{1,0:T(8,128)S(1)}, u32[]{:S(2)}, u32[]{:S(2)}) %collective-permute-start.1) | collective-permute-done | bytes 294944 | tf_op jit(solution)/shard_map/ppermute | solution.py:108
  28.5 2.0 %collective-permute-done.4.refs_4_ = bf16[136,1152]{1,0:T(8,128)(2,1)S(1)} collective-permute-done((bf16[136,1152]{1,0:T(8,128)(2,1)S(1)}, bf16[136,1152]{1,0:T(8,128)(2,1)S(1)}, u32[]{:S(2)}, u32[]{:S(2)}) %collective-permute-start.4) | collective-permute-done | bytes 313376 | tf_op jit(solution)/shard_map/ppermute | solution.py:108
  30.5 1.5 %collective-permute-done.3.refs_3_ = bf16[136,1152]{1,0:T(8,128)(2,1)S(1)} collective-permute-done((bf16[136,1152]{1,0:T(8,128)(2,1)S(1)}, bf16[136,1152]{1,0:T(8,128)(2,1)S(1)}, u32[]{:S(2)}, u32[]{:S(2)}) %collective-permute-start.3) | collective-permute-done | bytes 313376 | tf_op jit(solution)/shard_map/ppermute | solution.py:108
  33.2 1.6 %collective-permute-start.10 = (bf16[32,1152]{1,0:T(8,128)(2,1)S(1)}, bf16[32,1152]{1,0:T(8,128)(2,1)S(1)}, u32[]{:S(2)}, u32[]{:S(2)}) collective-permute-start(bf16[32,1152]{1,0:T(8,128)(2,1)S(1)} %get-tuple-element.47), channel_id=1, source_target_pairs={{0,1},{1,0},{2,3},{3,2},{4,5},{5,4},{6,7},{7,6},{8,9},{9,8},{10,11... | collective-permute-start | bytes 221192 | tf_op jit(solution)/shard_map/ppermute | solution.py:108
  34.8 1.6 %collective-permute-start.8 = (bf16[32,1152]{1,0:T(8,128)(2,1)S(1)}, bf16[32,1152]{1,0:T(8,128)(2,1)S(1)}, u32[]{:S(2)}, u32[]{:S(2)}) collective-permute-start(bf16[32,1152]{1,0:T(8,128)(2,1)S(1)} %get-tuple-element.46), channel_id=1, source_target_pairs={{0,16},{2,18},{4,20},{6,22},{8,24},{10,26},{12,28},{14,30},{16,0},... | collective-permute-start | bytes 221192 | tf_op jit(solution)/shard_map/ppermute | solution.py:108
  36.4 2.6 %collective-permute-done.6.refs_5_ = bf16[136,1152]{1,0:T(8,128)(2,1)S(1)} collective-permute-done((bf16[136,1152]{1,0:T(8,128)(2,1)S(1)}, bf16[136,1152]{1,0:T(8,128)(2,1)S(1)}, u32[]{:S(2)}, u32[]{:S(2)}) %collective-permute-start.6) | collective-permute-done | bytes 313376 | tf_op jit(solution)/shard_map/ppermute | solution.py:108
  39.6 0.8 collective-permute-done.10
  41.0 1.0 collective-permute-start.9
  42.0 2.2 %collective-permute-start.11 = (bf16[64,1152]{1,0:T(8,128)(2,1)S(1)}, bf16[64,1152]{1,0:T(8,128)(2,1)S(1)}, u32[]{:S(2)}, u32[]{:S(2)}) collective-permute-start(bf16[64,1152]{1,0:T(8,128)(2,1)S(1)} %pad_maximum_fusion.8), channel_id=1, source_target_pairs={{0,16},{2,18},{4,20},{6,22},{8,24},{10,26},{12,28},{14,30},{16,0},... | collective-permute-start | bytes 442376 | tf_op jit(solution)/shard_map/ppermute | solution.py:108
  44.8 1.2 %broadcast_select_fusion.3 = (bf16[288,1152]{1,0:T(8,128)(2,1)S(1)}, bf16[288,1152]{1,0:T(8,128)(2,1)S(1)}) fusion(bf16[288,1152]{1,0:T(8,128)(2,1)S(1)} %collective-permute-done.13, bf16[288,1152]{1,0:T(8,128)(2,1)} %collective-permute-done, pred[]{:T(512)S(6)} %ne.43), kind=kLoop, calls=%fused_computation.19 | loop fusion | flops 663552 | bytes 2654209 | tf_op jit(solution)/shard_map/jit(_where)/select_n | solution.py:120
  46.8 3.0 %collective-permute-done.11 = bf16[64,1152]{1,0:T(8,128)(2,1)S(1)} collective-permute-done((bf16[64,1152]{1,0:T(8,128)(2,1)S(1)}, bf16[64,1152]{1,0:T(8,128)(2,1)S(1)}, u32[]{:S(2)}, u32[]{:S(2)}) %collective-permute-start.11) | collective-permute-done | bytes 147488 | tf_op jit(solution)/shard_map/ppermute | solution.py:108
  50.0 1.2 %collective-permute-done.12.refs_7_ = bf16[136,1152]{1,0:T(8,128)(2,1)S(1)} collective-permute-done((bf16[136,1152]{1,0:T(8,128)(2,1)S(1)}, bf16[136,1152]{1,0:T(8,128)(2,1)S(1)}, u32[]{:S(2)}, u32[]{:S(2)}) %collective-permute-start.12) | collective-permute-done | bytes 313376 | tf_op jit(solution)/shard_map/ppermute | solution.py:108
  51.2 1.5 %collective-permute-start.14 = (bf16[128,1152]{1,0:T(8,128)(2,1)S(1)}, bf16[128,1152]{1,0:T(8,128)(2,1)S(1)}, u32[]{:S(2)}, u32[]{:S(2)}) collective-permute-start(bf16[128,1152]{1,0:T(8,128)(2,1)S(1)} %pad_maximum_fusion.5), channel_id=1, source_target_pairs={{0,4},{2,6},{4,0},{6,2},{8,12},{10,14},{12,8},{14,10},{16,20},{18,... | collective-permute-start | bytes 884744 | tf_op jit(solution)/shard_map/ppermute | solution.py:108
  53.0 7.6 %shard_map.131 = (bf16[1024,1152]{1,0:T(8,128)(2,1)}, f32[1024,1152]{1,0:T(8,128)}, f32[1024,1]{1,0:T(8,128)}, s32[1024,1]{1,0:T(8,128)}, bf16[576,1024]{1,0:T(8,128)(2,1)}) custom-call(s32[1]{0:T(128)} %bitcast.4.flags_ref, bf16[136,1152]{1,0:T(8,128)(2,1)S(1)} %pad_maximum_fusion.4.refs_0_, bf16[136,1152]{1,0:T(8,128)(2,1)S(1)} %collective-permute-done.5.refs_1_, ...), custom_call_target="tpu_custom_call" | custom-call | flops 5435817984 | bytes 11796480 | tf_op jit(solution)/shard_map/pallas_call | solution.py:197
  63.4 0.7 collective-permute-start.19
  64.1 10.7 %shard_map.132 = (f32[1024,1152]{1,0:T(8,128)}, f32[8,128]{1,0:T(8,128)}) custom-call(f32[3]{0:T(128)S(1)} %pad_maximum_fusion.9.knobs_ref, s32[4]{0:T(128)S(1)} %pad_add_fusion.1.offsets_ref, bf16[1024,1152]{1,0:T(8,128)(2,1)} %get-tuple-element.51.embed_ref, s32[1024,1]{1,0:T(8,128)} %get-tuple-element.55.caption_ref, ...), custom_call_target="tpu_custom_call" | custom-call | flops 9663676416 | bytes 9437184 | tf_op jit(solution)/shard_map/pallas_call | solution.py:310
  74.8 3.4 %collective-permute-done.18.refs_0_ = bf16[256,1152]{1,0:T(8,128)(2,1)S(1)} collective-permute-done((bf16[256,1152]{1,0:T(8,128)(2,1)S(1)}, bf16[256,1152]{1,0:T(8,128)(2,1)S(1)}, u32[]{:S(2)}, u32[]{:S(2)}) %collective-permute-start.18) | collective-permute-done | bytes 589856 | tf_op jit(solution)/shard_map/ppermute | solution.py:108
  79.0 1.4 %collective-permute-done.20.refs_1_ = bf16[256,1152]{1,0:T(8,128)(2,1)S(1)} collective-permute-done((bf16[256,1152]{1,0:T(8,128)(2,1)S(1)}, bf16[256,1152]{1,0:T(8,128)(2,1)S(1)}, u32[]{:S(2)}, u32[]{:S(2)}) %collective-permute-start.20) | collective-permute-done | bytes 589856 | tf_op jit(solution)/shard_map/ppermute | solution.py:108
  80.4 0.8 collective-permute-done.21.refs_3_
  81.3 0.7 copy-done.2
  82.0 14.6 %shard_map.133 = (f32[576,1152]{1,0:T(8,128)S(1)}, f32[8,128]{1,0:T(8,128)S(1)}) custom-call(f32[3]{0:T(128)S(1)} %pad_maximum_fusion.9.knobs_ref, s32[4]{0:T(128)S(1)} %pad_add_fusion.offsets_ref, bf16[1024,1152]{1,0:T(8,128)(2,1)} %get-tuple-element.51.embed_ref, s32[1024,1]{1,0:T(8,128)} %get-tuple-element.55.caption_ref, ...), custom_call_target="tpu_custom_call" | custom-call | flops 15099494400 | bytes 18874368 | tf_op jit(solution)/shard_map/pallas_call | solution.py:330
  97.2 4.5 %collective-permute-done.23 = f32[8,128]{1,0:T(8,128)S(1)} collective-permute-done((f32[8,128]{1,0:T(8,128)S(1)}, f32[8,128]{1,0:T(8,128)S(1)}, u32[]{:S(2)}, u32[]{:S(2)}) %collective-permute-start.23) | collective-permute-done | bytes 4128 | tf_op jit(solution)/shard_map/ppermute | solution.py:108
  102.8 1.3 %add_convert_fusion = bf16[576,1152]{1,0:T(8,128)(2,1)} fusion(f32[576,1152]{1,0:T(8,128)S(1)} %get-tuple-element.66, f32[576,1152]{1,0:T(8,128)S(1)} %collective-permute-done.22), kind=kLoop, calls=%fused_computation.1 | loop fusion | flops 1327104 | bytes 6635520 | tf_op jit(solution)/shard_map/convert_element_type | solution.py:464
  (75 shorter events, 8.9 us)
Async XLA Ops:
  0.6 4.3 %copy-start.8 = (s32[128]{0:T(128)S(1)}, s32[128]{0:T(128)}, u32[]{:S(2)}) copy-start(s32[128]{0:T(128)} %param.14) | copy-start | bytes 1540
  0.6 4.3 %copy-start.3 = (bf16[128,1152]{1,0:T(8,128)(2,1)S(1)}, bf16[128,1152]{1,0:T(8,128)(2,1)}, u32[]{:S(2)}) copy-start(bf16[128,1152]{1,0:T(8,128)(2,1)} %param.12) | copy-start | bytes 884740
  0.7 4.6 %copy-start.6 = (f32[1152]{0:T(1024)S(1)}, f32[1152]{0:T(1024)}, u32[]{:S(2)}) copy-start(f32[1152]{0:T(1024)} %param.15) | copy-start | bytes 13828
  0.7 4.9 %copy-start.5 = (bf16[128,1152]{1,0:T(8,128)(2,1)S(1)}, bf16[128,1152]{1,0:T(8,128)(2,1)}, u32[]{:S(2)}) copy-start(bf16[128,1152]{1,0:T(8,128)(2,1)} %param.13) | copy-start | bytes 884740
  1.9 18.0 %collective-permute-start = (bf16[288,1152]{1,0:T(8,128)(2,1)S(1)}, bf16[288,1152]{1,0:T(8,128)(2,1)}, u32[]{:S(2)}, u32[]{:S(2)}) collective-permute-start(bf16[288,1152]{1,0:T(8,128)(2,1)S(1)} %constant_dynamic-slice_fusion), channel_id=1, source_target_pairs={{0,1},{1,0},{2,3},{3,2},{4,5},{5,4},{6,7},{7,6},{8,9},{9,8},{10,11... | collective-permute-start | bytes 1990664 | tf_op jit(solution)/shard_map/ppermute | solution.py:108
  5.6 22.9 %collective-permute-start.5 = (bf16[136,1152]{1,0:T(8,128)(2,1)S(1)}, bf16[136,1152]{1,0:T(8,128)(2,1)S(1)}, u32[]{:S(2)}, u32[]{:S(2)}) collective-permute-start(bf16[136,1152]{1,0:T(8,128)(2,1)S(1)} %pad_maximum_fusion.4.refs_0_), channel_id=1, source_target_pairs={{0,8},{2,10},{4,12},{6,14},{8,0},{10,2},{12,4},{14,6},{16,24},{18,... | collective-permute-start | bytes 940040 | tf_op jit(solution)/shard_map/ppermute | solution.py:108
  7.2 16.2 %collective-permute-start.2 = (bf16[136,1152]{1,0:T(8,128)(2,1)S(1)}, bf16[136,1152]{1,0:T(8,128)(2,1)S(1)}, u32[]{:S(2)}, u32[]{:S(2)}) collective-permute-start(bf16[136,1152]{1,0:T(8,128)(2,1)S(1)} %pad_maximum_fusion.4.refs_0_), channel_id=1, source_target_pairs={{0,16},{2,18},{4,20},{6,22},{8,24},{10,26},{12,28},{14,30},{16,0},... | collective-permute-start | bytes 940040 | tf_op jit(solution)/shard_map/ppermute | solution.py:108
  19.9 8.3 %collective-permute-start.1 = (f32[64,1152]{1,0:T(8,128)S(1)}, f32[64,1152]{1,0:T(8,128)S(1)}, u32[]{:S(2)}, u32[]{:S(2)}) collective-permute-start(f32[64,1152]{1,0:T(8,128)S(1)} %slice_select_fusion), channel_id=1, source_target_pairs={{0,1},{1,0},{2,3},{3,2},{4,5},{5,4},{6,7},{7,6},{8,9},{9,8},{10,11... | collective-permute-start | bytes 884744 | tf_op jit(solution)/shard_map/ppermute | solution.py:108
  23.5 12.9 %copy-start.7 = (f32[1152]{0:T(1024)S(1)}, f32[1152]{0:T(1024)}, u32[]{:S(2)}) copy-start(f32[1152]{0:T(1024)} %param.16) | copy-start | bytes 13828
  23.5 7.0 %collective-permute-start.4 = (bf16[136,1152]{1,0:T(8,128)(2,1)S(1)}, bf16[136,1152]{1,0:T(8,128)(2,1)S(1)}, u32[]{:S(2)}, u32[]{:S(2)}) collective-permute-start(bf16[136,1152]{1,0:T(8,128)(2,1)S(1)} %broadcast_select_fusion.5), channel_id=1, source_target_pairs={{0,4},{2,6},{4,0},{6,2},{8,12},{10,14},{12,8},{14,10},{16,20},{18,... | collective-permute-start | bytes 940040 | tf_op jit(solution)/shard_map/ppermute | solution.py:108
  25.1 6.9 %collective-permute-start.3 = (bf16[136,1152]{1,0:T(8,128)(2,1)S(1)}, bf16[136,1152]{1,0:T(8,128)(2,1)S(1)}, u32[]{:S(2)}, u32[]{:S(2)}) collective-permute-start(bf16[136,1152]{1,0:T(8,128)(2,1)S(1)} %collective-permute-done.2.refs_2_), channel_id=1, source_target_pairs={{0,8},{2,10},{4,12},{6,14},{8,0},{10,2},{12,4},{14,6},{16,24},{18,... | collective-permute-start | bytes 940040 | tf_op jit(solution)/shard_map/ppermute | solution.py:108
  32.1 7.0 %collective-permute-start.6 = (bf16[136,1152]{1,0:T(8,128)(2,1)S(1)}, bf16[136,1152]{1,0:T(8,128)(2,1)S(1)}, u32[]{:S(2)}, u32[]{:S(2)}) collective-permute-start(bf16[136,1152]{1,0:T(8,128)(2,1)S(1)} %broadcast_select_fusion.4), channel_id=1, source_target_pairs={{0,4},{2,6},{4,0},{6,2},{8,12},{10,14},{12,8},{14,10},{16,20},{18,... | collective-permute-start | bytes 940040 | tf_op jit(solution)/shard_map/ppermute | solution.py:108
  32.7 6.9 %collective-permute-start.7 = (bf16[136,1152]{1,0:T(8,128)(2,1)S(1)}, bf16[136,1152]{1,0:T(8,128)(2,1)S(1)}, u32[]{:S(2)}, u32[]{:S(2)}) collective-permute-start(bf16[136,1152]{1,0:T(8,128)(2,1)S(1)} %collective-permute-done.4.refs_4_), channel_id=1, source_target_pairs={{0,1},{1,0},{2,3},{3,2},{4,5},{5,4},{6,7},{7,6},{8,9},{9,8},{10,11... | collective-permute-start | bytes 940040 | tf_op jit(solution)/shard_map/ppermute | solution.py:108
  33.2 7.2 %collective-permute-start.10 = (bf16[32,1152]{1,0:T(8,128)(2,1)S(1)}, bf16[32,1152]{1,0:T(8,128)(2,1)S(1)}, u32[]{:S(2)}, u32[]{:S(2)}) collective-permute-start(bf16[32,1152]{1,0:T(8,128)(2,1)S(1)} %get-tuple-element.47), channel_id=1, source_target_pairs={{0,1},{1,0},{2,3},{3,2},{4,5},{5,4},{6,7},{7,6},{8,9},{9,8},{10,11... | collective-permute-start | bytes 221192 | tf_op jit(solution)/shard_map/ppermute | solution.py:108
  34.8 6.1 %collective-permute-start.8 = (bf16[32,1152]{1,0:T(8,128)(2,1)S(1)}, bf16[32,1152]{1,0:T(8,128)(2,1)S(1)}, u32[]{:S(2)}, u32[]{:S(2)}) collective-permute-start(bf16[32,1152]{1,0:T(8,128)(2,1)S(1)} %get-tuple-element.46), channel_id=1, source_target_pairs={{0,16},{2,18},{4,20},{6,22},{8,24},{10,26},{12,28},{14,30},{16,0},... | collective-permute-start | bytes 221192 | tf_op jit(solution)/shard_map/ppermute | solution.py:108
  36.4 8.4 %collective-permute-start.13 = (bf16[288,1152]{1,0:T(8,128)(2,1)}, bf16[288,1152]{1,0:T(8,128)(2,1)S(1)}, u32[]{:S(2)}, u32[]{:S(2)}) collective-permute-start(bf16[288,1152]{1,0:T(8,128)(2,1)} %collective-permute-done), channel_id=1, source_target_pairs={{0,2},{2,0},{4,6},{6,4},{8,10},{10,8},{12,14},{14,12},{16,18},{18,... | collective-permute-start | bytes 1990664 | tf_op jit(solution)/shard_map/ppermute | solution.py:108
  41.0 8.8 %collective-permute-start.9 = (bf16[64,1152]{1,0:T(8,128)(2,1)S(1)}, bf16[64,1152]{1,0:T(8,128)(2,1)S(1)}, u32[]{:S(2)}, u32[]{:S(2)}) collective-permute-start(bf16[64,1152]{1,0:T(8,128)(2,1)S(1)} %pad_maximum_fusion.7), channel_id=1, source_target_pairs={{0,8},{2,10},{4,12},{6,14},{8,0},{10,2},{12,4},{14,6},{16,24},{18,... | collective-permute-start | bytes 442376 | tf_op jit(solution)/shard_map/ppermute | solution.py:108
  42.0 4.0 %copy-start.4 = (bf16[576,1152]{1,0:T(8,128)(2,1)S(1)}, bf16[576,1152]{1,0:T(8,128)(2,1)}, u32[]{:S(2)}) copy-start(bf16[576,1152]{1,0:T(8,128)(2,1)} %param.19) | copy-start | bytes 3981316
  42.0 7.7 %collective-permute-start.11 = (bf16[64,1152]{1,0:T(8,128)(2,1)S(1)}, bf16[64,1152]{1,0:T(8,128)(2,1)S(1)}, u32[]{:S(2)}, u32[]{:S(2)}) collective-permute-start(bf16[64,1152]{1,0:T(8,128)(2,1)S(1)} %pad_maximum_fusion.8), channel_id=1, source_target_pairs={{0,16},{2,18},{4,20},{6,22},{8,24},{10,26},{12,28},{14,30},{16,0},... | collective-permute-start | bytes 442376 | tf_op jit(solution)/shard_map/ppermute | solution.py:108
  44.3 6.9 %collective-permute-start.12 = (bf16[136,1152]{1,0:T(8,128)(2,1)S(1)}, bf16[136,1152]{1,0:T(8,128)(2,1)S(1)}, u32[]{:S(2)}, u32[]{:S(2)}) collective-permute-start(bf16[136,1152]{1,0:T(8,128)(2,1)S(1)} %collective-permute-done.6.refs_5_), channel_id=1, source_target_pairs={{0,1},{1,0},{2,3},{3,2},{4,5},{5,4},{6,7},{7,6},{8,9},{9,8},{10,11... | collective-permute-start | bytes 940040 | tf_op jit(solution)/shard_map/ppermute | solution.py:108
  51.2 9.4 %collective-permute-start.14 = (bf16[128,1152]{1,0:T(8,128)(2,1)S(1)}, bf16[128,1152]{1,0:T(8,128)(2,1)S(1)}, u32[]{:S(2)}, u32[]{:S(2)}) collective-permute-start(bf16[128,1152]{1,0:T(8,128)(2,1)S(1)} %pad_maximum_fusion.5), channel_id=1, source_target_pairs={{0,4},{2,6},{4,0},{6,2},{8,12},{10,14},{12,8},{14,10},{16,20},{18,... | collective-permute-start | bytes 884744 | tf_op jit(solution)/shard_map/ppermute | solution.py:108
  52.7 8.0 %collective-permute-start.15 = (bf16[128,1152]{1,0:T(8,128)(2,1)S(1)}, bf16[128,1152]{1,0:T(8,128)(2,1)S(1)}, u32[]{:S(2)}, u32[]{:S(2)}) collective-permute-start(bf16[128,1152]{1,0:T(8,128)(2,1)S(1)} %pad_maximum_fusion.6), channel_id=1, source_target_pairs={{0,8},{2,10},{4,12},{6,14},{8,0},{10,2},{12,4},{14,6},{16,24},{18,... | collective-permute-start | bytes 884744 | tf_op jit(solution)/shard_map/ppermute | solution.py:108
  60.7 3.4 %copy-start = (s32[1,256]{1,0:T(1,128)S(1)}, s32[1,256]{1,0:T(1,128)}, u32[]{:S(2)}) copy-start(s32[1,256]{1,0:T(1,128)} %constant.84.clone.refs_6_.refs_7_) | copy-start | bytes 3076
  60.7 3.4 %copy-start.1 = (s32[1,256]{1,0:T(1,128)S(1)}, s32[1,256]{1,0:T(1,128)}, u32[]{:S(2)}) copy-start(s32[1,256]{1,0:T(1,128)} %constant.83.clone.refs_4_.refs_5_) | copy-start | bytes 3076
  60.8 3.3 %collective-permute-start.16 = (bf16[256,1152]{1,0:T(8,128)(2,1)S(1)}, bf16[256,1152]{1,0:T(8,128)(2,1)S(1)}, u32[]{:S(2)}, u32[]{:S(2)}) collective-permute-start(bf16[256,1152]{1,0:T(8,128)(2,1)S(1)} %pad_maximum_fusion.2.refs_0_), channel_id=1, source_target_pairs={{0,2},{2,0},{4,6},{6,4},{8,10},{10,8},{12,14},{14,12},{16,18},{18,... | collective-permute-start | bytes 1769480 | tf_op jit(solution)/shard_map/ppermute | solution.py:108
  60.9 3.2 %collective-permute-start.17 = (bf16[256,1152]{1,0:T(8,128)(2,1)S(1)}, bf16[256,1152]{1,0:T(8,128)(2,1)S(1)}, u32[]{:S(2)}, u32[]{:S(2)}) collective-permute-start(bf16[256,1152]{1,0:T(8,128)(2,1)S(1)} %pad_maximum_fusion.3.refs_2_), channel_id=1, source_target_pairs={{0,2},{2,0},{4,6},{6,4},{8,10},{10,8},{12,14},{14,12},{16,18},{18,... | collective-permute-start | bytes 1769480 | tf_op jit(solution)/shard_map/ppermute | solution.py:108
  62.9 15.3 %collective-permute-start.18 = (bf16[256,1152]{1,0:T(8,128)(2,1)S(1)}, bf16[256,1152]{1,0:T(8,128)(2,1)S(1)}, u32[]{:S(2)}, u32[]{:S(2)}) collective-permute-start(bf16[256,1152]{1,0:T(8,128)(2,1)S(1)} %pad_maximum_fusion.2.refs_0_), channel_id=1, source_target_pairs={{0,1},{1,0},{2,3},{3,2},{4,5},{5,4},{6,7},{7,6},{8,9},{9,8},{10,11... | collective-permute-start | bytes 1769480 | tf_op jit(solution)/shard_map/ppermute | solution.py:108
  63.4 15.0 %collective-permute-start.19 = (bf16[256,1152]{1,0:T(8,128)(2,1)S(1)}, bf16[256,1152]{1,0:T(8,128)(2,1)S(1)}, u32[]{:S(2)}, u32[]{:S(2)}) collective-permute-start(bf16[256,1152]{1,0:T(8,128)(2,1)S(1)} %pad_maximum_fusion.3.refs_2_), channel_id=1, source_target_pairs={{0,4},{2,6},{4,0},{6,2},{8,12},{10,14},{12,8},{14,10},{16,20},{18,... | collective-permute-start | bytes 1769480 | tf_op jit(solution)/shard_map/ppermute | solution.py:108
  78.4 2.0 %collective-permute-start.20 = (bf16[256,1152]{1,0:T(8,128)(2,1)S(1)}, bf16[256,1152]{1,0:T(8,128)(2,1)S(1)}, u32[]{:S(2)}, u32[]{:S(2)}) collective-permute-start(bf16[256,1152]{1,0:T(8,128)(2,1)S(1)} %collective-permute-done.18.refs_0_), channel_id=1, source_target_pairs={{0,2},{2,0},{4,6},{6,4},{8,10},{10,8},{12,14},{14,12},{16,18},{18,... | collective-permute-start | bytes 1769480 | tf_op jit(solution)/shard_map/ppermute | solution.py:108
  78.4 2.8 %collective-permute-start.21 = (bf16[256,1152]{1,0:T(8,128)(2,1)S(1)}, bf16[256,1152]{1,0:T(8,128)(2,1)S(1)}, u32[]{:S(2)}, u32[]{:S(2)}) collective-permute-start(bf16[256,1152]{1,0:T(8,128)(2,1)S(1)} %collective-permute-done.19.refs_2_), channel_id=1, source_target_pairs={{0,2},{2,0},{4,6},{6,4},{8,10},{10,8},{12,14},{14,12},{16,18},{18,... | collective-permute-start | bytes 1769480 | tf_op jit(solution)/shard_map/ppermute | solution.py:108
  96.6 6.2 %collective-permute-start.22 = (f32[576,1152]{1,0:T(8,128)S(1)}, f32[576,1152]{1,0:T(8,128)S(1)}, u32[]{:S(2)}, u32[]{:S(2)}) collective-permute-start(f32[576,1152]{1,0:T(8,128)S(1)} %get-tuple-element.66), channel_id=1, source_target_pairs={{0,2},{2,0},{4,6},{6,4},{8,10},{10,8},{12,14},{14,12},{16,18},{18,... | collective-permute-start | bytes 7962632 | tf_op jit(solution)/shard_map/ppermute | solution.py:108
  96.8 4.8 %collective-permute-start.23 = (f32[8,128]{1,0:T(8,128)S(1)}, f32[8,128]{1,0:T(8,128)S(1)}, u32[]{:S(2)}, u32[]{:S(2)}) collective-permute-start(f32[8,128]{1,0:T(8,128)S(1)} %get-tuple-element.67), channel_id=1, source_target_pairs={{0,2},{2,0},{4,6},{6,4},{8,10},{10,8},{12,14},{14,12},{16,18},{18,... | collective-permute-start | bytes 12296 | tf_op jit(solution)/shard_map/ppermute | solution.py:108
  (1 other events, 0.7 us)
